TPU v7x, 32 devices: a whole 2x2x4 slice. The times are simulated.
32 devices in a mesh: dp: 16 (over z, x, core), seq: 2 (over y).
Axes of the slice: x: 2, y: 2, z: 4, core: 2. Of those that a mesh axis runs over, the one named last changes fastest.
Arguments:
- tokens: bfloat16 [64, 1024, 768], P('dp', 'seq'), may hold values from -6 to 6
- weight_qkv: float32 [768, 2304], P('dp'), may hold values from -0.3125 to 0.3125
- bias_qv: float32 [1536], P('dp'), may hold values from -3 to 3
- weight_out: float32 [768, 768], P('dp'), may hold values from -0.4375 to 0.4375
- bias_out: float32 [768], P('dp'), may hold values from -3 to 3
- gain_attn: float32 [768], P('dp'), may hold values from 0.25 to 1.75
- shift_attn: float32 [768], P('dp'), may hold values from -3 to 3
- weight_in: float32 [768, 3072], P('dp'), may hold values from -0.21875 to 0.21875
- bias_in: float32 [3072], P('dp'), may hold values from -3 to 3
- weight_ffo: float32 [3072, 768], P('dp'), may hold values from -0.109375 to 0.109375
- bias_ffo: float32 [768], P('dp'), may hold values from -3 to 3
- gain_ffn: float32 [768], P('dp'), may hold values from 0.25 to 1.75
- shift_ffn: float32 [768], P('dp'), may hold values from -3 to 3
- lengths: int32 [64, 8], P('dp'), may hold values from 0 to 512, as said below
- cotangent: bfloat16 [64, 1024, 768], P('dp', 'seq'), may hold values from -6 to 6
Outputs:
- output: bfloat16 [64, 1024, 768], P('dp', 'seq')
- input_grad: bfloat16 [64, 1024, 768], P('dp', 'seq')
- grad_weight_qkv: float32 [768, 2304], P('dp')
- grad_bias_qv: float32 [1536], P('dp')
- grad_weight_out: float32 [768, 768], P('dp')
- grad_bias_out: float32 [768], P('dp')
- grad_gain_attn: float32 [768], P('dp')
- grad_shift_attn: float32 [768], P('dp')
- grad_weight_in: float32 [768, 3072], P('dp')
- grad_bias_in: float32 [3072], P('dp')
- grad_weight_ffo: float32 [3072, 768], P('dp')
- grad_bias_ffo: float32 [768], P('dp')
- grad_gain_ffn: float32 [768], P('dp')
- grad_shift_ffn: float32 [768], P('dp')
Inputs may be any that keep to these rules, and one draw needn't show every extreme that they name: Each row's lengths sum to 1024. In each aligned group of 4 rows one row, which one drawn from the seed, holds three passages of 256, 512 and 256 tokens with its other entries 0; every other row holds 8 passages of 1 or more and fewer than 256 tokens each.
All inputs are finite; a program needn't handle non-finite values.
Results may differ from a plain program's by a relative error of at most 0.02.
The roundings to bfloat16 on the way count: a program that leaves them out, or rounds other values in their place, can miss the bound.
Values may be sent and summed in bfloat16 or wider, within the bound.
No kernel may reach another device: no remote copies, remote signals or barrier semaphores. Data moves between devices by JAX's collectives and lax.ppermute only.
A program may use at most 448 MiB of HBM per device.

v0:
```python
import math

import jax
import jax.numpy as jnp
from jax import lax
from jax.sharding import PartitionSpec as P

H = 12


def layer_norm(values, gain, shift):
    centred = values - jnp.mean(values, axis=-1, keepdims=True)
    spread = jnp.mean(centred * centred, axis=-1, keepdims=True)
    return centred * lax.rsqrt(spread + 1e-06) * gain + shift


def exact_gelu(values):
    return jax.nn.gelu(values, approximate=False)


def segment_table(lengths, row_len):
    bounds = jnp.cumsum(lengths, axis=1)
    positions = jnp.arange(row_len, dtype=jnp.int32)
    return jnp.sum((positions[None, :, None] >= bounds[:, None, :]).astype(jnp.int32), axis=2)


def split_pairs(kv_piece, head_count):
    row_count, key_count, double = kv_piece.shape
    half = double // 2
    key_part = kv_piece[:, :, :half].reshape(row_count, key_count, head_count, half // head_count)
    value_part = kv_piece[:, :, half:].reshape(row_count, key_count, head_count, half // head_count)
    return (key_part, value_part)


def block_scores(queries, key_part, query_segments, segment_full, offset, score_scale):
    key_count = key_part.shape[1]
    key_segments = lax.dynamic_slice_in_dim(segment_full, offset, key_count, 1)
    allowed = query_segments[:, None, :, None] == key_segments[:, None, None, :]
    scores = (
        jnp.einsum("rqhd,rkhd->rhqk", queries, key_part, preferred_element_type=jnp.float32)
        * score_scale
    )
    return (jnp.where(allowed, scores, -1e30), allowed)


def attend_block(running, kv_piece, offset, queries, query_segments, segment_full, score_scale):
    best, norm_sum, accum = running
    key_part, value_part = split_pairs(kv_piece, queries.shape[2])
    blocked, allowed = block_scores(
        queries, key_part, query_segments, segment_full, offset, score_scale
    )
    best_new = jnp.maximum(best, jnp.max(blocked, axis=-1))
    weights = jnp.where(allowed, jnp.exp(blocked - best_new[..., None]), 0.0)
    norm_sum = jnp.sum(weights, axis=-1)
    accum = jnp.einsum(
        "rhqk,rkhd->rhqd",
        weights.astype(jnp.bfloat16),
        value_part,
        preferred_element_type=jnp.float32,
    )
    return (best_new, norm_sum, accum)


def per_device(
    tokens,
    weight_qkv,
    bias_qv,
    weight_out,
    bias_out,
    gain_attn,
    shift_attn,
    weight_in,
    bias_in,
    weight_ffo,
    bias_ffo,
    gain_ffn,
    shift_ffn,
    lengths,
    cotangent,
):
    row_count, tok_seq, width_model = tokens.shape
    seq_count = lax.axis_size("seq")
    seq_index = lax.axis_index("seq")
    row_len = tok_seq * seq_count
    head_count = H
    head_dim = width_model // head_count
    score_scale = 1.0 / math.sqrt(head_dim)
    token_count = row_count * tok_seq
    f32 = jnp.float32
    bf16 = jnp.bfloat16
    segment_full = segment_table(lengths, row_len)
    query_segments = lax.dynamic_slice_in_dim(segment_full, seq_index * tok_seq, tok_seq, 1)
    masters = (
        weight_qkv,
        bias_qv,
        weight_out,
        bias_out,
        gain_attn,
        shift_attn,
        weight_in,
        bias_in,
        weight_ffo,
        bias_ffo,
        gain_ffn,
        shift_ffn,
    )
    lowered = [master.astype(bf16) for master in masters]
    fetched = (
        lax.all_gather(lowered[0], "dp", axis=0, tiled=True),
        lax.all_gather(lowered[1], "dp", axis=0, tiled=True),
        lax.all_gather(lowered[2], "dp", axis=0, tiled=True),
        lax.all_gather(lowered[3], "dp", axis=0, tiled=True),
        lax.all_gather(lowered[4], "dp", axis=0, tiled=True),
        lax.all_gather(lowered[5], "dp", axis=0, tiled=True),
        lax.all_gather(lowered[6], "dp", axis=0, tiled=True),
        lax.all_gather(lowered[7], "dp", axis=0, tiled=True),
        lax.all_gather(lowered[8], "dp", axis=0, tiled=True),
        lax.all_gather(lowered[9], "dp", axis=0, tiled=True),
        lax.all_gather(lowered[10], "dp", axis=0, tiled=True),
        lax.all_gather(lowered[11], "dp", axis=0, tiled=True),
    )
    token_rows = tokens.reshape(token_count, width_model)
    whole_bias_qv = fetched[1].astype(f32)
    qkv_bias = jnp.concatenate(
        [whole_bias_qv[:width_model], jnp.zeros((width_model,), f32), whole_bias_qv[width_model:]]
    )
    projected = jnp.dot(token_rows, fetched[0], preferred_element_type=f32) + qkv_bias
    query_low = projected[:, :width_model].astype(bf16)
    key_low = projected[:, width_model : 2 * width_model].astype(bf16)
    value_low = projected[:, 2 * width_model :].astype(bf16)
    queries = query_low.reshape(row_count, tok_seq, head_count, head_dim)
    kv_local = jnp.concatenate([key_low, value_low], axis=1).reshape(
        row_count, tok_seq, 2 * width_model
    )
    start_state = (
        jnp.full((row_count, head_count, tok_seq), -1e30, f32),
        jnp.zeros((row_count, head_count, tok_seq), f32),
        jnp.zeros((row_count, head_count, tok_seq, head_dim), f32),
    )
    best, norm_sum, accum = attend_block(
        start_state,
        lax.all_gather(kv_local, "seq", axis=1, tiled=True),
        jnp.int32(0),
        queries,
        query_segments,
        segment_full,
        score_scale,
    )
    attended = accum / norm_sum[..., None]
    log_total = best + jnp.log(norm_sum)
    attn_low = attended.transpose(0, 2, 1, 3).reshape(token_count, width_model).astype(bf16)
    branch = jnp.dot(attn_low, fetched[2], preferred_element_type=f32) + fetched[3].astype(f32)
    hidden, norm_one_back = jax.vjp(
        layer_norm, token_rows.astype(f32) + branch, fetched[4].astype(f32), fetched[5].astype(f32)
    )
    hidden_low = hidden.astype(bf16)
    pre_gelu = jnp.dot(hidden_low, fetched[6], preferred_element_type=f32) + fetched[7].astype(f32)
    activated, gelu_back = jax.vjp(exact_gelu, pre_gelu)
    activated_low = activated.astype(bf16)
    second = jnp.dot(activated_low, fetched[8], preferred_element_type=f32) + fetched[9].astype(f32)
    result, norm_two_back = jax.vjp(
        layer_norm, hidden + second, fetched[10].astype(f32), fetched[11].astype(f32)
    )
    back_weights = (
        lax.all_gather(lowered[0], "dp", axis=0, tiled=True),
        lax.all_gather(lowered[1], "dp", axis=0, tiled=True),
        lax.all_gather(lowered[2], "dp", axis=0, tiled=True),
        lax.all_gather(lowered[3], "dp", axis=0, tiled=True),
        lax.all_gather(lowered[4], "dp", axis=0, tiled=True),
        lax.all_gather(lowered[5], "dp", axis=0, tiled=True),
        lax.all_gather(lowered[6], "dp", axis=0, tiled=True),
        lax.all_gather(lowered[7], "dp", axis=0, tiled=True),
        lax.all_gather(lowered[8], "dp", axis=0, tiled=True),
        lax.all_gather(lowered[9], "dp", axis=0, tiled=True),
        lax.all_gather(lowered[10], "dp", axis=0, tiled=True),
        lax.all_gather(lowered[11], "dp", axis=0, tiled=True),
    )
    grad_result = cotangent.reshape(token_count, width_model).astype(f32)
    grad_r2, grad_gain_ffn, grad_shift_ffn = norm_two_back(grad_result)
    grad_second = grad_r2.astype(bf16)
    grad_weight_ffo = jnp.dot(activated_low.T, grad_second, preferred_element_type=f32)
    grad_bias_ffo = jnp.sum(grad_second.astype(f32), axis=0)
    (grad_pre,) = gelu_back(jnp.dot(grad_second, back_weights[8].T, preferred_element_type=f32))
    grad_pre_low = grad_pre.astype(bf16)
    grad_weight_in = jnp.dot(hidden_low.T, grad_pre_low, preferred_element_type=f32)
    grad_bias_in = jnp.sum(grad_pre_low.astype(f32), axis=0)
    grad_hidden = grad_r2 + jnp.dot(grad_pre_low, back_weights[6].T, preferred_element_type=f32)
    grad_r1, grad_gain_attn, grad_shift_attn = norm_one_back(grad_hidden)
    grad_branch = grad_r1.astype(bf16)
    grad_weight_out = jnp.dot(attn_low.T, grad_branch, preferred_element_type=f32)
    grad_bias_out = jnp.sum(grad_branch.astype(f32), axis=0)
    grad_attn = jnp.dot(grad_branch, back_weights[2].T, preferred_element_type=f32).astype(bf16)
    grad_attn = grad_attn.reshape(row_count, tok_seq, head_count, head_dim).transpose(0, 2, 1, 3)
    delta = jnp.sum(grad_attn.astype(f32) * attended, axis=-1)

    def block_terms(kv_piece, offset):
        key_part, value_part = split_pairs(kv_piece, head_count)
        blocked, allowed = block_scores(
            queries, key_part, query_segments, segment_full, offset, score_scale
        )
        probs = jnp.where(allowed, jnp.exp(blocked - log_total[..., None]), 0.0)
        grad_prob = jnp.einsum("rhqd,rkhd->rhqk", grad_attn, value_part, preferred_element_type=f32)
        grad_score = (probs * (grad_prob - delta[..., None])).astype(bf16)
        query_term = (
            jnp.einsum("rhqk,rkhd->rqhd", grad_score, key_part, preferred_element_type=f32)
            * score_scale
        )
        grad_key = (
            jnp.einsum("rhqk,rqhd->rkhd", grad_score, queries, preferred_element_type=f32)
            * score_scale
        )
        grad_value = jnp.einsum(
            "rhqk,rhqd->rkhd", probs.astype(bf16), grad_attn, preferred_element_type=f32
        )
        pair = jnp.concatenate(
            [
                grad_key.reshape(row_count, tok_seq, width_model),
                grad_value.reshape(row_count, tok_seq, width_model),
            ],
            axis=-1,
        )
        return (query_term, pair)

    query_start = jnp.zeros((row_count, tok_seq, head_count, head_dim), f32)
    kv_whole = lax.all_gather(kv_local, "seq", axis=1, tiled=True)

    def back_block(grad_query, block_index):
        offset = block_index * tok_seq
        kv_piece = lax.dynamic_slice_in_dim(kv_whole, offset, tok_seq, 1)
        query_term, pair = block_terms(kv_piece, offset)
        return (grad_query + query_term, pair)

    grad_query, kv_terms = lax.scan(back_block, query_start, jnp.arange(seq_count, dtype=jnp.int32))
    kv_summed = lax.psum_scatter(
        kv_terms.astype(jnp.bfloat16), "seq", scatter_dimension=0, tiled=True
    ).astype(jnp.float32)[0]
    grad_key_low = kv_summed[:, :, :width_model].reshape(token_count, width_model).astype(bf16)
    grad_value_low = kv_summed[:, :, width_model:].reshape(token_count, width_model).astype(bf16)
    grad_query_low = grad_query.reshape(token_count, width_model).astype(bf16)
    grad_qkv = jnp.concatenate([grad_query_low, grad_key_low, grad_value_low], axis=1)
    grad_weight_qkv = jnp.dot(token_rows.T, grad_qkv, preferred_element_type=f32)
    grad_bias_qv = jnp.concatenate(
        [jnp.sum(grad_query_low.astype(f32), axis=0), jnp.sum(grad_value_low.astype(f32), axis=0)]
    )
    grad_tokens = grad_r1 + jnp.dot(grad_qkv, back_weights[0].T, preferred_element_type=f32)
    grad_tokens = grad_tokens.astype(bf16).reshape(row_count, tok_seq, width_model)
    shared = (
        lax.psum_scatter(
            grad_weight_qkv.astype(jnp.bfloat16), "dp", scatter_dimension=0, tiled=True
        ).astype(jnp.float32),
        lax.psum_scatter(
            grad_bias_qv.astype(jnp.bfloat16), "dp", scatter_dimension=0, tiled=True
        ).astype(jnp.float32),
        lax.psum_scatter(
            grad_weight_out.astype(jnp.bfloat16), "dp", scatter_dimension=0, tiled=True
        ).astype(jnp.float32),
        lax.psum_scatter(
            grad_bias_out.astype(jnp.bfloat16), "dp", scatter_dimension=0, tiled=True
        ).astype(jnp.float32),
        lax.psum_scatter(
            grad_gain_attn.astype(jnp.bfloat16), "dp", scatter_dimension=0, tiled=True
        ).astype(jnp.float32),
        lax.psum_scatter(
            grad_shift_attn.astype(jnp.bfloat16), "dp", scatter_dimension=0, tiled=True
        ).astype(jnp.float32),
        lax.psum_scatter(
            grad_weight_in.astype(jnp.bfloat16), "dp", scatter_dimension=0, tiled=True
        ).astype(jnp.float32),
        lax.psum_scatter(
            grad_bias_in.astype(jnp.bfloat16), "dp", scatter_dimension=0, tiled=True
        ).astype(jnp.float32),
        lax.psum_scatter(
            grad_weight_ffo.astype(jnp.bfloat16), "dp", scatter_dimension=0, tiled=True
        ).astype(jnp.float32),
        lax.psum_scatter(
            grad_bias_ffo.astype(jnp.bfloat16), "dp", scatter_dimension=0, tiled=True
        ).astype(jnp.float32),
        lax.psum_scatter(
            grad_gain_ffn.astype(jnp.bfloat16), "dp", scatter_dimension=0, tiled=True
        ).astype(jnp.float32),
        lax.psum_scatter(
            grad_shift_ffn.astype(jnp.bfloat16), "dp", scatter_dimension=0, tiled=True
        ).astype(jnp.float32),
    )
    summed = (
        lax.psum(shared[0].astype(jnp.bfloat16), "seq").astype(jnp.float32),
        lax.psum(shared[1].astype(jnp.bfloat16), "seq").astype(jnp.float32),
        lax.psum(shared[2].astype(jnp.bfloat16), "seq").astype(jnp.float32),
        lax.psum(shared[3].astype(jnp.bfloat16), "seq").astype(jnp.float32),
        lax.psum(shared[4].astype(jnp.bfloat16), "seq").astype(jnp.float32),
        lax.psum(shared[5].astype(jnp.bfloat16), "seq").astype(jnp.float32),
        lax.psum(shared[6].astype(jnp.bfloat16), "seq").astype(jnp.float32),
        lax.psum(shared[7].astype(jnp.bfloat16), "seq").astype(jnp.float32),
        lax.psum(shared[8].astype(jnp.bfloat16), "seq").astype(jnp.float32),
        lax.psum(shared[9].astype(jnp.bfloat16), "seq").astype(jnp.float32),
        lax.psum(shared[10].astype(jnp.bfloat16), "seq").astype(jnp.float32),
        lax.psum(shared[11].astype(jnp.bfloat16), "seq").astype(jnp.float32),
    )
    return (
        result.astype(bf16).reshape(row_count, tok_seq, width_model),
        grad_tokens,
        summed[0],
        summed[1],
        summed[2],
        summed[3],
        summed[4],
        summed[5],
        summed[6],
        summed[7],
        summed[8],
        summed[9],
        summed[10],
        summed[11],
    )


def solution(mesh):
    placed = (
        P("dp", "seq", None),
        P("dp", None),
        P("dp"),
        P("dp", None),
        P("dp"),
        P("dp"),
        P("dp"),
        P("dp", None),
        P("dp"),
        P("dp", None),
        P("dp"),
        P("dp"),
        P("dp"),
        P("dp", None),
        P("dp", "seq", None),
    )
    return jax.shard_map(
        per_device,
        mesh=mesh,
        in_specs=placed,
        out_specs=(
            P("dp", "seq", None),
            P("dp", "seq", None),
            P("dp", None),
            P("dp"),
            P("dp", None),
            P("dp"),
            P("dp"),
            P("dp"),
            P("dp", None),
            P("dp"),
            P("dp", None),
            P("dp"),
            P("dp"),
            P("dp"),
        ),
        check_vma=False,
    )
```

profile of v0, /device:TPU:12, one launch (start us, length us, event | category | flops | bytes accessed | tf_op | source)
XLA Modules:
  0.0 1396.5 jit_solution(7193263665823173469)
XLA Ops:
  18.4 53.9 %all-reduce.17 = (bf16[1536]{0:T(1024)(128)(2,1)S(1)}, bf16[768]{0:T(1024)(128)(2,1)S(1)}, bf16[768]{0:T(1024)(128)(2,1)S(1)}, bf16[768]{0:T(1024)(128)(2,1)S(1)...) all-reduce(bf16[1536]{0:T(1024)(128)(2,1)S(1)} %dynamic-update-slic, ...), channel_id=1, replica_groups=mesh['dp'=16,'seq'=2] {'dp'}, use_global_device_ids=true, to_apply=%add | all-reduce | flops 8448 | bytes 33792
  72.4 10.2 add_convert_fusion.1
  88.1 8.7 copy.70
  112.1 5.1 reshape.173
  119.7 134.1 %all-gather.8.cloned.1.call-done = bf16[4,1024,1536]{1,2,0:T(8,128)(2,1)} async-done(((bf16[4,512,1536]{1,2,0:T(8,128)(2,1)}), bf16[4,1024,1536]{1,2,0:T(8,128)(2,1)}) %all-gather.8.cloned.1.call-update) | async-done | bytes 12582928 | tf_op jit(solution)/shard_map/all_gather | solution.py:142
  253.8 10.6 fusion.49
  264.3 37.6 %fusion.11 = (f32[4,12,512]{2,1,0:T(8,128)S(1)}, f32[4,12,512,1024]{3,2,1,0:T(8,128)}) fusion(pred[4,512,1024]{2,1,0:T(8,128)(4,1)S(1)} %copy-done.2, bf16[4,1024,12,64]{1,3,2,0:T(8,128)(2,1)} %bitcast.151, bf16[4,512,12,64]{1,0,3,2:T(4,128)(2,1)S(1)} %reshape.173), kind=kOutput, calls=%fused_computation.22 | convolution fusion | flops 3296698368 | bytes 112295936 | tf_op jit(solution)/shard_map/rqhd,rkhd->rhqk/dot_general | solution.py:40
  302.0 41.6 %fusion.12 = f32[4,12,512]{2,1,0:T(8,128)S(1)} fusion(f32[4,12,512,1024]{3,2,1,0:T(8,128)} %get-tuple-element.289, f32[4,12,512]{2,1,0:T(8,128)S(1)} %broadcast_maximum_fusion, pred[4,512,1024]{2,1,0:T(8,128)(4,1)} %broadcast_compare_fusion.1), kind=kLoop, calls=%fused_computation.23 | loop fusion | flops 125804544 | bytes 102957056 | tf_op jit(solution)/shard_map/reduce_sum | solution.py:54
  344.3 41.1 %fusion.27 = (bf16[4,512,12,64]{1,3,2,0:T(8,128)(2,1)}, f32[4,12,512,64]{2,3,1,0:T(8,128)}) fusion(f32[4,512,12]{1,2,0:T(8,128)S(1)} %bitcast.165, bf16[4,1024,12,64]{1,3,2,0:T(8,128)(2,1)} %bitcast.158, f32[4,12,512,1024]{3,2,1,0:T(8,128)} %get-tuple-element.289, f32[4,12,512]{2,1,0:T(8,128)S(1)} %broadcast_maximum_fusion, ...), kind=kOutput, calls=%fused_computation.55 | convolution fusion | flops 3350200320 | bytes 118685696 | tf_op jit(solution)/shard_map/rhqk,rkhd->rhqd/dot_general | solution.py:55
  390.8 6.6 fusion.53
  401.6 70.6 %multiply_convert_fusion = (bf16[2048,3072]{1,0:T(8,128)(2,1)}, f32[2048,3072]{1,0:T(8,128)}, f32[2048,3072]{1,0:T(8,128)}) fusion(f32[3072]{0:T(1024)S(1)} %copy-done.38, bf16[768,3072]{1,0:T(8,128)(2,1)} %all-gather.12.cloned.1.call-done, f32[2048,768]{1,0:T(8,128)} %copy-done.8, f32[768]{0:T(1024)S(1)} %copy-done.43, f32[768]{0:T(1024)S(1)} %copy-done.36, ...), kind=kOutput, calls=%fused_computation.30 | convolution fusion | flops 10086776832 | bytes 73959424 | tf_op jit(solution)/shard_map/dot_general | solution.py:157
  472.2 16.2 %fusion.54 = (f32[2048]{0:T(1024)S(1)}, f32[2048,768]{1,0:T(8,128)S(1)}) fusion(f32[768]{0:T(1024)S(1)} %copy-done.45, bf16[2048,3072]{1,0:T(8,128)(2,1)} %get-tuple-element.275, bf16[3072,768]{1,0:T(8,128)(2,1)} %all-gather.14.cloned.1.call-done, f32[768]{0:T(1024)S(1)} %copy-done.43, f32[768]{0:T(1024)S(1)} %copy-done.36, f32[2048]{0:T(1024)S(1)} %fusion.31, ...), kind=kOutput, calls=%fused_computation.115 | convolution fusion | flops 9674684416 | bytes 29918208 | tf_op jit(solution)/shard_map/dot_general | solution.py:160
  503.0 29.1 %fusion.55 = (bf16[3072]{0:T(1024)(128)(2,1)}, bf16[2048,3072]{1,0:T(8,128)(2,1)}) fusion(f32[2048,3072]{1,0:T(8,128)} %get-tuple-element.276, bf16[2048,768]{1,0:T(8,128)(2,1)S(1)} %get-tuple-element.266, bf16[3072,768]{1,0:T(8,128)(2,1)} %all-gather.14.cloned.1.call-done, f32[2048,3072]{1,0:T(8,128)} %get-tuple-element.294, f32[3072]{0:T(1024)S(1)} %copy-done.38), kind=kOutput, calls=%fused_computation.116 | convolution fusion | flops 9764336640 | bytes 70797312 | tf_op jit(solution)/shard_map/dot_general | solution.py:183
  532.1 19.2 %multiply_reduce_fusion = (bf16[768]{0:T(1024)(128)(2,1)}, f32[2048]{0:T(1024)S(1)}, bf16[768]{0:T(1024)(128)(2,1)}, f32[2048,768]{1,0:T(8,128)S(1)}) fusion(f32[2048,768]{1,0:T(8,128)} %copy-done.8, f32[2048]{0:T(1024)S(1)} %fusion.31, f32[2048]{0:T(1024)S(1)} %broadcast_multiply_fusion.2, f32[768]{0:T(1024)S(1)} %copy-done.36, ...), kind=kOutput, calls=%fused_computation.56 | convolution fusion | flops 9679400960 | bytes 36214784 | tf_op jit(solution)/shard_map/dot_general | solution.py:187
  566.9 4.8 reshape.178
  578.7 264.4 %while.13 = (s32[]{:T(128)}, f32[4,512,12,64]{1,3,2,0:T(8,128)}, bf16[2,4,512,1536]{3,2,1,0:T(8,128)(2,1)}, s32[2]{0:T(128)S(1)}, bf16[4,1024,1536]{1,2,0:T(8,12...) while((s32[]{:T(128)}, f32[4,512,12,64]{1,3,2,0:T(8,128)}, ...), condition=%wide.region_14.15_spmd.clone, body=%wide.region_13.14_spmd.clone.sunk | while | flops 8225554432 | bytes 334168864 | solution.py:233
  580.1 5.2 constant_dynamic-slice_fusion.6
  585.3 21.3 %fusion.112 = f32[4,12,512,512]{3,2,1,0:T(8,128)} fusion(bf16[4,512,12,64]{1,3,2,0:T(8,128)(2,1)S(1)} %bitcast.146, bf16[4,512,12,64]{1,3,2,0:T(8,128)(2,1)} %get-tuple-element.410), kind=kOutput, calls=%fused_computation.117.clone.1 | convolution fusion | flops 1610612736 | bytes 56623104 | tf_op jit(solution)/shard_map/while/body/eval_jaxpr/rqhd,rkhd->rhqk/dot_general | solution.py:40
  608.1 30.5 %fusion.113 = bf16[4,12,512,512]{2,3,1,0:T(8,128)(2,1)} fusion(f32[4,12,512,512]{3,2,1,0:T(8,128)} %fusion.112, f32[4,12,512]{2,1,0:T(8,128)S(1)} %get-tuple-element.413, f32[4,12,512]{2,1,0:T(8,128)S(1)} %copy-done.23, pred[4,512,512]{1,2,0:T(8,128)(4,1)} %broadcast_compare_fusion.3, bf16[4,512,12,64]{1,3,2,0:T(8,128)(2,1)} %bitcast.148, ...), kind=kOutput, calls=%fused_computation.1.clone.1 | convolution fusion | flops 1698693120 | bytes 83034112 | tf_op jit(solution)/shard_map/while/body/eval_jaxpr/rhqd,rkhd->rhqk/dot_general | solution.py:202
  638.6 14.5 %broadcast_multiply_fusion.4 = bf16[4,12,512,64]{2,3,1,0:T(8,128)(2,1)} fusion(bf16[4,12,512,512]{2,3,1,0:T(8,128)(2,1)} %fusion.113, bf16[4,512,12,64]{1,3,2,0:T(8,128)(2,1)} %get-tuple-element.410), kind=kOutput, calls=%fused_computation.11.clone.1 | convolution fusion | flops 1613758464 | bytes 31457280 | tf_op jit(solution)/shard_map/while/body/eval_jaxpr/rhqk,rqhd->rkhd/dot_general | solution.py:209
  653.1 22.5 %fusion.114 = bf16[4,12,512,64]{2,3,1,0:T(8,128)(2,1)} fusion(bf16[4,12,512,64]{2,3,1,0:T(8,128)(2,1)} %get-tuple-element.412, f32[4,12,512,512]{3,2,1,0:T(8,128)} %fusion.112, f32[4,12,512]{2,1,0:T(8,128)S(1)} %copy-done.23, pred[4,512,512]{1,2,0:T(8,128)(4,1)} %broadcast_compare_fusion.3), kind=kOutput, calls=%fused_computation.7.clone.1 | convolution fusion | flops 1673527296 | bytes 57769984 | tf_op jit(solution)/shard_map/while/body/eval_jaxpr/rhqk,rhqd->rkhd/dot_general | solution.py:212
  675.6 4.9 maximum_bitcast_fusion.2
  680.5 8.7 copy.112
  689.2 5.7 constant_dynamic-update-slice_fusion.2
  694.9 14.9 %bitcast_add_fusion.2 = f32[4,512,12,64]{1,3,2,0:T(8,128)} fusion(f32[4,512,12,64]{1,3,2,0:T(8,128)} %get-tuple-element.388, pred[]{:T(512)S(6)} %compare.3, bf16[4,512,12,64]{1,3,2,0:T(8,128)(2,1)S(1)} %bitcast.147, bf16[4,12,512,512]{2,3,1,0:T(8,128)(2,1)} %fusion.113), kind=kOutput, calls=%fused_computation.10.clone.1 | convolution fusion | flops 1615331328 | bytes 40894464 | tf_op jit(solution)/shard_map/while/body/eval_jaxpr/rhqk,rkhd->rqhd/dot_general | solution.py:205
  711.0 5.2 constant_dynamic-slice_fusion.6
  716.2 21.3 %fusion.112 = f32[4,12,512,512]{3,2,1,0:T(8,128)} fusion(bf16[4,512,12,64]{1,3,2,0:T(8,128)(2,1)S(1)} %bitcast.146, bf16[4,512,12,64]{1,3,2,0:T(8,128)(2,1)} %get-tuple-element.410), kind=kOutput, calls=%fused_computation.117.clone.1 | convolution fusion | flops 1610612736 | bytes 56623104 | tf_op jit(solution)/shard_map/while/body/eval_jaxpr/rqhd,rkhd->rhqk/dot_general | solution.py:40
  739.0 30.5 %fusion.113 = bf16[4,12,512,512]{2,3,1,0:T(8,128)(2,1)} fusion(f32[4,12,512,512]{3,2,1,0:T(8,128)} %fusion.112, f32[4,12,512]{2,1,0:T(8,128)S(1)} %get-tuple-element.413, f32[4,12,512]{2,1,0:T(8,128)S(1)} %copy-done.23, pred[4,512,512]{1,2,0:T(8,128)(4,1)} %broadcast_compare_fusion.3, bf16[4,512,12,64]{1,3,2,0:T(8,128)(2,1)} %bitcast.148, ...), kind=kOutput, calls=%fused_computation.1.clone.1 | convolution fusion | flops 1698693120 | bytes 83034112 | tf_op jit(solution)/shard_map/while/body/eval_jaxpr/rhqd,rkhd->rhqk/dot_general | solution.py:202
  769.5 14.5 %broadcast_multiply_fusion.4 = bf16[4,12,512,64]{2,3,1,0:T(8,128)(2,1)} fusion(bf16[4,12,512,512]{2,3,1,0:T(8,128)(2,1)} %fusion.113, bf16[4,512,12,64]{1,3,2,0:T(8,128)(2,1)} %get-tuple-element.410), kind=kOutput, calls=%fused_computation.11.clone.1 | convolution fusion | flops 1613758464 | bytes 31457280 | tf_op jit(solution)/shard_map/while/body/eval_jaxpr/rhqk,rqhd->rkhd/dot_general | solution.py:209
  784.0 22.5 %fusion.114 = bf16[4,12,512,64]{2,3,1,0:T(8,128)(2,1)} fusion(bf16[4,12,512,64]{2,3,1,0:T(8,128)(2,1)} %get-tuple-element.412, f32[4,12,512,512]{3,2,1,0:T(8,128)} %fusion.112, f32[4,12,512]{2,1,0:T(8,128)S(1)} %copy-done.23, pred[4,512,512]{1,2,0:T(8,128)(4,1)} %broadcast_compare_fusion.3), kind=kOutput, calls=%fused_computation.7.clone.1 | convolution fusion | flops 1673527296 | bytes 57769984 | tf_op jit(solution)/shard_map/while/body/eval_jaxpr/rhqk,rhqd->rkhd/dot_general | solution.py:212
  806.5 4.9 maximum_bitcast_fusion.2
  811.4 8.7 copy.112
  820.1 5.9 constant_dynamic-update-slice_fusion.2
  825.9 16.8 %bitcast_add_fusion.2 = f32[4,512,12,64]{1,3,2,0:T(8,128)} fusion(f32[4,512,12,64]{1,3,2,0:T(8,128)} %get-tuple-element.388, pred[]{:T(512)S(6)} %compare.3, bf16[4,512,12,64]{1,3,2,0:T(8,128)(2,1)S(1)} %bitcast.147, bf16[4,12,512,512]{2,3,1,0:T(8,128)(2,1)} %fusion.113), kind=kOutput, calls=%fused_computation.10.clone.1 | convolution fusion | flops 1615331328 | bytes 40894464 | tf_op jit(solution)/shard_map/while/body/eval_jaxpr/rhqk,rkhd->rqhd/dot_general | solution.py:205
  851.8 136.6 %reduce-scatter.8.cloned.1.call-done = bf16[1,4,512,1536]{3,2,1,0:T(8,128)(2,1)} async-done(((bf16[2,4,512,1536]{3,2,1,0:T(8,128)(2,1)}), bf16[1,4,512,1536]{3,2,1,0:T(8,128)(2,1)}) %reduce-scatter.8.cloned.1.call-update) | async-done | bytes 6291472 | tf_op jit(solution)/shard_map/reduce_scatter | solution.py:234
  988.3 4.6 fusion.50
  992.9 4.8 copy.78
  1000.6 12.2 fusion.29
  1016.9 6.6 convolution_convert_fusion.4
  1023.6 14.9 %convolution_convert_fusion = bf16[3072,768]{1,0:T(8,128)(2,1)} fusion(bf16[2048,3072]{1,0:T(8,128)(2,1)} %get-tuple-element.275, bf16[2048,768]{1,0:T(8,128)(2,1)S(1)} %copy-done.12), kind=kOutput, calls=%fused_computation.70 | convolution fusion | flops 9666035712 | bytes 20447232 | tf_op jit(solution)/shard_map/dot_general | solution.py:181
  1038.7 17.9 %convolution_convert_fusion.1 = bf16[768,3072]{1,0:T(8,128)(2,1)} fusion(bf16[2048,3072]{1,0:T(8,128)(2,1)} %get-tuple-element.299, f32[2048,768]{1,0:T(8,128)} %copy-done.8, f32[768]{0:T(1024)S(1)} %copy-done.44, f32[768]{0:T(1024)S(1)} %copy-done.37, f32[2048]{0:T(1024)S(1)} %copy-done.33, f32[2048]{0:T(1024)S(1)} %copy-done.27), kind=kOutput, calls=%fused_computation.71 | convolution fusion | flops 9673900032 | bytes 23615488 | tf_op jit(solution)/shard_map/dot_general | solution.py:185
  1061.6 23.9 %reduce-scatter.16.cloned.1.call-done = bf16[48,2304]{1,0:T(8,128)(2,1)} async-done(((bf16[768,2304]{1,0:T(8,128)(2,1)}), bf16[48,2304]{1,0:T(8,128)(2,1)}) %reduce-scatter.16.cloned.1.call-update) | async-done | bytes 221200
  1087.4 59.6 %reduce-scatter.10.cloned.1.call-done = bf16[48,768]{1,0:T(8,128)(2,1)} async-done(((bf16[768,768]{1,0:T(8,128)(2,1)}), bf16[48,768]{1,0:T(8,128)(2,1)}) %reduce-scatter.10.cloned.1.call-update) | async-done | bytes 73744 | tf_op jit(solution)/shard_map/reduce_scatter | solution.py:254
  1147.0 78.0 %reduce-scatter.14.cloned.1.call-done = bf16[192,768]{1,0:T(8,128)(2,1)} async-done(((bf16[3072,768]{1,0:T(8,128)(2,1)}), bf16[192,768]{1,0:T(8,128)(2,1)}) %reduce-scatter.14.cloned.1.call-update) | async-done | bytes 294928 | tf_op jit(solution)/shard_map/reduce_scatter | solution.py:272
  1225.0 78.8 %reduce-scatter.12.cloned.1.call-done = bf16[48,3072]{1,0:T(8,128)(2,1)} async-done(((bf16[768,3072]{1,0:T(8,128)(2,1)}), bf16[48,3072]{1,0:T(8,128)(2,1)}) %reduce-scatter.12.cloned.1.call-update) | async-done | bytes 294928 | tf_op jit(solution)/shard_map/reduce_scatter | solution.py:266
  1303.9 13.6 add_convert_fusion.2
  1317.6 50.7 %all-reduce.16 = (bf16[768]{0:T(1024)(128)(2,1)S(1)}, bf16[1536]{0:T(1024)(128)(2,1)S(1)}, bf16[768]{0:T(1024)(128)(2,1)S(1)}, bf16[768]{0:T(1024)(128)(2,1)S(1)...) all-reduce(bf16[768]{0:T(1024)(128)(2,1)S(1)} %dynamic-update-slice, ...), channel_id=1, replica_groups=mesh['dp'=16,'seq'=2] {'dp'}, use_global_device_ids=true, to_apply=%add.7 | all-reduce | flops 9984 | bytes 39936
  1368.9 4.9 all-reduce.18
  (245 shorter events, 120.9 us)
Async XLA Ops:
  7.2 65.2 %all-gather.6.cloned.1.call-start = ((), (), s32[]{:S(2)}) async-start(), calls=%async_computation.5 | async-start | bytes 3760128 | tf_op jit(solution)/shard_map/all_gather | solution.py:109
  9.0 244.8 %all-gather.8.cloned.1.call-start = ((), (), s32[]{:S(2)}) async-start(), calls=%async_computation.6 | async-start | bytes 18874368 | tf_op jit(solution)/shard_map/all_gather | solution.py:142
  96.8 5.6 copy-start.49
  96.9 12.4 slice-start
  96.9 293.9 %all-gather.10.cloned.1.call-start = ((), (), s32[]{:S(2)}) async-start(), calls=%async_computation.7 | async-start | bytes 1253376 | tf_op jit(solution)/shard_map/all_gather | solution.py:111
  98.4 303.1 %all-gather.12.cloned.1.call-start = ((), (), s32[]{:S(2)}) async-start(), calls=%async_computation.8 | async-start | bytes 5013504 | tf_op jit(solution)/shard_map/all_gather | solution.py:115
  100.3 371.9 %all-gather.14.cloned.1.call-start = ((), (), s32[]{:S(2)}) async-start(), calls=%async_computation.9 | async-start | bytes 5013504 | tf_op jit(solution)/shard_map/all_gather | solution.py:117
  102.2 886.1 %reduce-scatter.8.cloned.1.call-start = ((), (), s32[]{:S(2)}) async-start(), calls=%async_computation.10 | async-start | bytes 18874368 | tf_op jit(solution)/shard_map/reduce_scatter | solution.py:234
  102.8 9.4 copy-start.16
  253.8 10.6 copy-start.2
  301.9 42.3 %copy-start.3 = (pred[4,512,1024]{2,1,0:T(8,128)(4,1)S(1)}, pred[4,512,1024]{2,1,0:T(8,128)(4,1)}, u32[]{:S(2)}) copy-start(pred[4,512,1024]{2,1,0:T(8,128)(4,1)} %broadcast_compare_fusion.1) | copy-start | bytes 6291460
  343.6 41.8 %copy-start.14 = (f32[4,12,512]{2,1,0:T(8,128)}, f32[4,12,512]{2,1,0:T(8,128)S(1)}, u32[]{:S(2)}) copy-start(f32[4,12,512]{2,1,0:T(8,128)S(1)} %fusion.12) | copy-start | bytes 294916
  390.8 6.7 copy-start.10
  397.5 153.8 %copy-start.26 = (f32[2048]{0:T(1024)}, f32[2048]{0:T(1024)S(1)}, u32[]{:S(2)}) copy-start(f32[2048]{0:T(1024)S(1)} %broadcast_multiply_fusion.2) | copy-start | bytes 24580
  401.5 149.8 %copy-start.32 = (f32[2048]{0:T(1024)}, f32[2048]{0:T(1024)S(1)}, u32[]{:S(2)}) copy-start(f32[2048]{0:T(1024)S(1)} %fusion.31) | copy-start | bytes 24580
  401.5 70.6 %copy-start.45 = (f32[768]{0:T(1024)S(1)}, f32[768]{0:T(1024)}, u32[]{:S(2)}) copy-start(f32[768]{0:T(1024)} %convert_element_type.260) | copy-start | bytes 9220
  488.4 7.5 copy-start
  488.5 7.4 copy-start.20
  492.6 6.5 copy-start.24
  503.0 29.1 %copy-start.11 = (bf16[2048,768]{1,0:T(8,128)(2,1)}, bf16[2048,768]{1,0:T(8,128)(2,1)S(1)}, u32[]{:S(2)}) copy-start(bf16[2048,768]{1,0:T(8,128)(2,1)S(1)} %get-tuple-element.266) | copy-start | bytes 9437188
  532.1 19.2 %copy-start.29 = (f32[2048]{0:T(1024)S(1)}, f32[2048]{0:T(1024)}, u32[]{:S(2)}) copy-start(f32[2048]{0:T(1024)} %copy-done.28) | copy-start | bytes 24580
  555.5 5.6 copy-start.50
  566.9 7.2 copy-start.15
  585.3 22.8 %copy-start.23 = (f32[4,12,512]{2,1,0:T(8,128)S(1)}, f32[4,12,512]{2,1,0:T(8,128)}, u32[]{:S(2)}) copy-start(f32[4,12,512]{2,1,0:T(8,128)} %get-tuple-element.411) | copy-start | bytes 294916 | tf_op jit(solution)/shard_map/while
  653.1 22.5 %copy-start.1 = (bf16[4,12,512,64]{2,3,1,0:T(8,128)(2,1)S(1)}, bf16[4,12,512,64]{2,3,1,0:T(8,128)(2,1)}, u32[]{:S(2)}) copy-start(bf16[4,12,512,64]{2,3,1,0:T(8,128)(2,1)} %broadcast_multiply_fusion.4) | copy-start | bytes 9437188 | tf_op jit(solution)/shard_map/while
  716.2 22.8 %copy-start.23 = (f32[4,12,512]{2,1,0:T(8,128)S(1)}, f32[4,12,512]{2,1,0:T(8,128)}, u32[]{:S(2)}) copy-start(f32[4,12,512]{2,1,0:T(8,128)} %get-tuple-element.411) | copy-start | bytes 294916 | tf_op jit(solution)/shard_map/while
  784.0 22.5 %copy-start.1 = (bf16[4,12,512,64]{2,3,1,0:T(8,128)(2,1)S(1)}, bf16[4,12,512,64]{2,3,1,0:T(8,128)(2,1)}, u32[]{:S(2)}) copy-start(bf16[4,12,512,64]{2,3,1,0:T(8,128)(2,1)} %broadcast_multiply_fusion.4) | copy-start | bytes 9437188 | tf_op jit(solution)/shard_map/while
  843.1 242.3 %reduce-scatter.16.cloned.1.call-start = ((), (), s32[]{:S(2)}) async-start(), calls=%async_computation.14 | async-start | bytes 3760128
  1016.9 6.8 copy-start.12
  1016.9 130.1 %reduce-scatter.10.cloned.1.call-start = ((), (), s32[]{:S(2)}) async-start(), calls=%async_computation.11 | async-start | bytes 1253376 | tf_op jit(solution)/shard_map/reduce_scatter | solution.py:254
  1023.5 15.1 %copy-start.27 = (f32[2048]{0:T(1024)S(1)}, f32[2048]{0:T(1024)}, u32[]{:S(2)}) copy-start(f32[2048]{0:T(1024)} %copy-done.26) | copy-start | bytes 24580
  1023.6 15.1 %copy-start.33 = (f32[2048]{0:T(1024)S(1)}, f32[2048]{0:T(1024)}, u32[]{:S(2)}) copy-start(f32[2048]{0:T(1024)} %copy-done.32) | copy-start | bytes 24580
  1023.6 15.1 %copy-start.37 = (f32[768]{0:T(1024)S(1)}, f32[768]{0:T(1024)}, u32[]{:S(2)}) copy-start(f32[768]{0:T(1024)} %convert_element_type.250) | copy-start | bytes 9220
  1023.6 15.1 %copy-start.44 = (f32[768]{0:T(1024)S(1)}, f32[768]{0:T(1024)}, u32[]{:S(2)}) copy-start(f32[768]{0:T(1024)} %convert_element_type.252) | copy-start | bytes 9220
  1023.6 201.4 %reduce-scatter.14.cloned.1.call-start = ((), (), s32[]{:S(2)}) async-start(), calls=%async_computation.13 | async-start | bytes 5013504 | tf_op jit(solution)/shard_map/reduce_scatter | solution.py:272
  1038.6 18.1 %copy-start.51 = (f32[48]{0:T(128)S(1)}, f32[48]{0:T(128)}, u32[]{:S(2)}) copy-start(f32[48]{0:T(128)} %param.29) | copy-start | bytes 580
  1038.6 265.2 %reduce-scatter.12.cloned.1.call-start = ((), (), s32[]{:S(2)}) async-start(), calls=%async_computation.12 | async-start | bytes 5013504 | tf_op jit(solution)/shard_map/reduce_scatter | solution.py:266
  1056.6 247.2 %copy-start.35 = (f32[2048]{0:T(1024)S(1)}, f32[2048]{0:T(1024)}, u32[]{:S(2)}) copy-start(f32[2048]{0:T(1024)} %copy-done.34) | copy-start | bytes 24580
  1056.7 325.9 %all-reduce.22.cloned.1.call-start = ((), (), s32[]{:S(2)}) async-start(), calls=%async_computation.15 | async-start | bytes 2506752 | tf_op jit(solution)/shard_map/psum | solution.py:286
  1303.9 13.7 copy-start.39
  1303.9 13.7 copy-start.40
  1303.9 13.7 copy-start.41
  1303.9 13.7 copy-start.42
  1303.9 13.7 copy-start.47
  1303.9 13.7 copy-start.48
  1303.9 74.1 %copy-start.21 = (f32[2048]{0:T(1024)S(1)}, f32[2048]{0:T(1024)}, u32[]{:S(2)}) copy-start(f32[2048]{0:T(1024)} %copy-done.20) | copy-start | bytes 24580
  1303.9 74.1 %copy-start.25 = (f32[2048]{0:T(1024)S(1)}, f32[2048]{0:T(1024)}, u32[]{:S(2)}) copy-start(f32[2048]{0:T(1024)} %copy-done.24) | copy-start | bytes 24580
  1303.9 74.1 %copy-start.31 = (f32[768]{0:T(1024)S(1)}, f32[768]{0:T(1024)}, u32[]{:S(2)}) copy-start(f32[768]{0:T(1024)} %convert_element_type.262) | copy-start | bytes 9220
  (18 other events, 58.2 us)
Sparse Core Ops, SparseCore 0:
  10.9 49.1 all-gather.5
  97.0 156.7 all-gather.7
  256.1 38.4 all-gather.9
  297.2 53.1 all-gather.11
  353.1 51.9 all-gather.13
  843.3 145.0 reduce-scatter.7
  1017.0 68.4 reduce-scatter.15
  1089.6 57.3 reduce-scatter.9
  1150.9 74.0 reduce-scatter.13
  1229.2 74.5 reduce-scatter.11
  1306.9 43.9 all-reduce.21
where the time goes:
time: 1410 us; the launch traced here: 1400 us
  waiting for transfers between devices  511 us (36%)
  matrix products  508 us (36%)
  local copies, waits for them, and re-layouts  133 us (9%)
  other arithmetic  114 us (8%)
  blocking collectives  110 us (8%)
  between operations  18.8 us (1%)
    reduce_scatter x1, waiting for transfers between devices, per_device(): lax.psum_scatter(kv_terms.astype(jnp.bfloat16), 'seq', scatter_dimension=...  137 us
    all_gather x1, waiting for transfers between devices, per_device(): lax.all_gather(kv_local, 'seq', axis=1, tiled=True)  134 us
    unnamed x2, blocking collectives  105 us
    dot_general x3, matrix products, block_scores(): jnp.einsum('rqhd,rkhd->rhqk', queries, key_part, preferred_element_type=j...  80.1 us
    reduce_scatter x1, waiting for transfers between devices, per_device(): lax.psum_scatter(grad_weight_in.astype(jnp.bfloat16), 'dp', scatter_dimen...  78.8 us
    reduce_scatter x1, waiting for transfers between devices, per_device(): lax.psum_scatter(grad_weight_ffo.astype(jnp.bfloat16), 'dp', scatter_dime...  78 us
    dot_general x1, matrix products, per_device(): jnp.dot(hidden_low, fetched[6], preferred_element_type=f32)  70.6 us
    dot_general x2, matrix products, block_terms(): jnp.einsum('rhqd,rkhd->rhqk', grad_attn, value_part, preferred_element_ty...  61 us
  transfers between devices with their start and end apart: 11, of which 6 were waited for; matrix products, arithmetic and copies ran while one was open for 23% of the time, Pallas kernels for 0%

commit v1 on v0

v1 whole, which is shorter than its diff:
```python
import functools
import math

import jax
import jax.numpy as jnp
from jax import lax
from jax.experimental import pallas as pl
from jax.experimental.pallas import tpu as pltpu
from jax.sharding import PartitionSpec as P

H = 12
HD = 64
PAIR = 2 * HD
LANES = 128
f32 = jnp.float32
bf16 = jnp.bfloat16
SCORE_SCALE = 1.0 / math.sqrt(HD)
EXP2_SCALE = SCORE_SCALE * math.log2(math.e)
MASKED = -1e30
VMEM_LIMIT = 60 << 20
BLOCK = 256
WINDOWS = (2, 3, 4, 5, 6)


def dot(a, b):
    return jnp.dot(a, b, preferred_element_type=f32)


def dot_nt(a, b):
    return lax.dot_general(a, b, (((1,), (1,)), ((), ())), preferred_element_type=f32)


def dot_tn(a, b):
    return lax.dot_general(a, b, (((0,), (0,)), ((), ())), preferred_element_type=f32)


def column_sum(values):
    return jnp.sum(values, axis=0, keepdims=True)


def shape_of(shape, dtype):
    return jax.ShapeDtypeStruct(shape, dtype)


def project_kernel(x_ref, w_ref, b_ref, out_ref, outT_ref):
    low = (dot(x_ref[...], w_ref[...]) + b_ref[0:1, :]).astype(bf16)
    out_ref[...] = low
    outT_ref[...] = low.T


def project(x, weight, bias, block):
    tokens, width = x.shape
    columns = weight.shape[1]
    return pl.pallas_call(
        project_kernel,
        grid=(tokens // block,),
        in_specs=[
            pl.BlockSpec((block, width), lambda i: (i, 0)),
            pl.BlockSpec((width, columns), lambda i: (0, 0), pipeline_mode=pl.Buffered(1)),
            pl.BlockSpec((8, columns), lambda i: (0, 0), pipeline_mode=pl.Buffered(1)),
        ],
        out_specs=[
            pl.BlockSpec((block, columns), lambda i: (i, 0)),
            pl.BlockSpec((columns, block), lambda i: (0, i)),
        ],
        out_shape=[shape_of((tokens, columns), bf16), shape_of((columns, tokens), bf16)],
        compiler_params=pltpu.CompilerParams(vmem_limit_bytes=VMEM_LIMIT),
        cost_estimate=pl.CostEstimate(
            flops=2 * tokens * width * columns,
            bytes_accessed=2 * (tokens * width + width * columns + 2 * tokens * columns),
            transcendentals=0,
        ),
        name="project",
    )(x, weight, bias)


def passage_range(bounds_ref, row, start, size, row_len):
    first = jnp.int32(0)
    last = jnp.int32(row_len)
    for j in range(bounds_ref.shape[1]):
        bound = bounds_ref[row, j]
        first = jnp.where(bound <= start, jnp.maximum(first, bound), first)
        last = jnp.where(bound >= start + size, jnp.minimum(last, bound), last)
    return first, last


def segments_at(bounds_ref, row, positions):
    count = jnp.zeros(positions.shape, jnp.int32)
    for j in range(bounds_ref.shape[1]):
        count = count + (positions >= bounds_ref[row, j]).astype(jnp.int32)
    return count


def with_window(first, last, row_len, body):
    first_tile = first // LANES
    needed = (last + LANES - 1) // LANES - first_tile
    below = 0
    for tiles in WINDOWS:

        @pl.when((needed > below) & (needed <= tiles))
        def _(tiles=tiles):
            start = jnp.minimum(first_tile, row_len // LANES - tiles)
            body(pl.multiple_of(start * LANES, LANES), tiles * LANES)

        below = tiles


def mask_bias(bounds_ref, row, sub_start, sub_len, lane_start, lane_len):
    down = segments_at(
        bounds_ref, row, sub_start + lax.broadcasted_iota(jnp.int32, (sub_len, LANES), 0)
    )
    across = segments_at(
        bounds_ref, row, lane_start + lax.broadcasted_iota(jnp.int32, (1, lane_len), 1)
    )
    down = jnp.concatenate([down] * (lane_len // LANES), axis=1)
    return jnp.where(down == across, 0.0, MASKED).astype(f32)


def head_rows(h):
    return slice(HD * h, HD * h + HD)


def pair_lanes(h):
    return slice(PAIR * (h // 2), PAIR * (h // 2) + PAIR)


def in_pair(h, rows):
    zero = jnp.zeros_like(rows)
    return jnp.concatenate([rows, zero] if h % 2 == 0 else [zero, rows], axis=0)


def attend_kernel(bounds_ref, k_ref, qT_ref, vT_ref, out_ref, outT_ref, log_ref, bias_ref):
    row = pl.program_id(0)
    row_len, width = k_ref.shape
    block = qT_ref.shape[1]
    heads = width // HD
    q_start = pl.program_id(1) * block
    first, last = passage_range(bounds_ref, row, q_start, block, row_len)

    def body(start, window):
        keys = pl.ds(start, window)
        bias_ref[:window, :] = mask_bias(bounds_ref, row, start, window, q_start, block)

        def score(h):
            return dot(k_ref[keys, pair_lanes(h)], in_pair(h, qT_ref[head_rows(h), :]))

        def weigh(scores):
            masked = scores + bias_ref[:window, :]
            best = jnp.max(masked, axis=0, keepdims=True)
            return best, jnp.exp2((masked - best) * EXP2_SCALE).astype(bf16)

        def attend(h, best, weights):
            values = jnp.concatenate(
                [vT_ref[head_rows(h), keys], jnp.ones((16, window), bf16)], axis=0
            )
            summed = dot(values, weights)
            total = summed[HD : HD + 1]
            outT_ref[head_rows(h), :] = (summed[:HD] * (1.0 / total)).astype(bf16)
            log_ref[h : h + 1, :] = best * EXP2_SCALE + jnp.log2(total)

        scores = [score(0), score(1)]
        held = None
        for h in range(0, heads, 2):
            now = scores
            if h + 2 < heads:
                scores = [score(h + 2), score(h + 3)]
            weighed = [weigh(s) for s in now]
            if held is not None:
                attend(h - 2, *held[0])
                attend(h - 1, *held[1])
            held = weighed
        attend(heads - 2, *held[0])
        attend(heads - 1, *held[1])

    with_window(first, last, row_len, body)
    out_ref[...] = outT_ref[...].T


def attend_rows(bounds, qkv, qkvT, block):
    rows = bounds.shape[0]
    tokens = qkv.shape[0]
    width = qkv.shape[1] // 3
    row_len = tokens // rows
    blocks = row_len // block
    return pl.pallas_call(
        attend_kernel,
        grid_spec=pltpu.PrefetchScalarGridSpec(
            num_scalar_prefetch=1,
            grid=(rows, blocks),
            in_specs=[
                pl.BlockSpec((row_len, width), lambda r, b, s: (r, 1)),
                pl.BlockSpec((width, block), lambda r, b, s: (0, r * blocks + b)),
                pl.BlockSpec((width, row_len), lambda r, b, s: (2, r)),
            ],
            out_specs=[
                pl.BlockSpec((block, width), lambda r, b, s: (r * blocks + b, 0)),
                pl.BlockSpec((width, block), lambda r, b, s: (0, r * blocks + b)),
                pl.BlockSpec((16, block), lambda r, b, s: (0, r * blocks + b)),
            ],
            scratch_shapes=[pltpu.VMEM((max(WINDOWS) * LANES, block), f32)],
        ),
        out_shape=[
            shape_of((tokens, width), bf16),
            shape_of((width, tokens), bf16),
            shape_of((16, tokens), f32),
        ],
        compiler_params=pltpu.CompilerParams(vmem_limit_bytes=VMEM_LIMIT),
        cost_estimate=pl.CostEstimate(
            flops=16 * tokens * row_len * width // 4,
            bytes_accessed=10 * tokens * width,
            transcendentals=0,
        ),
        name="attend",
    )(bounds, qkv, qkvT, qkvT)


def attend_back_kernel(
    bounds_ref, k_ref, kT_ref, v_ref, q_ref, qT_ref, do_ref, doT_ref, outT_ref, log_ref,
    dq_ref, dk_ref, dv_ref, sum_ref, bias_ref, dqT_ref, delta_ref,
):
    row = pl.program_id(0)
    at = pl.program_id(1)
    row_len, width = q_ref.shape
    block = k_ref.shape[0]
    heads = width // HD
    k_start = at * block

    @pl.when((row == 0) & (at == 0))
    def _():
        sum_ref[...] = jnp.zeros(sum_ref.shape, f32)

    @pl.when(at == 0)
    def _():
        dqT_ref[...] = jnp.zeros(dqT_ref.shape, f32)
        for h in range(heads):
            both = doT_ref[head_rows(h), :].astype(f32) * outT_ref[head_rows(h), :].astype(f32)
            delta_ref[h : h + 1, :] = column_sum(both)

    first, last = passage_range(bounds_ref, row, k_start, block, row_len)
    low_half = lax.broadcasted_iota(jnp.int32, (block, PAIR), 1) < HD

    def body(start, window):
        queries = pl.ds(start, window)
        bias_ref[:, :window] = mask_bias(bounds_ref, row, k_start, block, start, window)
        even = {}

        def products(h):
            lanes = pair_lanes(h)
            scores = dot(k_ref[:, lanes], in_pair(h, qT_ref[head_rows(h), queries]))
            grad_prob = dot(v_ref[:, lanes], in_pair(h, doT_ref[head_rows(h), queries]))
            return scores, grad_prob

        def weigh(h, scores, grad_prob):
            shift = bias_ref[:, :window] - log_ref[h : h + 1, queries]
            probs = jnp.exp2(scores * EXP2_SCALE + shift)
            grad_score = probs * (grad_prob - delta_ref[h : h + 1, queries])
            return probs.astype(bf16), grad_score.astype(bf16)

        def gather(h, probs, grad_score):
            lanes = pair_lanes(h)
            dv = dot(probs, do_ref[queries, lanes])
            dk = dot(grad_score, q_ref[queries, lanes])
            dqT_ref[head_rows(h), queries] += dot(kT_ref[head_rows(h), :], grad_score)
            if h % 2 == 0:
                even[0] = (dv, dk)
            else:
                dk_ref[:, lanes] = (jnp.where(low_half, even[0][1], dk) * SCORE_SCALE).astype(bf16)
                dv_ref[:, lanes] = jnp.where(low_half, even[0][0], dv).astype(bf16)

        made = products(0)
        held = None
        for h in range(heads):
            now = made
            if h + 1 < heads:
                made = products(h + 1)
            weighed = weigh(h, *now)
            if held is not None:
                gather(h - 1, *held)
            held = weighed
        gather(heads - 1, *held)

    with_window(first, last, row_len, body)
    sum_ref[1:2, :] += column_sum(dv_ref[...].astype(f32))

    @pl.when(at == pl.num_programs(1) - 1)
    def _():
        dq = (dqT_ref[...] * SCORE_SCALE).astype(bf16).T
        dq_ref[...] = dq
        sum_ref[0:1, :] += column_sum(dq.astype(f32))


def attend_rows_back(bounds, qkv, qkvT, do, doT, outT, log, block):
    rows = bounds.shape[0]
    tokens, width = do.shape
    row_len = tokens // rows
    blocks = row_len // block
    whole = pl.BlockSpec((row_len, width), lambda r, b, s: (r, 0))
    wholeT = pl.BlockSpec((width, row_len), lambda r, b, s: (0, r))
    part = pl.BlockSpec((block, width), lambda r, b, s: (r * blocks + b, 0))
    return pl.pallas_call(
        attend_back_kernel,
        grid_spec=pltpu.PrefetchScalarGridSpec(
            num_scalar_prefetch=1,
            grid=(rows, blocks),
            in_specs=[
                pl.BlockSpec((block, width), lambda r, b, s: (r * blocks + b, 1)),
                pl.BlockSpec((width, block), lambda r, b, s: (1, r * blocks + b)),
                pl.BlockSpec((block, width), lambda r, b, s: (r * blocks + b, 2)),
                whole,
                wholeT,
                whole,
                wholeT,
                wholeT,
                pl.BlockSpec((16, row_len), lambda r, b, s: (0, r)),
            ],
            out_specs=[whole, part, part, pl.BlockSpec((8, width), lambda r, b, s: (0, 0))],
            scratch_shapes=[
                pltpu.VMEM((block, max(WINDOWS) * LANES), f32),
                pltpu.VMEM((width, row_len), f32),
                pltpu.VMEM((16, row_len), f32),
            ],
        ),
        out_shape=[shape_of((tokens, width), bf16)] * 3 + [shape_of((8, width), f32)],
        compiler_params=pltpu.CompilerParams(vmem_limit_bytes=VMEM_LIMIT),
        cost_estimate=pl.CostEstimate(
            flops=40 * tokens * row_len * width // 4,
            bytes_accessed=22 * tokens * width,
            transcendentals=0,
        ),
        name="attend_back",
    )(bounds, qkv, qkvT, qkv, qkv, qkvT, do, doT, outT, log)


def gelu_and_slope(x):
    share = 0.5 + 0.5 * lax.erf(x * math.sqrt(0.5))
    density = jnp.exp(x * x * -0.5) * (1.0 / math.sqrt(2.0 * math.pi))
    return x * share, share + x * density


def normalise(values):
    centred = values - jnp.mean(values, axis=-1, keepdims=True)
    scale = lax.rsqrt(jnp.mean(centred * centred, axis=-1, keepdims=True) + 1e-06)
    return centred * scale, scale


def normalise_back(grad, normed, scale):
    along = jnp.mean(grad * normed, axis=-1, keepdims=True)
    return scale * (grad - jnp.mean(grad, axis=-1, keepdims=True) - normed * along)


def dense_kernel(
    attn_ref, x_ref, cot_ref, wo_ref, wi_ref, wf_ref, vec_ref, bi_ref,
    out_ref, act_ref, gp_ref, gs_ref, low_ref, gr1_ref, gb_ref, do_ref, doT_ref, sum_ref,
    sum_in_ref, slope_ref, *, chunk,
):
    width = x_ref.shape[1]
    inner = wi_ref.shape[1]
    bias_out, gain_a, shift_a, bias_ffo, gain_f, shift_f = [vec_ref[j : j + 1, :] for j in range(6)]

    @pl.when(pl.program_id(0) == 0)
    def _():
        sum_ref[...] = jnp.zeros(sum_ref.shape, f32)
        sum_in_ref[...] = jnp.zeros(sum_in_ref.shape, f32)

    branch = dot(attn_ref[...], wo_ref[...]) + bias_out
    normed_a, scale_a = normalise(x_ref[...].astype(f32) + branch)
    hidden = normed_a * gain_a + shift_a
    low = hidden.astype(bf16)
    low_ref[...] = low
    cuts = [slice(c * chunk, (c + 1) * chunk) for c in range(inner // chunk)]
    last = len(cuts) - 1

    second = None
    held = None
    made = dot(low, wi_ref[:, cuts[0]])
    for c, cut in enumerate(cuts):
        pre = made + bi_ref[0:1, cut]
        if c < last:
            made = dot(low, wi_ref[:, cuts[c + 1]])
        value, slope = gelu_and_slope(pre)
        value = value.astype(bf16)
        act_ref[:, cut] = value
        slope_ref[:, cut] = slope.astype(bf16)
        if held is not None:
            term = dot(held, wf_ref[cuts[c - 1], :])
            second = term if second is None else second + term
        held = value
    term = dot(held, wf_ref[cuts[last], :])
    second = term if second is None else second + term

    normed_f, scale_f = normalise(hidden + (second + bias_ffo))
    out_ref[...] = (normed_f * gain_f + shift_f).astype(bf16)
    cot = cot_ref[...].astype(f32)
    grad_r2 = normalise_back(cot * gain_f, normed_f, scale_f)
    grad_second = grad_r2.astype(bf16)
    gs_ref[...] = grad_second
    sum_ref[0:1, :] += column_sum(cot * normed_f)
    sum_ref[1:2, :] += column_sum(cot)
    sum_ref[2:3, :] += column_sum(grad_second.astype(f32))

    grad_hidden = grad_r2
    held = None
    made = dot_nt(grad_second, wf_ref[cuts[0], :])
    for c, cut in enumerate(cuts):
        grad_act = made
        if c < last:
            made = dot_nt(grad_second, wf_ref[cuts[c + 1], :])
        grad_pre = (grad_act * slope_ref[:, cut].astype(f32)).astype(bf16)
        gp_ref[:, cut] = grad_pre
        sum_in_ref[0:1, cut] += column_sum(grad_pre.astype(f32))
        if held is not None:
            grad_hidden = grad_hidden + dot_nt(held, wi_ref[:, cuts[c - 1]])
        held = grad_pre
    grad_hidden = grad_hidden + dot_nt(held, wi_ref[:, cuts[last]])

    grad_r1 = normalise_back(grad_hidden * gain_a, normed_a, scale_a)
    gr1_ref[...] = grad_r1
    grad_branch = grad_r1.astype(bf16)
    gb_ref[...] = grad_branch
    sum_ref[3:4, :] += column_sum(grad_hidden * normed_a)
    sum_ref[4:5, :] += column_sum(grad_hidden)
    sum_ref[5:6, :] += column_sum(grad_branch.astype(f32))
    grad_attn = dot_nt(grad_branch, wo_ref[...]).astype(bf16)
    do_ref[...] = grad_attn
    doT_ref[...] = grad_attn.T


def dense(attn, x, cot, w_out, w_in, w_ffo, vectors, bias_in, block, chunk):
    tokens, width = x.shape
    inner = w_in.shape[1]
    narrow = pl.BlockSpec((block, width), lambda i: (i, 0))
    wide = pl.BlockSpec((block, inner), lambda i: (i, 0))

    def held(a):
        return pl.BlockSpec(a.shape, lambda i: (0, 0), pipeline_mode=pl.Buffered(1))

    return pl.pallas_call(
        functools.partial(dense_kernel, chunk=chunk),
        grid=(tokens // block,),
        in_specs=[narrow, narrow, narrow]
        + [held(a) for a in (w_out, w_in, w_ffo, vectors, bias_in)],
        out_specs=[
            narrow, wide, wide, narrow, narrow, narrow, narrow, narrow,
            pl.BlockSpec((width, block), lambda i: (0, i)),
            pl.BlockSpec((8, width), lambda i: (0, 0)),
            pl.BlockSpec((8, inner), lambda i: (0, 0)),
        ],
        out_shape=[
            shape_of((tokens, width), bf16),
            shape_of((tokens, inner), bf16),
            shape_of((tokens, inner), bf16),
            shape_of((tokens, width), bf16),
            shape_of((tokens, width), bf16),
            shape_of((tokens, width), f32),
            shape_of((tokens, width), bf16),
            shape_of((tokens, width), bf16),
            shape_of((width, tokens), bf16),
            shape_of((8, width), f32),
            shape_of((8, inner), f32),
        ],
        scratch_shapes=[pltpu.VMEM((block, inner), bf16)],
        compiler_params=pltpu.CompilerParams(vmem_limit_bytes=VMEM_LIMIT),
        cost_estimate=pl.CostEstimate(
            flops=2 * tokens * width * (2 * width + 4 * inner),
            bytes_accessed=tokens * (22 * width + 4 * inner) + 4 * width * inner,
            transcendentals=2 * tokens * inner,
        ),
        name="dense",
    )(attn, x, cot, w_out, w_in, w_ffo, vectors, bias_in)


def split_heads(values):
    return values.reshape(values.shape[0], values.shape[1], H, HD)


def gathered_probs(queries, keys, allowed):
    scores = jnp.einsum("rqhd,rkhd->rhqk", queries, keys, preferred_element_type=f32)
    return jax.nn.softmax(jnp.where(allowed, scores * SCORE_SCALE, MASKED), axis=-1)


def attend_gathered(bounds, qkv, rows, seq_index):
    width = qkv.shape[1] // 3
    parts = qkv.reshape(rows, -1, 3 * width)
    tok_seq = parts.shape[1]
    whole = lax.all_gather(parts[:, :, width:], "seq", axis=1, tiled=True)
    row_len = whole.shape[1]
    queries = split_heads(parts[:, :, :width])
    keys = split_heads(whole[:, :, :width])
    values = split_heads(whole[:, :, width:])
    positions = jnp.arange(row_len, dtype=jnp.int32)
    segments = jnp.sum((positions[None, :, None] >= bounds[:, None, :]).astype(jnp.int32), axis=2)
    mine = lax.dynamic_slice_in_dim(segments, seq_index * tok_seq, tok_seq, 1)
    allowed = mine[:, None, :, None] == segments[:, None, None, :]
    probs = gathered_probs(queries, keys, allowed)
    attended = jnp.einsum(
        "rhqk,rkhd->rqhd", probs.astype(bf16), values, preferred_element_type=f32
    )
    return attended.astype(bf16).reshape(-1, width), (queries, keys, values, allowed)


def attend_gathered_back(saved, attn, do):
    queries, keys, values, allowed = saved
    rows, tok_seq = queries.shape[:2]
    width = attn.shape[1]
    probs = gathered_probs(queries, keys, allowed)
    do = do.reshape(rows, tok_seq, H, HD)
    delta = jnp.sum(do.astype(f32) * attn.reshape(do.shape).astype(f32), axis=-1)
    grad_prob = jnp.einsum("rqhd,rkhd->rhqk", do, values, preferred_element_type=f32)
    grad_score = (probs * (grad_prob - delta.transpose(0, 2, 1)[..., None])).astype(bf16)
    dq = jnp.einsum("rhqk,rkhd->rqhd", grad_score, keys, preferred_element_type=f32) * SCORE_SCALE
    dk = (
        jnp.einsum("rhqk,rqhd->rkhd", grad_score, queries, preferred_element_type=f32)
        * SCORE_SCALE
    )
    dv = jnp.einsum("rhqk,rqhd->rkhd", probs.astype(bf16), do, preferred_element_type=f32)
    pair = jnp.concatenate([dk.reshape(rows, -1, width), dv.reshape(rows, -1, width)], axis=-1)
    pair = lax.psum_scatter(pair.astype(bf16), "seq", scatter_dimension=1, tiled=True)
    pair = pair.reshape(-1, 2 * width)
    dq = dq.astype(bf16).reshape(-1, width)
    dk, dv = pair[:, :width], pair[:, width:]
    sums = jnp.stack([jnp.sum(dq.astype(f32), axis=0), jnp.sum(dv.astype(f32), axis=0)])
    return dq, dk, dv, sums


def rows_of(values, seq_index, seq_count):
    rows, part, width = values.shape
    mine = rows // seq_count
    whole = jnp.zeros((mine, part * seq_count, width), values.dtype)
    for step in range(seq_count):
        to = (seq_index + step) % seq_count
        source = (seq_index - step) % seq_count
        piece = lax.dynamic_slice_in_dim(values, to * mine, mine, 0)
        if step:
            piece = lax.ppermute(
                piece, "seq", [(s, (s + step) % seq_count) for s in range(seq_count)]
            )
        whole = lax.dynamic_update_slice_in_dim(whole, piece, source * part, 1)
    return whole


def parts_of(values, seq_index, seq_count):
    mine, row_len, width = values.shape
    part = row_len // seq_count
    parts = jnp.zeros((mine * seq_count, part, width), values.dtype)
    for step in range(seq_count):
        to = (seq_index + step) % seq_count
        source = (seq_index - step) % seq_count
        piece = lax.dynamic_slice_in_dim(values, to * part, part, 1)
        if step:
            piece = lax.ppermute(
                piece, "seq", [(s, (s + step) % seq_count) for s in range(seq_count)]
            )
        parts = lax.dynamic_update_slice_in_dim(parts, piece, source * mine, 0)
    return parts


def per_device(
    tokens,
    weight_qkv,
    bias_qv,
    weight_out,
    bias_out,
    gain_attn,
    shift_attn,
    weight_in,
    bias_in,
    weight_ffo,
    bias_ffo,
    gain_ffn,
    shift_ffn,
    lengths,
    cotangent,
):
    rows, tok_seq, width = tokens.shape
    seq_count = lax.axis_size("seq")
    seq_index = lax.axis_index("seq")
    whole_rows = rows % seq_count == 0
    inner = weight_in.shape[1]
    shard = weight_qkv.shape[0]
    token_count = rows * tok_seq

    small = (bias_qv, bias_out, gain_attn, shift_attn, bias_in, bias_ffo, gain_ffn, shift_ffn)
    small_cols = [v.shape[0] // shard for v in small]
    packed = jnp.concatenate([v.reshape(shard, -1) for v in small], axis=1)
    packed = jnp.pad(packed, ((0, 0), (0, LANES - packed.shape[1])))
    first = jnp.concatenate([weight_qkv, packed], axis=1).astype(bf16)
    first = lax.all_gather(first, "dp", axis=0, tiled=True)
    w_qkv = first[:, : 3 * width]
    vectors = []
    at = 3 * width
    for cols in small_cols:
        vectors.append(first[:, at : at + cols].astype(f32).reshape(-1))
        at += cols
    v_qv, v_out, v_ga, v_sa, v_in, v_ffo, v_gf, v_sf = vectors
    w_out = lax.all_gather(weight_out.astype(bf16), "dp", axis=0, tiled=True)
    w_in = lax.all_gather(weight_in.astype(bf16), "dp", axis=0, tiled=True)
    w_ffo = lax.all_gather(weight_ffo.astype(bf16), "dp", axis=0, tiled=True)
    qkv_bias = jnp.concatenate([v_qv[:width], jnp.zeros((width,), f32), v_qv[width:]])
    qkv_bias = jnp.broadcast_to(qkv_bias[None], (8, 3 * width))
    vec = jnp.stack([v_out, v_ga, v_sa, v_ffo, v_gf, v_sf, v_sf, v_sf])
    in_bias = jnp.broadcast_to(v_in[None], (8, inner))

    bounds = jnp.cumsum(lengths, axis=1)
    if whole_rows:
        mine = rows // seq_count
        bounds = lax.dynamic_slice_in_dim(bounds, seq_index * mine, mine, 0)
        x = rows_of(tokens, seq_index, seq_count).reshape(token_count, width)
        cot = rows_of(cotangent, seq_index, seq_count).reshape(token_count, width)
    else:
        x = tokens.reshape(token_count, width)
        cot = cotangent.reshape(token_count, width)

    qkv, qkvT = project(x, w_qkv, qkv_bias, BLOCK)
    if whole_rows:
        attn, attnT, log = attend_rows(bounds, qkv, qkvT, BLOCK)
    else:
        attn, saved = attend_gathered(bounds, qkv, rows, seq_index)
    out, act, gp, gs, low, gr1, gb, do, doT, sums, sums_in = dense(
        attn, x, cot, w_out, w_in, w_ffo, vec, in_bias, BLOCK, width
    )
    grad_w_ffo = dot_tn(act, gs).astype(bf16)
    grad_w_in = dot_tn(low, gp).astype(bf16)
    grad_w_out = dot_tn(attn, gb).astype(bf16)
    if whole_rows:
        dq, dk, dv, sums_qv = attend_rows_back(bounds, qkv, qkvT, do, doT, attnT, log, BLOCK)
    else:
        dq, dk, dv, sums_qv = attend_gathered_back(saved, attn, do)
    grad_qkv = jnp.concatenate([dq, dk, dv], axis=1)
    grad_w_qkv = dot_tn(x, grad_qkv).astype(bf16)
    grad_x = (gr1 + dot_nt(grad_qkv, w_qkv)).astype(bf16)

    if whole_rows:
        out = parts_of(out.reshape(mine, -1, width), seq_index, seq_count)
        grad_x = parts_of(grad_x.reshape(mine, -1, width), seq_index, seq_count)
    else:
        out = out.reshape(rows, tok_seq, width)
        grad_x = grad_x.reshape(rows, tok_seq, width)

    def scatter(values):
        return lax.psum_scatter(values, "dp", scatter_dimension=0, tiled=True)

    small_grads = (
        sums_qv[:2].reshape(-1), sums[5], sums[3], sums[4], sums_in[0], sums[2], sums[0], sums[1],
    )
    dp_count = lax.axis_size("dp")
    packed = jnp.concatenate([v.reshape(dp_count * shard, -1) for v in small_grads], axis=1)
    packed = jnp.pad(packed, ((0, 0), (0, LANES - packed.shape[1]))).astype(bf16)
    last = scatter(jnp.concatenate([grad_w_qkv, packed], axis=1))
    shared = lax.psum(
        (scatter(grad_w_ffo), scatter(grad_w_in), scatter(grad_w_out), last), "seq"
    )
    d_ffo, d_in, d_out, last = [v.astype(f32) for v in shared]
    d_small = []
    at = 3 * width
    for cols in small_cols:
        d_small.append(last[:, at : at + cols].reshape(-1))
        at += cols
    g_qv, g_bo, g_ga, g_sa, g_bi, g_bf, g_gf, g_sf = d_small
    return (
        out, grad_x, last[:, : 3 * width], g_qv, d_out, g_bo, g_ga, g_sa, d_in, g_bi, d_ffo,
        g_bf, g_gf, g_sf,
    )


def solution(mesh):
    by_token = P("dp", "seq", None)
    weight = P("dp", None)
    vector = P("dp")
    params = (
        weight, vector, weight, vector, vector, vector, weight, vector, weight, vector, vector,
        vector,
    )
    return jax.shard_map(
        per_device,
        mesh=mesh,
        in_specs=(by_token,) + params + (weight, by_token),
        out_specs=(by_token, by_token) + params,
        check_vma=False,
    )
```

time: 1410 us -> 687 us (0.49)
  matrix products: 508 us -> 55.4 us
  Pallas kernels: 0 us -> 144 us
  waiting for transfers between devices: 511 us -> 381 us
  blocking collectives: 110 us -> 0 us
  other arithmetic: 114 us -> 24.3 us
  local copies, waits for them, and re-layouts: 133 us -> 60.1 us
    dot_general x24 -> x5, matrix products: 508 us -> 55.4 us  [the longest x4 43.8 us: dot_tn(): lax.dot_general(a, b, (((0,), (0,)), ((), ())), preferred_element_type=f32)]
    pallas_call x0 -> x4, Pallas kernels: none -> 144 us  [the longest x1 68.6 us: dense(): pl.pallas_call(functools.partial(dense_kernel, chunk=chunk), grid=(tokens...]
    reduce_scatter x4, waiting for transfers between devices: 353 us -> 213 us  [scatter(): return lax.psum_scatter(values, 'dp', scatter_dimension=0, tiled=True)]
    unnamed x2 -> x0, blocking collectives: 105 us -> none
    reduce_sum x12 -> x0, other arithmetic: 64.7 us -> none  [the longest x1 41.6 us: attend_block(): norm_sum = jnp.sum(weights, axis=-1)]
    all_gather x5 -> x4, waiting for transfers between devices: 134 us -> 71.5 us  [the longest x1 54.5 us: per_device(): w_in = lax.all_gather(weight_in.astype(bf16), 'dp', axis=0, tiled=True)]
    ppermute x0 -> x4, waiting for transfers between devices: none -> 61.7 us  [the longest x2 61.7 us: rows_of(): lax.ppermute(piece, 'seq', [(s, (s + step) % seq_count) for s in range(se...]
    psum x1, waiting for transfers between devices: 0.01 us -> 34.5 us  [per_device(): lax.psum((scatter(grad_w_ffo), scatter(grad_w_in), scatter(grad_w_out), l...]
  transfers between devices with their start and end apart: 11 -> 13, of which waited for: 6 -> 8; matrix products, arithmetic and copies ran while one was open for 23% -> 14% of each run, Pallas kernels for 0% -> 5%
where the time goes in v1:
time: 687 us; the launch traced here: 680 us
  waiting for transfers between devices  381 us (55%)
  Pallas kernels  144 us (21%)
  local copies, waits for them, and re-layouts  60.1 us (9%)
  matrix products  55.4 us (8%)
  other arithmetic  24.3 us (4%)
  between operations  14.5 us (2%)
    reduce_scatter x4, waiting for transfers between devices, scatter(): return lax.psum_scatter(values, 'dp', scatter_dimension=0, tiled=True)  213 us
    pallas_call x1, Pallas kernels, dense(): pl.pallas_call(functools.partial(dense_kernel, chunk=chunk), grid=(tokens...  68.6 us
    ppermute x2, waiting for transfers between devices, rows_of(): lax.ppermute(piece, 'seq', [(s, (s + step) % seq_count) for s in range(se...  61.7 us
    all_gather x1, waiting for transfers between devices, per_device(): w_in = lax.all_gather(weight_in.astype(bf16), 'dp', axis=0, tiled=True)  54.5 us
    dot_general x4, matrix products, dot_tn(): lax.dot_general(a, b, (((0,), (0,)), ((), ())), preferred_element_type=f32)  43.8 us
    pallas_call x1, Pallas kernels, attend_rows_back(): pl.pallas_call(attend_back_kernel, grid_spec=pltpu.PrefetchScalarGridSpec...  38.7 us
    psum x1, waiting for transfers between devices, per_device(): lax.psum((scatter(grad_w_ffo), scatter(grad_w_in), scatter(grad_w_out), l...  34.5 us
    pallas_call x1, Pallas kernels, attend_rows(): pl.pallas_call(attend_kernel, grid_spec=pltpu.PrefetchScalarGridSpec(num_...  22.7 us
  transfers between devices with their start and end apart: 13, of which 8 were waited for; matrix products, arithmetic and copies ran while one was open for 14% of the time, Pallas kernels for 5%

profile of v1, /device:TPU:12, one launch (start us, length us, event | category | flops | bytes accessed | tf_op | source)
XLA Modules:
  0.0 680.2 jit_solution(13549926201286116136)
XLA Ops:
  7.2 1.0 convert.78
  15.4 1.7 convert_element_type.53
  17.2 1.8 convert_element_type.55
  19.0 1.8 convert_element_type.54
  21.2 1.4 constant_dynamic-slice_fusion.3
  23.3 2.4 copy-done.8
  25.7 1.4 constant_dynamic-slice_fusion.2
  28.4 31.8 %collective-permute-done = bf16[2,512,768]{2,1,0:T(8,128)(2,1)} collective-permute-done((bf16[2,512,768]{2,1,0:T(8,128)(2,1)}, bf16[2,512,768]{2,1,0:T(8,128)(2,1)}, u32[]{:S(2)}, u32[]{:S(2)}) %collective-permute-start) | collective-permute-done | bytes 1572896 | tf_op jit(solution)/shard_map/ppermute | solution.py:534
  60.2 2.7 constant_dynamic-update-slice_fusion.5
  62.9 29.8 %collective-permute-done.1 = bf16[2,512,768]{2,1,0:T(8,128)(2,1)} collective-permute-done((bf16[2,512,768]{2,1,0:T(8,128)(2,1)}, bf16[2,512,768]{2,1,0:T(8,128)(2,1)}, u32[]{:S(2)}, u32[]{:S(2)}) %collective-permute-start.1) | collective-permute-done | bytes 1572896 | tf_op jit(solution)/shard_map/ppermute | solution.py:534
  92.8 1.6 constant_dynamic-update-slice_fusion.4
  94.4 1.2 slice_convert_fusion.1
  96.5 2.5 slice_reduce_fusion
  99.7 1.0 slice_convert_fusion
  101.0 4.2 slice.128.w_ref
  105.8 13.9 %project.1 = (bf16[2048,2304]{1,0:T(8,128)(2,1)}, bf16[2304,2048]{1,0:T(8,128)(2,1)}) custom-call(bf16[2048,768]{1,0:T(8,128)(2,1)} %bitcast.41, bf16[768,2304]{1,0:T(8,128)(2,1)} %slice.128.w_ref, f32[8,2304]{1,0:T(8,128)} %broadcast_in_dim.20.b_ref), custom_call_target="tpu_custom_call" | custom-call | flops 7247757312 | bytes 25559040 | tf_op jit(solution)/shard_map/project/pallas_call | solution.py:54
  119.7 22.7 %attend.1 = (bf16[2048,768]{1,0:T(8,128)(2,1)}, bf16[768,2048]{1,0:T(8,128)(2,1)}, f32[16,2048]{1,0:T(8,128)}) custom-call(s32[2,8]{1,0:T(2,128)} %constant_dynamic-slice_fusion.4.bounds_ref, bf16[2048,2304]{1,0:T(8,128)(2,1)} %get-tuple-element.34.k_ref.v_ref.q_ref, bf16[2304,2048]{1,0:T(8,128)(2,1)} %get-tuple-element.35.qT_ref.vT_ref.kT_ref, ...), custom_call_target="tpu_custom_call" | custom-call | flops 6442450944 | bytes 15728640 | tf_op jit(solution)/shard_map/attend/pallas_call | solution.py:185
  142.4 16.9 %all-gather.11.cloned.1.call-done.wf_ref = bf16[3072,768]{1,0:T(8,128)(2,1)} async-done(((bf16[192,768]{1,0:T(8,128)(2,1)}), bf16[3072,768]{1,0:T(8,128)(2,1)}) %all-gather.11.cloned.1.call-update) | async-done | bytes 4718608 | tf_op jit(solution)/shard_map/all_gather | solution.py:597
  159.3 54.5 %all-gather.9.cloned.1.call-done.wi_ref = bf16[768,3072]{1,0:T(8,128)(2,1)} async-done(((bf16[48,3072]{1,0:T(8,128)(2,1)}), bf16[768,3072]{1,0:T(8,128)(2,1)}) %all-gather.9.cloned.1.call-update) | async-done | bytes 4718608 | tf_op jit(solution)/shard_map/all_gather | solution.py:596
  214.5 68.6 %dense.1 = (bf16[2048,768]{1,0:T(8,128)(2,1)}, bf16[2048,3072]{1,0:T(8,128)(2,1)}, bf16[2048,3072]{1,0:T(8,128)(2,1)}, bf16[2048,768]{1,0:T(8,128)(2,1)}, bf16[2...) custom-call(bf16[2048,768]{1,0:T(8,128)(2,1)} %get-tuple-element.36., ...), custom_call_target="tpu_custom_call" | custom-call | flops 43486543872 | bytes 69206016 | tf_op jit(solution)/shard_map/dense/pallas_call | solution.py:437
  283.2 38.7 %attend_back.1 = (bf16[2048,768]{1,0:T(8,128)(2,1)}, bf16[2048,768]{1,0:T(8,128)(2,1)}, bf16[2048,768]{1,0:T(8,128)(2,1)}, f32[8,768]{1,0:T(8,128)}) custom-call(s32[2,8]{1,0:T(2,128)} %constant_dynamic-slice_fusion.4.bounds_ref, bf16[2048,2304]{1,0:T(8,128)(2,1)} %get-tuple-element.34.k_ref.v_ref.q_ref, ...), custom_call_target="tpu_custom_call" | custom-call | flops 16106127360 | bytes 34603008 | tf_op jit(solution)/shard_map/attend_back/pallas_call | solution.py:300
  328.5 1.1 reshape_squeeze.31
  329.6 3.9 constant_dynamic-update-slice_fusion.2
  334.5 3.7 convolution_convert_fusion.3
  338.3 1.9 constant_dynamic-update-slice_fusion.1
  340.2 1.1 copy-done
  341.3 1.9 constant_dynamic-update-slice_fusion
  343.2 2.6 concatenate.25
  345.8 11.1 %convolution_convert_fusion.2 = bf16[768,2304]{1,0:T(8,128)(2,1)S(1)} fusion(bf16[2048,768]{1,0:T(8,128)(2,1)S(1)} %bitcast.43, bf16[2048,2304]{1,0:T(8,128)(2,1)} %constant_dynamic-update-slice_fusion), kind=kOutput, calls=%fused_computation.5 | convolution fusion | flops 7249526784 | bytes 16121856 | tf_op jit(solution)/shard_map/dot_general | solution.py:34
  356.9 2.1 fusion.1
  359.1 1.8 copy-done.18
  360.9 14.6 %convolution_convert_fusion = bf16[3072,768]{1,0:T(8,128)(2,1)} fusion(bf16[2048,3072]{1,0:T(8,128)(2,1)} %get-tuple-element.52, bf16[2048,768]{1,0:T(8,128)(2,1)S(1)} %copy-done.18), kind=kOutput, calls=%fused_computation.3 | convolution fusion | flops 9666035712 | bytes 20447232 | tf_op jit(solution)/shard_map/dot_general | solution.py:34
  375.6 1.8 copy-done.17
  377.4 14.4 %convolution_convert_fusion.1 = bf16[768,3072]{1,0:T(8,128)(2,1)} fusion(bf16[2048,768]{1,0:T(8,128)(2,1)S(1)} %copy-done.17, bf16[2048,3072]{1,0:T(8,128)(2,1)} %get-tuple-element.51), kind=kOutput, calls=%fused_computation.4 | convolution fusion | flops 9666035712 | bytes 20447232 | tf_op jit(solution)/shard_map/dot_general | solution.py:34
  391.9 11.6 %fusion.5 = f32[2048,768]{1,0:T(8,128)S(1)} fusion(bf16[2048,2304]{1,0:T(8,128)(2,1)} %constant_dynamic-update-slice_fusion, bf16[768,2432]{1,0:T(8,128)(2,1)} %all-gather.5.cloned.1.call-done), kind=kOutput, calls=%fused_computation.57 | convolution fusion | flops 7247757312 | bytes 19267584 | tf_op jit(solution)/shard_map/dot_general | solution.py:30
  403.5 1.4 add_convert_fusion
  405.2 1.4 constant_dynamic-slice_fusion.1
  406.9 2.9 copy-done.9
  409.8 1.4 constant_dynamic-slice_fusion
  411.3 55.4 %reduce-scatter.5.cloned.1.call-done = bf16[48,2432]{1,0:T(8,128)(2,1)} async-done(((bf16[768,2432]{1,0:T(8,128)(2,1)}), bf16[48,2432]{1,0:T(8,128)(2,1)}) %reduce-scatter.5.cloned.1.call-update) | async-done | bytes 233488 | tf_op jit(solution)/shard_map/reduce_scatter | solution.py:640
  466.6 78.9 %reduce-scatter.11.cloned.1.call-done = bf16[192,768]{1,0:T(8,128)(2,1)} async-done(((bf16[3072,768]{1,0:T(8,128)(2,1)}), bf16[192,768]{1,0:T(8,128)(2,1)}) %reduce-scatter.11.cloned.1.call-update) | async-done | bytes 294928 | tf_op jit(solution)/shard_map/reduce_scatter | solution.py:640
  545.6 78.4 %reduce-scatter.9.cloned.1.call-done = bf16[48,3072]{1,0:T(8,128)(2,1)} async-done(((bf16[768,3072]{1,0:T(8,128)(2,1)}), bf16[48,3072]{1,0:T(8,128)(2,1)}) %reduce-scatter.9.cloned.1.call-update) | async-done | bytes 294928 | tf_op jit(solution)/shard_map/reduce_scatter | solution.py:640
  624.1 2.7 constant_dynamic-update-slice_fusion.6
  626.7 1.6 constant_dynamic-update-slice_fusion.3
  628.3 34.5 %all-reduce.5.cloned.1.call-done = (bf16[48,2432]{1,0:T(8,128)(2,1)}, bf16[48,768]{1,0:T(8,128)(2,1)}, bf16[48,3072]{1,0:T(8,128)(2,1)}, bf16[192,768]{1,0:T(8,128)(2,1)}) async-done(((bf16[48,2432]{1,0:T(8,128)(2,1)}, bf16[48,768]{1,0:T(8,128)(2,1)}, bf16[48,3072]{1,0:T(8,128)(2,1)}, bf16[192,768]{1,0:T(8,128)(2,1)}), (bf16[48,2432]{1,0:T(8,128)(2,1)}, bf16[48,768]{1,0:T(8,128)(2,1)}, ...) | async-done | bytes 897040 | tf_op jit(solution)/shard_map/psum | solution.py:649
  663.9 1.7 slice.147
  667.1 1.8 convert_element_type.62
  668.9 1.8 convert_element_type.64
  (123 shorter events, 26.3 us)
Async XLA Ops:
  7.2 87.2 %all-gather.5.cloned.1.call-start = ((), (), s32[]{:S(2)}) async-start(), calls=%async_computation.4 | async-start | bytes 3969024 | tf_op jit(solution)/shard_map/all_gather | solution.py:587
  15.3 5.9 copy-start.7
  15.3 127.1 %all-gather.7.cloned.1.call-start = ((), (), s32[]{:S(2)}) async-start(), calls=%async_computation.5 | async-start | bytes 1253376 | tf_op jit(solution)/shard_map/all_gather | solution.py:595
  17.1 142.2 %all-gather.11.cloned.1.call-start = ((), (), s32[]{:S(2)}) async-start(), calls=%async_computation.7 | async-start | bytes 5013504 | tf_op jit(solution)/shard_map/all_gather | solution.py:597
  19.0 194.9 %all-gather.9.cloned.1.call-start = ((), (), s32[]{:S(2)}) async-start(), calls=%async_computation.6 | async-start | bytes 5013504 | tf_op jit(solution)/shard_map/all_gather | solution.py:596
  20.9 390.4 %reduce-scatter.7.cloned.1.call-start = ((), (), s32[]{:S(2)}) async-start(), calls=%async_computation.9 | async-start | bytes 1253376 | tf_op jit(solution)/shard_map/reduce_scatter | solution.py:640
  22.6 4.5 copy-start.5
  22.6 3.1 copy-start.8
  22.6 37.6 %collective-permute-start = (bf16[2,512,768]{2,1,0:T(8,128)(2,1)}, bf16[2,512,768]{2,1,0:T(8,128)(2,1)}, u32[]{:S(2)}, u32[]{:S(2)}) collective-permute-start(bf16[2,512,768]{2,1,0:T(8,128)(2,1)} %get-tuple-element.76), channel_id=1, source_target_pairs={{0,1},{1,0},{2,3},{3,2},{4,5},{5,4},{6,7},{7,6},{8,9},{9,8},{10,11... | collective-permute-start | bytes 4718600 | tf_op jit(solution)/shard_map/ppermute | solution.py:534
  25.7 2.0 copy-start.14
  27.1 65.6 %collective-permute-start.1 = (bf16[2,512,768]{2,1,0:T(8,128)(2,1)}, bf16[2,512,768]{2,1,0:T(8,128)(2,1)}, u32[]{:S(2)}, u32[]{:S(2)}) collective-permute-start(bf16[2,512,768]{2,1,0:T(8,128)(2,1)} %get-tuple-element.74), channel_id=1, source_target_pairs={{0,1},{1,0},{2,3},{3,2},{4,5},{5,4},{6,7},{7,6},{8,9},{9,8},{10,11... | collective-permute-start | bytes 4718600 | tf_op jit(solution)/shard_map/ppermute | solution.py:534
  94.4 10.8 %copy-start.3 = (bf16[2,1024,768]{2,1,0:T(8,128)(2,1)}, bf16[2,1024,768]{2,1,0:T(8,128)(2,1)S(1)}, u32[]{:S(2)}) copy-start(bf16[2,1024,768]{2,1,0:T(8,128)(2,1)S(1)} %constant_dynamic-update-slice_fusion.4) | copy-start | bytes 9437188
  101.0 4.2 copy-start.13
  283.1 39.9 %copy-start.12 = (f32[8,768]{1,0:T(8,128)S(1)}, f32[8,768]{1,0:T(8,128)}, u32[]{:S(2)}) copy-start(f32[8,768]{1,0:T(8,128)} %get-tuple-element.47) | copy-start | bytes 73732
  329.6 3.9 copy-start.15
  329.6 4.9 copy-start.16
  334.5 3.8 copy-start.1
  338.2 128.4 %reduce-scatter.5.cloned.1.call-start = ((), (), s32[]{:S(2)}) async-start(), calls=%async_computation.8 | async-start | bytes 3969024 | tf_op jit(solution)/shard_map/reduce_scatter | solution.py:640
  338.3 3.0 copy-start
  341.3 4.5 copy-start.6
  345.8 11.1 %copy-start.10 = (bf16[768,12]{1,0:T(8,128)(2,1)S(1)}, bf16[768,12]{1,0:T(8,128)(2,1)}, u32[]{:S(2)}) copy-start(bf16[768,12]{1,0:T(8,128)(2,1)} %concatenate.25) | copy-start | bytes 55300
  359.0 1.9 copy-start.18
  359.0 186.5 %reduce-scatter.11.cloned.1.call-start = ((), (), s32[]{:S(2)}) async-start(), calls=%async_computation.11 | async-start | bytes 5013504 | tf_op jit(solution)/shard_map/reduce_scatter | solution.py:640
  375.5 1.9 copy-start.17
  375.5 248.5 %reduce-scatter.9.cloned.1.call-start = ((), (), s32[]{:S(2)}) async-start(), calls=%async_computation.10 | async-start | bytes 5013504 | tf_op jit(solution)/shard_map/reduce_scatter | solution.py:640
  391.8 11.7 %slice-start = ((s8[6291456]{0:T(1024)(128)(4,1)}), s8[2097152]{0:T(1024)(128)(4,1)S(1)}, s32[]{:S(2)}) async-start(s8[6291456]{0:T(1024)(128)(4,1)} %bitcast.38), calls=%async_computation.13 | async-start | bytes 4194304
  391.9 271.0 %all-reduce.5.cloned.1.call-start = ((), (), s32[]{:S(2)}) async-start(), calls=%async_computation.12 | async-start | bytes 1794048 | tf_op jit(solution)/shard_map/psum | solution.py:649
  391.9 11.6 %slice-start.1 = ((s8[6291456]{0:T(1024)(128)(4,1)}), s8[4194304]{0:T(1024)(128)(4,1)S(1)}, s32[]{:S(2)}) async-start(s8[6291456]{0:T(1024)(128)(4,1)} %bitcast.38), calls=%async_computation.14 | async-start | bytes 8388608
  406.6 4.6 copy-start.4
  406.6 3.2 copy-start.9
  406.6 217.5 %collective-permute-start.3 = (bf16[2,512,768]{2,1,0:T(8,128)(2,1)}, bf16[2,512,768]{2,1,0:T(8,128)(2,1)}, u32[]{:S(2)}, u32[]{:S(2)}) collective-permute-start(bf16[2,512,768]{2,1,0:T(8,128)(2,1)} %get-tuple-element.70), channel_id=1, source_target_pairs={{0,1},{1,0},{2,3},{3,2},{4,5},{5,4},{6,7},{7,6},{8,9},{9,8},{10,11... | collective-permute-start | bytes 4718600 | tf_op jit(solution)/shard_map/ppermute | solution.py:550
  411.2 215.5 %collective-permute-start.2 = (bf16[2,512,768]{2,1,0:T(8,128)(2,1)}, bf16[2,512,768]{2,1,0:T(8,128)(2,1)}, u32[]{:S(2)}, u32[]{:S(2)}) collective-permute-start(bf16[2,512,768]{2,1,0:T(8,128)(2,1)} %get-tuple-element.72), channel_id=1, source_target_pairs={{0,1},{1,0},{2,3},{3,2},{4,5},{5,4},{6,7},{7,6},{8,9},{9,8},{10,11... | collective-permute-start | bytes 4718600 | tf_op jit(solution)/shard_map/ppermute | solution.py:550
  628.3 45.2 %copy-start.2 = (bf16[4,512,768]{2,1,0:T(8,128)(2,1)}, bf16[4,512,768]{2,1,0:T(8,128)(2,1)S(1)}, u32[]{:S(2)}) copy-start(bf16[4,512,768]{2,1,0:T(8,128)(2,1)S(1)} %constant_dynamic-update-slice_fusion.3) | copy-start | bytes 9437188
  662.9 8.7 %copy-start.11 = (bf16[48,768]{1,0:T(8,128)(2,1)S(1)}, bf16[48,768]{1,0:T(8,128)(2,1)}, u32[]{:S(2)}) copy-start(bf16[48,768]{1,0:T(8,128)(2,1)} %get-tuple-element.67) | copy-start | bytes 221188
Sparse Core Ops, SparseCore 0:
  15.5 49.6 all-gather.4
  67.4 35.9 all-gather.6
  106.3 53.0 all-gather.10
  162.0 51.7 all-gather.8
  338.3 56.4 reduce-scatter.6
  398.6 67.9 reduce-scatter.4
  471.0 74.5 reduce-scatter.10
  549.4 74.5 reduce-scatter.8
  626.7 36.0 all-reduce.4

commit v2 on v1

--- a/solution.py
+++ b/solution.py
@@ -42,36 +42,181 @@
     return jax.ShapeDtypeStruct(shape, dtype)
 
 
-def project_kernel(x_ref, w_ref, b_ref, out_ref, outT_ref):
-    low = (dot(x_ref[...], w_ref[...]) + b_ref[0:1, :]).astype(bf16)
+def vector_rows(sizes):
+    rows = []
+    at = 0
+    for size in sizes:
+        rows.append(at)
+        at += -(-size // LANES)
+    return rows, at
+
+
+def lower_kernel(*refs):
+    w_qkv, w_in, w_ffo, w_out = refs[:4]
+    small = refs[4:-3]
+    first_ref, others_ref, block_ref = refs[-3:]
+    columns = w_qkv.shape[1]
+    shard, width = w_out.shape
+    first_ref[:, :columns] = w_qkv[...].astype(bf16)
+    block_ref[...] = jnp.zeros(block_ref.shape, f32)
+    for ref, row in zip(small, vector_rows([r.shape[1] for r in small])[0]):
+        size = ref.shape[1]
+        for at in range(0, size, LANES):
+            n = min(LANES, size - at)
+            block_ref[row : row + 1, :n] = ref[:, at : at + n]
+            row += 1
+    first_ref[:, columns:] = block_ref[...].astype(bf16)
+    chunks = w_in.shape[1] // width
+    for c in range(chunks):
+        others_ref[c * shard : (c + 1) * shard, :] = w_in[:, c * width : (c + 1) * width].astype(bf16)
+    others_ref[chunks * shard : 2 * chunks * shard, :] = w_ffo[...].astype(bf16)
+    others_ref[2 * chunks * shard :, :] = w_out[...].astype(bf16)
+
+
+def lower(w_qkv, w_in, w_ffo, w_out, small):
+    shard, columns = w_qkv.shape
+    width = w_out.shape[1]
+    chunks = w_in.shape[1] // width
+    return pl.pallas_call(
+        lower_kernel,
+        out_shape=[
+            shape_of((shard, columns + LANES), bf16),
+            shape_of(((2 * chunks + 1) * shard, width), bf16),
+        ],
+        scratch_shapes=[pltpu.VMEM((shard, LANES), f32)],
+        compiler_params=pltpu.CompilerParams(vmem_limit_bytes=VMEM_LIMIT),
+        name="lower",
+    )(w_qkv, w_in, w_ffo, w_out, *[v.reshape(1, -1) for v in small])
+
+
+def spread_vector(block, row, size, shards):
+    total = size * shards
+    place = lax.broadcasted_iota(jnp.int32, (LANES, total), 1) % size
+    lane = lax.broadcasted_iota(jnp.int32, (LANES, total), 0)
+    found = jnp.zeros((shards, total), f32)
+    for at in range(0, size, LANES):
+        pick = jnp.where(place == lane + at, 1.0, 0.0).astype(bf16)
+        found = found + dot(block[:, row + at // LANES, :].astype(bf16), pick)
+    owner = lax.broadcasted_iota(jnp.int32, (shards, total), 0)
+    mine = lax.broadcasted_iota(jnp.int32, (shards, total), 1) // size
+    return column_sum(jnp.where(owner == mine, found, 0.0))
+
+
+def gather_vector(vector, shards):
+    total = vector.shape[1]
+    size = total // shards
+    place = lax.broadcasted_iota(jnp.int32, (total, LANES), 0) % size
+    lane = lax.broadcasted_iota(jnp.int32, (total, LANES), 1)
+    owner = lax.broadcasted_iota(jnp.int32, (shards, total), 0)
+    mine = lax.broadcasted_iota(jnp.int32, (shards, total), 1) // size
+    own = jnp.where(owner == mine, vector, 0.0).astype(bf16)
+    return [
+        dot(own, jnp.where(place == lane + at, 1.0, 0.0).astype(bf16))
+        for at in range(0, size, LANES)
+    ]
+
+
+def project_kernel(place_ref, mine_ref, other_ref, *refs, shards, pieces):
+    x_ref, out_ref, outT_ref, w_ref, vec_ref, bi_ref, bias_ref, sems = refs[len(pieces) :]
+    width = x_ref.shape[1]
+    columns = out_ref.shape[1]
+    shard = width // shards
+
+    @pl.when((pl.program_id(0) == 0) & (pl.program_id(1) == 0) & (pl.program_id(2) == 0))
+    def _():
+        copies = []
+        for j, (ref, back) in enumerate(zip(refs, pieces)):
+            start = jnp.int32(0) if back is None else piece_owner(place_ref[1], back, shards) * shard
+            rows = pl.ds(pl.multiple_of(start, 16), ref.shape[0])
+            copies.append(pltpu.make_async_copy(ref, w_ref.at[rows, :], sems.at[j]))
+        for copy in copies:
+            copy.start()
+        for copy in copies:
+            copy.wait()
+        block = w_ref[:, columns:].astype(f32).reshape(shards, shard, LANES)
+        inner = bi_ref.shape[1]
+        totals = (2 * width, width, width, width, inner, width, width, width)
+        sizes = [total // shards for total in totals]
+        found = [
+            spread_vector(block, row, size, shards)
+            for row, size in zip(vector_rows(sizes)[0], sizes)
+        ]
+        bias_ref[0:1, :width] = found[0][:, :width]
+        bias_ref[0:1, width : 2 * width] = jnp.zeros((1, width), f32)
+        bias_ref[0:1, 2 * width :] = found[0][:, width:]
+        bi_ref[0:1, :] = found[4]
+        for j, v in enumerate(found[1:4] + found[5:]):
+            vec_ref[j : j + 1, :] = v
+
+    x = jnp.where(pl.program_id(1) == place_ref[0], mine_ref[...], other_ref[...])
+    x_ref[...] = x
+    low = (dot(x, w_ref[:, :columns]) + bias_ref[0:1, :]).astype(bf16)
     out_ref[...] = low
     outT_ref[...] = low.T
 
 
-def project(x, weight, bias, block):
-    tokens, width = x.shape
-    columns = weight.shape[1]
+def halves(block_rows, blocks):
+    def at(used, r, h, b):
+        rest = jnp.where(h == 0, 0, blocks - 1)
+        return (r * blocks + jnp.where(used, b, rest), 0)
+
+    return (
+        lambda r, h, b, s: at(h == s[0], r, h, b),
+        lambda r, h, b, s: at(h != s[0], r, h, b),
+    )
+
+
+def project(place, mine, other, weight, inner, block):
+    rows, half, width = mine.shape
+    block = min(block, half)
+    blocks = half // block
+    columns = 3 * width
+    tokens = 2 * rows * half
+    shards = lax.axis_size("dp")
+    mine_at, other_at = halves(block, blocks)
+
+    def at(r, h, b, s):
+        return ((r * 2 + h) * blocks + b, 0)
+
     return pl.pallas_call(
-        project_kernel,
-        grid=(tokens // block,),
-        in_specs=[
-            pl.BlockSpec((block, width), lambda i: (i, 0)),
-            pl.BlockSpec((width, columns), lambda i: (0, 0), pipeline_mode=pl.Buffered(1)),
-            pl.BlockSpec((8, columns), lambda i: (0, 0), pipeline_mode=pl.Buffered(1)),
+        functools.partial(project_kernel, shards=shards, pieces=[back for _, back in weight]),
+        grid_spec=pltpu.PrefetchScalarGridSpec(
+            num_scalar_prefetch=1,
+            grid=(rows, 2, blocks),
+            in_specs=[
+                pl.BlockSpec((block, width), mine_at),
+                pl.BlockSpec((block, width), other_at),
+            ]
+            + [pl.BlockSpec(memory_space=pl.ANY)] * len(weight),
+            out_specs=[
+                pl.BlockSpec((block, width), at),
+                pl.BlockSpec((block, columns), at),
+                pl.BlockSpec((columns, block), lambda *i: (0, at(*i)[0])),
+                pl.BlockSpec((width, columns + LANES), lambda *_: (0, 0)),
+                pl.BlockSpec((8, width), lambda *_: (0, 0)),
+                pl.BlockSpec((8, inner), lambda *_: (0, 0)),
+            ],
+            scratch_shapes=[
+                pltpu.VMEM((8, columns), f32),
+                pltpu.SemaphoreType.DMA((len(weight),)),
+            ],
+        ),
+        out_shape=[
+            shape_of((tokens, width), bf16),
+            shape_of((tokens, columns), bf16),
+            shape_of((columns, tokens), bf16),
+            shape_of((width, columns + LANES), bf16),
+            shape_of((8, width), f32),
+            shape_of((8, inner), f32),
         ],
-        out_specs=[
-            pl.BlockSpec((block, columns), lambda i: (i, 0)),
-            pl.BlockSpec((columns, block), lambda i: (0, i)),
-        ],
-        out_shape=[shape_of((tokens, columns), bf16), shape_of((columns, tokens), bf16)],
         compiler_params=pltpu.CompilerParams(vmem_limit_bytes=VMEM_LIMIT),
         cost_estimate=pl.CostEstimate(
             flops=2 * tokens * width * columns,
-            bytes_accessed=2 * (tokens * width + width * columns + 2 * tokens * columns),
+            bytes_accessed=2 * (2 * tokens * width + 2 * width * columns + 2 * tokens * columns),
             transcendentals=0,
         ),
         name="project",
-    )(x, weight, bias)
+    )(place, mine.reshape(-1, width), other.reshape(-1, width), *[w for w, _ in weight])
 
 
 def passage_range(bounds_ref, row, start, size, row_len):
@@ -349,20 +494,36 @@
 
 
 def dense_kernel(
-    attn_ref, x_ref, cot_ref, wo_ref, wi_ref, wf_ref, vec_ref, bi_ref,
+    side_ref, attn_ref, x_ref, mine_ref, other_ref, wo_ref, wi_ref, wf_ref, vec_ref, bi_ref,
     out_ref, act_ref, gp_ref, gs_ref, low_ref, gr1_ref, gb_ref, do_ref, doT_ref, sum_ref,
-    sum_in_ref, slope_ref, *, chunk,
+    sum_in_ref, slope_ref,
 ):
     width = x_ref.shape[1]
-    inner = wi_ref.shape[1]
+    inner = bi_ref.shape[1]
+    chunk = width
+    groups, per_group = wi_ref.shape[:2]
+    in_rows = per_group * chunk // inner
+    ffo_groups = max(1, groups * chunk // inner)
+
+    def w_out():
+        return wo_ref[...].reshape(width, width)
+
+    def w_in(c):
+        return wi_ref[:, c * in_rows : (c + 1) * in_rows, :].reshape(width, chunk)
+
+    def w_ffo(c):
+        if groups == 1:
+            return wf_ref[0, c * chunk : (c + 1) * chunk, :]
+        return wf_ref[c * ffo_groups : (c + 1) * ffo_groups].reshape(chunk, width)
+
     bias_out, gain_a, shift_a, bias_ffo, gain_f, shift_f = [vec_ref[j : j + 1, :] for j in range(6)]
 
-    @pl.when(pl.program_id(0) == 0)
+    @pl.when((pl.program_id(0) == 0) & (pl.program_id(1) == 0) & (pl.program_id(2) == 0))
     def _():
         sum_ref[...] = jnp.zeros(sum_ref.shape, f32)
         sum_in_ref[...] = jnp.zeros(sum_in_ref.shape, f32)
 
-    branch = dot(attn_ref[...], wo_ref[...]) + bias_out
+    branch = dot(attn_ref[...], w_out()) + bias_out
     normed_a, scale_a = normalise(x_ref[...].astype(f32) + branch)
     hidden = normed_a * gain_a + shift_a
     low = hidden.astype(bf16)
@@ -372,25 +533,25 @@
 
     second = None
     held = None
-    made = dot(low, wi_ref[:, cuts[0]])
+    made = dot(low, w_in(0))
     for c, cut in enumerate(cuts):
         pre = made + bi_ref[0:1, cut]
         if c < last:
-            made = dot(low, wi_ref[:, cuts[c + 1]])
+            made = dot(low, w_in(c + 1))
         value, slope = gelu_and_slope(pre)
         value = value.astype(bf16)
         act_ref[:, cut] = value
         slope_ref[:, cut] = slope.astype(bf16)
         if held is not None:
-            term = dot(held, wf_ref[cuts[c - 1], :])
+            term = dot(held, w_ffo(c - 1))
             second = term if second is None else second + term
         held = value
-    term = dot(held, wf_ref[cuts[last], :])
+    term = dot(held, w_ffo(last))
     second = term if second is None else second + term
 
     normed_f, scale_f = normalise(hidden + (second + bias_ffo))
     out_ref[...] = (normed_f * gain_f + shift_f).astype(bf16)
-    cot = cot_ref[...].astype(f32)
+    cot = jnp.where(pl.program_id(1) == side_ref[0], mine_ref[...], other_ref[...]).astype(f32)
     grad_r2 = normalise_back(cot * gain_f, normed_f, scale_f)
     grad_second = grad_r2.astype(bf16)
     gs_ref[...] = grad_second
@@ -400,18 +561,18 @@
 
     grad_hidden = grad_r2
     held = None
-    made = dot_nt(grad_second, wf_ref[cuts[0], :])
+    made = dot_nt(grad_second, w_ffo(0))
     for c, cut in enumerate(cuts):
         grad_act = made
         if c < last:
-            made = dot_nt(grad_second, wf_ref[cuts[c + 1], :])
+            made = dot_nt(grad_second, w_ffo(c + 1))
         grad_pre = (grad_act * slope_ref[:, cut].astype(f32)).astype(bf16)
         gp_ref[:, cut] = grad_pre
         sum_in_ref[0:1, cut] += column_sum(grad_pre.astype(f32))
         if held is not None:
-            grad_hidden = grad_hidden + dot_nt(held, wi_ref[:, cuts[c - 1]])
+            grad_hidden = grad_hidden + dot_nt(held, w_in(c - 1))
         held = grad_pre
-    grad_hidden = grad_hidden + dot_nt(held, wi_ref[:, cuts[last]])
+    grad_hidden = grad_hidden + dot_nt(held, w_in(last))
 
     grad_r1 = normalise_back(grad_hidden * gain_a, normed_a, scale_a)
     gr1_ref[...] = grad_r1
@@ -420,31 +581,49 @@
     sum_ref[3:4, :] += column_sum(grad_hidden * normed_a)
     sum_ref[4:5, :] += column_sum(grad_hidden)
     sum_ref[5:6, :] += column_sum(grad_branch.astype(f32))
-    grad_attn = dot_nt(grad_branch, wo_ref[...]).astype(bf16)
+    grad_attn = dot_nt(grad_branch, w_out()).astype(bf16)
     do_ref[...] = grad_attn
     doT_ref[...] = grad_attn.T
 
 
-def dense(attn, x, cot, w_out, w_in, w_ffo, vectors, bias_in, block, chunk):
-    tokens, width = x.shape
-    inner = w_in.shape[1]
-    narrow = pl.BlockSpec((block, width), lambda i: (i, 0))
-    wide = pl.BlockSpec((block, inner), lambda i: (i, 0))
-
-    def held(a):
-        return pl.BlockSpec(a.shape, lambda i: (0, 0), pipeline_mode=pl.Buffered(1))
+def dense(side, attn, x, mine, other, weights, vectors, bias_in, block):
+    rows, half, width = mine.shape
+    tokens = 2 * rows * half
+    inner = bias_in.shape[1]
+    block = min(block, half)
+    blocks = half // block
+    mine_at, other_at = halves(block, blocks)
+
+    def at(r, h, b, s):
+        return ((r * 2 + h) * blocks + b, 0)
+
+    narrow = pl.BlockSpec((block, width), at)
+    wide = pl.BlockSpec((block, inner), at)
+
+    def held(shape, index):
+        return pl.BlockSpec(shape, lambda *_: index, pipeline_mode=pl.Buffered(1))
 
     return pl.pallas_call(
-        functools.partial(dense_kernel, chunk=chunk),
-        grid=(tokens // block,),
-        in_specs=[narrow, narrow, narrow]
-        + [held(a) for a in (w_out, w_in, w_ffo, vectors, bias_in)],
-        out_specs=[
-            narrow, wide, wide, narrow, narrow, narrow, narrow, narrow,
-            pl.BlockSpec((width, block), lambda i: (0, i)),
-            pl.BlockSpec((8, width), lambda i: (0, 0)),
-            pl.BlockSpec((8, inner), lambda i: (0, 0)),
-        ],
+        dense_kernel,
+        grid_spec=pltpu.PrefetchScalarGridSpec(
+            num_scalar_prefetch=1,
+            grid=(rows, 2, blocks),
+            in_specs=[
+                narrow,
+                narrow,
+                pl.BlockSpec((block, width), mine_at),
+                pl.BlockSpec((block, width), other_at),
+            ]
+            + [held(shape, index) for _, shape, index in weights]
+            + [held(vectors.shape, (0, 0)), held(bias_in.shape, (0, 0))],
+            out_specs=[
+                narrow, wide, wide, narrow, narrow, narrow, narrow, narrow,
+                pl.BlockSpec((width, block), lambda *i: (0, at(*i)[0])),
+                pl.BlockSpec((8, width), lambda *_: (0, 0)),
+                pl.BlockSpec((8, inner), lambda *_: (0, 0)),
+            ],
+            scratch_shapes=[pltpu.VMEM((block, inner), bf16)],
+        ),
         out_shape=[
             shape_of((tokens, width), bf16),
             shape_of((tokens, inner), bf16),
@@ -458,7 +637,6 @@
             shape_of((8, width), f32),
             shape_of((8, inner), f32),
         ],
-        scratch_shapes=[pltpu.VMEM((block, inner), bf16)],
         compiler_params=pltpu.CompilerParams(vmem_limit_bytes=VMEM_LIMIT),
         cost_estimate=pl.CostEstimate(
             flops=2 * tokens * width * (2 * width + 4 * inner),
@@ -466,7 +644,77 @@
             transcendentals=2 * tokens * inner,
         ),
         name="dense",
-    )(attn, x, cot, w_out, w_in, w_ffo, vectors, bias_in)
+    )(
+        side, attn, x, mine.reshape(-1, width), other.reshape(-1, width),
+        *[array for array, _, _ in weights], vectors, bias_in,
+    )
+
+
+def product_kernel(a_ref, b_ref, *rest):
+    out_ref = rest[-1]
+    out_ref[...] = dot_tn(a_ref[...], b_ref[...]).astype(bf16).reshape(out_ref.shape)
+
+
+def product_into(buffer, shape, a, b, out_block, out_at, a_moves, steps):
+    tokens = a.shape[0]
+    a_cols = a.shape[1] // (steps if a_moves else 1)
+    b_cols = b.shape[1] // (1 if a_moves else steps)
+    moving = {"index_map": lambda i: (0, i)}
+    still = {"index_map": lambda i: (0, 0), "pipeline_mode": pl.Buffered(1)}
+    in_specs = [
+        pl.BlockSpec((tokens, a_cols), **(moving if a_moves else still)),
+        pl.BlockSpec((tokens, b_cols), **(still if a_moves else moving)),
+    ]
+    operands = [a, b]
+    aliases = {}
+    if buffer is not None:
+        in_specs.append(pl.BlockSpec(memory_space=pl.ANY))
+        operands.append(buffer)
+        aliases = {2: 0}
+    return pl.pallas_call(
+        product_kernel,
+        grid=(steps,),
+        in_specs=in_specs,
+        out_specs=pl.BlockSpec(out_block, out_at),
+        out_shape=shape_of(shape, bf16),
+        input_output_aliases=aliases,
+        compiler_params=pltpu.CompilerParams(vmem_limit_bytes=VMEM_LIMIT),
+        cost_estimate=pl.CostEstimate(
+            flops=2 * tokens * a.shape[1] * b.shape[1],
+            bytes_accessed=2 * (a.size + b.size + a.shape[1] * b.shape[1]),
+            transcendentals=0,
+        ),
+        name="product",
+    )(*operands)
+
+
+def input_grad_kernel(dq_ref, dk_ref, dv_ref, gr1_ref, w_ref, out_ref):
+    width = out_ref.shape[1]
+    total = gr1_ref[...]
+    for j, ref in enumerate((dq_ref, dk_ref, dv_ref)):
+        total = total + dot_nt(ref[...], w_ref[:, j * width : (j + 1) * width])
+    out_ref[...] = total.astype(bf16)
+
+
+def input_grad(dq, dk, dv, grad_r1, weight, block):
+    tokens, width = dq.shape
+    block = min(block, tokens)
+    part = pl.BlockSpec((block, width), lambda i: (i, 0))
+    return pl.pallas_call(
+        input_grad_kernel,
+        grid=(tokens // block,),
+        in_specs=[part] * 4
+        + [pl.BlockSpec(weight.shape, lambda i: (0, 0), pipeline_mode=pl.Buffered(1))],
+        out_specs=part,
+        out_shape=shape_of((tokens, width), bf16),
+        compiler_params=pltpu.CompilerParams(vmem_limit_bytes=VMEM_LIMIT),
+        cost_estimate=pl.CostEstimate(
+            flops=6 * tokens * width * width,
+            bytes_accessed=12 * tokens * width + 6 * width * width,
+            transcendentals=0,
+        ),
+        name="input_grad",
+    )(dq, dk, dv, grad_r1, weight)
 
 
 def split_heads(values):
@@ -522,36 +770,98 @@
     return dq, dk, dv, sums
 
 
-def rows_of(values, seq_index, seq_count):
-    rows, part, width = values.shape
-    mine = rows // seq_count
-    whole = jnp.zeros((mine, part * seq_count, width), values.dtype)
-    for step in range(seq_count):
-        to = (seq_index + step) % seq_count
-        source = (seq_index - step) % seq_count
-        piece = lax.dynamic_slice_in_dim(values, to * mine, mine, 0)
-        if step:
-            piece = lax.ppermute(
-                piece, "seq", [(s, (s + step) % seq_count) for s in range(seq_count)]
-            )
-        whole = lax.dynamic_update_slice_in_dim(whole, piece, source * part, 1)
-    return whole
-
-
-def parts_of(values, seq_index, seq_count):
-    mine, row_len, width = values.shape
-    part = row_len // seq_count
-    parts = jnp.zeros((mine * seq_count, part, width), values.dtype)
-    for step in range(seq_count):
-        to = (seq_index + step) % seq_count
-        source = (seq_index - step) % seq_count
-        piece = lax.dynamic_slice_in_dim(values, to * part, part, 1)
-        if step:
-            piece = lax.ppermute(
-                piece, "seq", [(s, (s + step) % seq_count) for s in range(seq_count)]
-            )
-        parts = lax.dynamic_update_slice_in_dim(parts, piece, source * mine, 0)
-    return parts
+def collect_kernel(sums_qv_ref, sums_ref, sums_in_ref, *refs):
+    out_ref = refs[-1]
+    shards = out_ref.shape[0]
+    qv = jnp.concatenate([sums_qv_ref[0:1, :], sums_qv_ref[1:2, :]], axis=1)
+    rows = [sums_ref[j : j + 1, :] for j in range(6)]
+    found = []
+    for v in (qv, rows[5], rows[3], rows[4], sums_in_ref[0:1, :], rows[2], rows[0], rows[1]):
+        found.extend(gather_vector(v, shards))
+    out_ref[...] = jnp.zeros(out_ref.shape, bf16)
+    for j, v in enumerate(found):
+        out_ref[:, j : j + 1, :LANES] = v.astype(bf16).reshape(shards, 1, LANES)
+
+
+def collect(buffer, sums_qv, sums, sums_in, shards):
+    rows = buffer.shape[1]
+    width = buffer.shape[2]
+    whole = [pl.BlockSpec(v.shape, lambda i: (0, 0)) for v in (sums_qv, sums, sums_in)]
+    return pl.pallas_call(
+        collect_kernel,
+        grid=(1,),
+        in_specs=whole + [pl.BlockSpec(memory_space=pl.ANY)],
+        out_specs=pl.BlockSpec((shards, 16, width), lambda i: (0, rows // 16 - 1, 0)),
+        out_shape=shape_of(buffer.shape, bf16),
+        input_output_aliases={3: 0},
+        compiler_params=pltpu.CompilerParams(vmem_limit_bytes=VMEM_LIMIT),
+        name="collect",
+    )(sums_qv, sums, sums_in, buffer)
+
+
+def swapped(values):
+    return lax.ppermute(values, "seq", [(0, 1), (1, 0)])
+
+
+def halves_of_rows(values, seq_index):
+    mine = values.shape[0] // 2
+    return (
+        lax.dynamic_slice_in_dim(values, seq_index * mine, mine, 0),
+        swapped(lax.dynamic_slice_in_dim(values, (1 - seq_index) * mine, mine, 0)),
+    )
+
+
+def rows_of_halves(values, seq_index):
+    half = values.shape[1] // 2
+    kept = lax.dynamic_slice_in_dim(values, seq_index * half, half, 1)
+    came = swapped(lax.dynamic_slice_in_dim(values, (1 - seq_index) * half, half, 1))
+    first = seq_index == 0
+    return jnp.concatenate([jnp.where(first, kept, came), jnp.where(first, came, kept)], axis=0)
+
+
+def coordinates(count):
+    return ((2, 1), (count // 8, 2), (4, count // 4))
+
+
+def turned(values, axis, size, stride, step):
+    perm = []
+    for i in range(lax.axis_size(axis)):
+        at = (i // stride) % size
+        perm.append((i, i + ((at + step) % size - at) * stride))
+    return lax.ppermute(values, axis, perm)
+
+
+def scatter_sum(values, axis):
+    index = lax.axis_index(axis)
+    rest = values
+    for size, stride in coordinates(lax.axis_size(axis)):
+        blocks = rest.reshape((-1, size) + values.shape[1:])
+        here = (index // stride) % size
+        total = lax.dynamic_index_in_dim(blocks, here, 1, False).astype(f32)
+        for step in range(1, size):
+            piece = lax.dynamic_index_in_dim(blocks, (here + step) % size, 1, False)
+            total = total + turned(piece, axis, size, stride, step).astype(f32)
+        rest = total.astype(values.dtype)
+    return rest[0]
+
+
+def gather_pieces(values, axis):
+    pieces = [(values, (0, 0, 0))]
+    for at, (size, stride) in reversed(list(enumerate(coordinates(lax.axis_size(axis))))):
+        more = []
+        for piece, back in pieces:
+            for step in range(1, size):
+                came = turned(piece, axis, size, stride, step)
+                more.append((came, back[:at] + (step,) + back[at + 1 :]))
+        pieces = pieces + more
+    return pieces
+
+
+def piece_owner(index, back, count):
+    owner = jnp.int32(0)
+    for (size, stride), step in zip(coordinates(count), back):
+        owner = owner + lax.rem(lax.rem(index // stride, size) + (size - step), size) * stride
+    return owner
 
 
 def per_device(
@@ -574,90 +884,132 @@
     rows, tok_seq, width = tokens.shape
     seq_count = lax.axis_size("seq")
     seq_index = lax.axis_index("seq")
-    whole_rows = rows % seq_count == 0
+    shards = lax.axis_size("dp")
+    shard = weight_qkv.shape[0]
+    by_rows = seq_count == 2 and rows % 2 == 0 and shards % 8 == 0 and shard % 16 == 0
     inner = weight_in.shape[1]
-    shard = weight_qkv.shape[0]
+    chunks = inner // width
     token_count = rows * tok_seq
 
     small = (bias_qv, bias_out, gain_attn, shift_attn, bias_in, bias_ffo, gain_ffn, shift_ffn)
-    small_cols = [v.shape[0] // shard for v in small]
-    packed = jnp.concatenate([v.reshape(shard, -1) for v in small], axis=1)
-    packed = jnp.pad(packed, ((0, 0), (0, LANES - packed.shape[1])))
-    first = jnp.concatenate([weight_qkv, packed], axis=1).astype(bf16)
-    first = lax.all_gather(first, "dp", axis=0, tiled=True)
-    w_qkv = first[:, : 3 * width]
-    vectors = []
-    at = 3 * width
-    for cols in small_cols:
-        vectors.append(first[:, at : at + cols].astype(f32).reshape(-1))
-        at += cols
-    v_qv, v_out, v_ga, v_sa, v_in, v_ffo, v_gf, v_sf = vectors
-    w_out = lax.all_gather(weight_out.astype(bf16), "dp", axis=0, tiled=True)
-    w_in = lax.all_gather(weight_in.astype(bf16), "dp", axis=0, tiled=True)
-    w_ffo = lax.all_gather(weight_ffo.astype(bf16), "dp", axis=0, tiled=True)
-    qkv_bias = jnp.concatenate([v_qv[:width], jnp.zeros((width,), f32), v_qv[width:]])
-    qkv_bias = jnp.broadcast_to(qkv_bias[None], (8, 3 * width))
-    vec = jnp.stack([v_out, v_ga, v_sa, v_ffo, v_gf, v_sf, v_sf, v_sf])
-    in_bias = jnp.broadcast_to(v_in[None], (8, inner))
+    first, others = lower(weight_qkv, weight_in, weight_ffo, weight_out, small)
+    if by_rows:
+        first = gather_pieces(first, "dp")
+    else:
+        first = [(lax.all_gather(first, "dp", axis=0, tiled=True), None)]
+    others = lax.all_gather(others[None], "dp", axis=0, tiled=True)
+    if shard % 16 == 0:
+        weights = (
+            (others, (shards, shard, width), (0, 2 * chunks, 0)),
+            (others, (shards, chunks * shard, width), (0, 0, 0)),
+            (others, (shards, chunks * shard, width), (0, 1, 0)),
+        )
+    else:
+        part = chunks * shard
+        w_in = others[:, :part].reshape(shards, chunks, shard, width).transpose(1, 0, 2, 3)
+        w_in = w_in.reshape(1, inner, width)
+        w_ffo = others[:, part : 2 * part].reshape(1, inner, width)
+        w_out = others[:, 2 * part :].reshape(1, width, width)
+        weights = [(w, w.shape, (0, 0, 0)) for w in (w_out, w_in, w_ffo)]
 
     bounds = jnp.cumsum(lengths, axis=1)
-    if whole_rows:
-        mine = rows // seq_count
+    if by_rows:
+        mine = rows // 2
         bounds = lax.dynamic_slice_in_dim(bounds, seq_index * mine, mine, 0)
-        x = rows_of(tokens, seq_index, seq_count).reshape(token_count, width)
-        cot = rows_of(cotangent, seq_index, seq_count).reshape(token_count, width)
+        side = jnp.stack([seq_index, lax.axis_index("dp")]).astype(jnp.int32)
+        x_halves = halves_of_rows(tokens, seq_index)
+        cot_halves = halves_of_rows(cotangent, seq_index)
     else:
-        x = tokens.reshape(token_count, width)
-        cot = cotangent.reshape(token_count, width)
-
-    qkv, qkvT = project(x, w_qkv, qkv_bias, BLOCK)
-    if whole_rows:
+        side = jnp.zeros((2,), jnp.int32)
+        x_halves = tokens.reshape(2, 1, -1, width)
+        cot_halves = cotangent.reshape(2, 1, -1, width)
+
+    x, qkv, qkvT, w_qkv, vec, in_bias = project(side, *x_halves, first, inner, BLOCK)
+    if by_rows:
         attn, attnT, log = attend_rows(bounds, qkv, qkvT, BLOCK)
     else:
         attn, saved = attend_gathered(bounds, qkv, rows, seq_index)
     out, act, gp, gs, low, gr1, gb, do, doT, sums, sums_in = dense(
-        attn, x, cot, w_out, w_in, w_ffo, vec, in_bias, BLOCK, width
+        side, attn, x, *cot_halves, weights, vec, in_bias, BLOCK
     )
-    grad_w_ffo = dot_tn(act, gs).astype(bf16)
-    grad_w_in = dot_tn(low, gp).astype(bf16)
-    grad_w_out = dot_tn(attn, gb).astype(bf16)
-    if whole_rows:
+    if by_rows:
+        out = rows_of_halves(out.reshape(mine, -1, width), seq_index)
+    else:
+        out = out.reshape(rows, tok_seq, width)
+
+    per_shard = (2 * chunks + 1) * shard
+    if shard % 16 == 0:
+        grads = product_into(
+            None, (shards, per_shard, width), low, gp,
+            (shards, shard, width), lambda i: (0, i, 0), False, chunks,
+        )
+        grads = product_into(
+            grads, grads.shape, act, gs,
+            (shards // chunks, chunks * shard, width), lambda i: (i, 1, 0), True, chunks,
+        )
+        grads = product_into(
+            grads, grads.shape, attn, gb,
+            (shards, shard, width), lambda i: (0, 2 * chunks, 0), False, 1,
+        )
+    else:
+        g_in = dot_tn(low, gp).astype(bf16).reshape(shards, shard, chunks, width)
+        g_in = g_in.transpose(0, 2, 1, 3).reshape(shards, chunks * shard, width)
+        g_ffo = dot_tn(act, gs).astype(bf16).reshape(shards, chunks * shard, width)
+        g_out = dot_tn(attn, gb).astype(bf16).reshape(shards, shard, width)
+        grads = jnp.concatenate([g_in, g_ffo, g_out], axis=1)
+    grads, do = lax.optimization_barrier((grads, do))
+    reduced = lax.psum_scatter(grads, "dp", scatter_dimension=0, tiled=True)[0]
+
+    if by_rows:
         dq, dk, dv, sums_qv = attend_rows_back(bounds, qkv, qkvT, do, doT, attnT, log, BLOCK)
     else:
         dq, dk, dv, sums_qv = attend_gathered_back(saved, attn, do)
-    grad_qkv = jnp.concatenate([dq, dk, dv], axis=1)
-    grad_w_qkv = dot_tn(x, grad_qkv).astype(bf16)
-    grad_x = (gr1 + dot_nt(grad_qkv, w_qkv)).astype(bf16)
-
-    if whole_rows:
-        out = parts_of(out.reshape(mine, -1, width), seq_index, seq_count)
-        grad_x = parts_of(grad_x.reshape(mine, -1, width), seq_index, seq_count)
+
+    if by_rows:
+        g_qkv = []
+        for g in (dq, dk, dv):
+            extra = 16 if g is dv else 0
+            g_qkv.append(
+                product_into(
+                    None, (shards, shard + extra, width), x, g,
+                    (shards, shard, width), lambda i: (0, 0, 0), False, 1,
+                )
+            )
+        g_qkv[2] = collect(g_qkv[2], sums_qv, sums, sums_in, shards)
+        g_qkv = [scatter_sum(g, "dp") for g in g_qkv]
     else:
-        out = out.reshape(rows, tok_seq, width)
+        vectors = jnp.zeros((shards, 16, width), bf16)
+        vectors = collect(vectors, sums_qv, sums, sums_in, shards)
+        g_qkv = [dot_tn(x, g).astype(bf16).reshape(shards, shard, width) for g in (dq, dk, dv)]
+        g_qkv[2] = jnp.concatenate([g_qkv[2], vectors], axis=1)
+        g_qkv = [lax.psum_scatter(g, "dp", scatter_dimension=0, tiled=True)[0] for g in g_qkv]
+
+    grad_x = input_grad(dq, dk, dv, gr1, w_qkv, BLOCK)
+    if by_rows:
+        grad_x = rows_of_halves(grad_x.reshape(mine, -1, width), seq_index)
+    else:
         grad_x = grad_x.reshape(rows, tok_seq, width)
 
-    def scatter(values):
-        return lax.psum_scatter(values, "dp", scatter_dimension=0, tiled=True)
-
-    small_grads = (
-        sums_qv[:2].reshape(-1), sums[5], sums[3], sums[4], sums_in[0], sums[2], sums[0], sums[1],
-    )
-    dp_count = lax.axis_size("dp")
-    packed = jnp.concatenate([v.reshape(dp_count * shard, -1) for v in small_grads], axis=1)
-    packed = jnp.pad(packed, ((0, 0), (0, LANES - packed.shape[1]))).astype(bf16)
-    last = scatter(jnp.concatenate([grad_w_qkv, packed], axis=1))
-    shared = lax.psum(
-        (scatter(grad_w_ffo), scatter(grad_w_in), scatter(grad_w_out), last), "seq"
-    )
-    d_ffo, d_in, d_out, last = [v.astype(f32) for v in shared]
+    def over_seq(values):
+        if seq_count == 2:
+            return values.astype(f32) + swapped(values).astype(f32)
+        return lax.psum(values, "seq").astype(f32)
+
+    reduced = over_seq(reduced)
+    g_qkv = [over_seq(g) for g in g_qkv]
+    vectors = g_qkv[2][shard:, :LANES]
+    d_qkv = jnp.concatenate([g[:shard] for g in g_qkv], axis=1)
+    d_in = reduced[: chunks * shard].reshape(chunks, shard, width).transpose(1, 0, 2)
+    d_in = d_in.reshape(shard, inner)
+    d_ffo = reduced[chunks * shard : 2 * chunks * shard]
+    d_out = reduced[2 * chunks * shard :]
+    sizes = [v.shape[0] for v in small]
     d_small = []
-    at = 3 * width
-    for cols in small_cols:
-        d_small.append(last[:, at : at + cols].reshape(-1))
-        at += cols
+    for row, size in zip(vector_rows(sizes)[0], sizes):
+        d_small.append(vectors[row : row - (-size // LANES)].reshape(-1)[:size])
     g_qv, g_bo, g_ga, g_sa, g_bi, g_bf, g_gf, g_sf = d_small
     return (
-        out, grad_x, last[:, : 3 * width], g_qv, d_out, g_bo, g_ga, g_sa, d_in, g_bi, d_ffo,
+        out, grad_x, d_qkv, g_qv, d_out, g_bo, g_ga, g_sa, d_in, g_bi, d_ffo,
         g_bf, g_gf, g_sf,
     )
 

time: 687 us -> 431 us (0.63)
  waiting for transfers between devices: 381 us -> 109 us
  Pallas kernels: 144 us -> 226 us
  matrix products: 55.4 us -> 0 us
  local copies, waits for them, and re-layouts: 60.1 us -> 21.6 us
  starting transfers between devices: 1.58 us -> 38.7 us
  other arithmetic: 24.3 us -> 12.5 us
    reduce_scatter x4 -> x1, waiting for transfers between devices: 213 us -> 0.01 us  [per_device(): reduced = lax.psum_scatter(grads, 'dp', scatter_dimension=0, tiled=True)[0]]
    pallas_call x2 -> x11, Pallas kernels: 82.5 us -> 163 us  [the longest x1 70 us: dense(): pl.pallas_call(dense_kernel, grid_spec=pltpu.PrefetchScalarGridSpec(num_s...]
    all_gather x4 -> x1, waiting for transfers between devices: 71.5 us -> 0.02 us  [per_device(): others = lax.all_gather(others[None], 'dp', axis=0, tiled=True)]
    dot_general x5 -> x0, matrix products: 55.4 us -> none  [the longest x4 43.8 us: dot_tn(): lax.dot_general(a, b, (((0,), (0,)), ((), ())), preferred_element_type=f32)]
    ppermute x4 -> x38, waiting for transfers between devices: 61.7 us -> 109 us  [the longest x30 75.3 us: turned(): return lax.ppermute(values, axis, perm)]
    ppermute x4 -> x38, starting transfers between devices: 1.21 us -> 38.7 us  [the longest x30 24.8 us: turned(): return lax.ppermute(values, axis, perm)]
    psum x1 -> x0, waiting for transfers between devices: 34.5 us -> none  [per_device(): lax.psum((scatter(grad_w_ffo), scatter(grad_w_in), scatter(grad_w_out), l...]
    unnamed x44 -> x34, local copies, waits for them, and re-layouts: 16.9 us -> 2.08 us
  transfers between devices with their start and end apart: 13 -> 40, of which waited for: 8 -> 15; matrix products, arithmetic and copies ran while one was open for 14% -> 7% of each run, Pallas kernels for 5% -> 28%
where the time goes in v2:
time: 431 us; the launch traced here: 423 us
  Pallas kernels  226 us (52%)
  waiting for transfers between devices  109 us (25%)
  starting transfers between devices  38.7 us (9%)
  local copies, waits for them, and re-layouts  21.6 us (5%)
  between operations  15 us (3%)
  other arithmetic  12.5 us (3%)
    ppermute x30, waiting for transfers between devices, turned(): return lax.ppermute(values, axis, perm)  75.3 us
    pallas_call x1, Pallas kernels, dense(): pl.pallas_call(dense_kernel, grid_spec=pltpu.PrefetchScalarGridSpec(num_s...  70 us
    pallas_call x6, Pallas kernels, product_into(): pl.pallas_call(product_kernel, grid=(steps,), in_specs=in_specs, out_spec...  55.3 us
    pallas_call x1, Pallas kernels, attend_rows_back(): pl.pallas_call(attend_back_kernel, grid_spec=pltpu.PrefetchScalarGridSpec...  40.1 us
    ppermute x8, waiting for transfers between devices, swapped(): return lax.ppermute(values, 'seq', [(0, 1), (1, 0)])  33.5 us
    ppermute x30, starting transfers between devices, turned(): return lax.ppermute(values, axis, perm)  24.8 us
    pallas_call x1, Pallas kernels, attend_rows(): pl.pallas_call(attend_kernel, grid_spec=pltpu.PrefetchScalarGridSpec(num_...  22.9 us
    pallas_call x1, Pallas kernels, project(): pl.pallas_call(functools.partial(project_kernel, shards=shards, pieces=[b...  17.6 us
  transfers between devices with their start and end apart: 40, of which 15 were waited for; matrix products, arithmetic and copies ran while one was open for 7% of the time, Pallas kernels for 28%

profile of v2, /device:TPU:12, one launch (start us, length us, event | category | flops | bytes accessed | tf_op | source)
XLA Modules:
  0.0 423.2 jit_solution(8867567627892413700)
XLA Ops:
  7.2 2.4 lower.1
  9.8 3.4 constant_dynamic-slice_fusion.13
  13.7 1.6 collective-permute-start.1
  16.3 2.0 collective-permute-start.3
  19.8 11.6 %collective-permute-done.1.refs_1_ = bf16[48,2432]{1,0:T(8,128)(2,1)S(1)} collective-permute-done((bf16[48,2432]{1,0:T(8,128)(2,1)S(1)}, bf16[48,2432]{1,0:T(8,128)(2,1)S(1)}, u32[]{:S(2)}, u32[]{:S(2)}) %collective-permute-start.1) | collective-permute-done | bytes 233504 | tf_op jit(solution)/shard_map/ppermute | solution.py:831
  31.3 20.9 %collective-permute-done.2.refs_2_ = bf16[48,2432]{1,0:T(8,128)(2,1)S(1)} collective-permute-done((bf16[48,2432]{1,0:T(8,128)(2,1)S(1)}, bf16[48,2432]{1,0:T(8,128)(2,1)S(1)}, u32[]{:S(2)}, u32[]{:S(2)}) %collective-permute-start.2) | collective-permute-done | bytes 233504 | tf_op jit(solution)/shard_map/ppermute | solution.py:831
  52.2 1.5 collective-permute-start.5
  53.7 2.8 collective-permute-done.3.refs_3_
  59.0 6.1 %collective-permute-done.6.refs_6_ = bf16[48,2432]{1,0:T(8,128)(2,1)} collective-permute-done((bf16[48,2432]{1,0:T(8,128)(2,1)S(1)}, bf16[48,2432]{1,0:T(8,128)(2,1)}, u32[]{:S(2)}, u32[]{:S(2)}) %collective-permute-start.6) | collective-permute-done | bytes 233504 | tf_op jit(solution)/shard_map/ppermute | solution.py:831
  65.2 7.9 %collective-permute-done.7.refs_7_ = bf16[48,2432]{1,0:T(8,128)(2,1)} collective-permute-done((bf16[48,2432]{1,0:T(8,128)(2,1)S(1)}, bf16[48,2432]{1,0:T(8,128)(2,1)}, u32[]{:S(2)}, u32[]{:S(2)}) %collective-permute-start.7) | collective-permute-done | bytes 233504 | tf_op jit(solution)/shard_map/ppermute | solution.py:831
  74.4 2.5 collective-permute-start.16
  80.4 17.6 %project.1 = (bf16[2048,768]{1,0:T(8,128)(2,1)}, bf16[2048,2304]{1,0:T(8,128)(2,1)}, bf16[2304,2048]{1,0:T(8,128)(2,1)}, bf16[768,2432]{1,0:T(8,128)(2,1)}, f32[8,768]{1,0:T(8,128)}, /*index=5*/f32[8,3072]{1,0:T(8,128)}) custom-call(s32[2]{0:T(128)} %pad_add_fusion.place_ref.side_ref, bf16[1024,768]{1,0:T(8,128)(2,1)} %bitcast.106, ...), custom_call_target="tpu_custom_call" | custom-call | flops 7247757312 | bytes 32243712 | tf_op jit(solution)/shard_map/project/pallas_call | solution.py:181
  98.0 22.9 %attend.1 = (bf16[2048,768]{1,0:T(8,128)(2,1)}, bf16[768,2048]{1,0:T(8,128)(2,1)}, f32[16,2048]{1,0:T(8,128)}) custom-call(s32[2,8]{1,0:T(2,128)} %constant_dynamic-slice_fusion.15.bounds_ref, bf16[2048,2304]{1,0:T(8,128)(2,1)} %get-tuple-element.43.k_ref.v_ref.q_ref, bf16[2304,2048]{1,0:T(8,128)(2,1)} %get-tuple-element.44.qT_ref.vT_ref.kT_ref, ...), custom_call_target="tpu_custom_call" | custom-call | flops 6442450944 | bytes 15728640 | tf_op jit(solution)/shard_map/attend/pallas_call | solution.py:330
  120.9 70.0 %dense.1 = (bf16[2048,768]{1,0:T(8,128)(2,1)}, bf16[2048,3072]{1,0:T(8,128)(2,1)}, bf16[2048,3072]{1,0:T(8,128)(2,1)}, bf16[2048,768]{1,0:T(8,128)(2,1)}, bf16[2...) custom-call(s32[2]{0:T(128)} %pad_add_fusion.place_ref.side_ref, ...), custom_call_target="tpu_custom_call" | custom-call | flops 43486543872 | bytes 69206016 | tf_op jit(solution)/shard_map/dense/pallas_call | solution.py:606
  191.0 14.6 %product.6.rest_0_ = bf16[16,432,768]{2,1,0:T(8,128)(2,1)} custom-call(bf16[2048,768]{1,0:T(8,128)(2,1)} %get-tuple-element.54.a_ref, bf16[2048,3072]{1,0:T(8,128)(2,1)} %get-tuple-element.55.b_ref), custom_call_target="tpu_custom_call" | custom-call | flops 9663676416 | bytes 20447232 | tf_op jit(solution)/shard_map/product/pallas_call | solution.py:674
  205.5 14.6 %product.7.rest_0_ = bf16[16,432,768]{2,1,0:T(8,128)(2,1)} custom-call(bf16[2048,3072]{1,0:T(8,128)(2,1)} %get-tuple-element.52.a_ref, bf16[2048,768]{1,0:T(8,128)(2,1)} %get-tuple-element.53.b_ref, bf16[16,432,768]{2,1,0:T(8,128)(2,1)} %product.6.rest_0_), custom_call_target="tpu_custom_call", output_to_operand_aliasing={{}: (2, {})} | custom-call | flops 9663676416 | bytes 20447232 | tf_op jit(solution)/shard_map/product/pallas_call | solution.py:674
  220.1 6.5 %product.8 = bf16[16,432,768]{2,1,0:T(8,128)(2,1)} custom-call(bf16[2048,768]{1,0:T(8,128)(2,1)} %get-tuple-element.45.attn_ref.a_ref, bf16[2048,768]{1,0:T(8,128)(2,1)} %get-tuple-element.51.b_ref, bf16[16,432,768]{2,1,0:T(8,128)(2,1)} %product.7.rest_0_), custom_call_target="tpu_custom_call", output_to_operand_aliasing={{}: (2, {})} | custom-call | flops 2415919104 | bytes 7471104 | tf_op jit(solution)/shard_map/product/pallas_call | solution.py:674
  226.8 40.1 %attend_back.1 = (bf16[2048,768]{1,0:T(8,128)(2,1)}, bf16[2048,768]{1,0:T(8,128)(2,1)}, bf16[2048,768]{1,0:T(8,128)(2,1)}, f32[8,768]{1,0:T(8,128)}) custom-call(s32[2,8]{1,0:T(2,128)} %constant_dynamic-slice_fusion.15.bounds_ref, bf16[2048,2304]{1,0:T(8,128)(2,1)} %get-tuple-element.43.k_ref.v_ref.q_ref, ...), custom_call_target="tpu_custom_call" | custom-call | flops 16106127360 | bytes 34603008 | tf_op jit(solution)/shard_map/attend_back/pallas_call | solution.py:445
  266.9 6.5 %product.9 = bf16[16,48,768]{2,1,0:T(8,128)(2,1)} custom-call(bf16[2048,768]{1,0:T(8,128)(2,1)} %get-tuple-element.46.x_ref.a_ref, bf16[2048,768]{1,0:T(8,128)(2,1)} %get-tuple-element.61.dq_ref.b_ref), custom_call_target="tpu_custom_call" | custom-call | flops 2415919104 | bytes 7471104 | tf_op jit(solution)/shard_map/product/pallas_call | solution.py:674
  273.5 1.9 dynamic-slice_bitcast_fusion.2
  275.4 6.5 %product.10 = bf16[16,48,768]{2,1,0:T(8,128)(2,1)} custom-call(bf16[2048,768]{1,0:T(8,128)(2,1)} %get-tuple-element.46.x_ref.a_ref, bf16[2048,768]{1,0:T(8,128)(2,1)} %get-tuple-element.62.dk_ref.b_ref), custom_call_target="tpu_custom_call" | custom-call | flops 2415919104 | bytes 7471104 | tf_op jit(solution)/shard_map/product/pallas_call | solution.py:674
  281.9 1.9 dynamic-slice_bitcast_fusion.1
  284.3 6.6 %product.11.refs_0_ = bf16[16,64,768]{2,1,0:T(8,128)(2,1)} custom-call(bf16[2048,768]{1,0:T(8,128)(2,1)} %get-tuple-element.46.x_ref.a_ref, bf16[2048,768]{1,0:T(8,128)(2,1)} %get-tuple-element.63.dv_ref.b_ref), custom_call_target="tpu_custom_call" | custom-call | flops 2415919104 | bytes 7471104 | tf_op jit(solution)/shard_map/product/pallas_call | solution.py:674
  290.9 3.2 collect.1
  294.1 2.1 dynamic-slice_bitcast_fusion
  296.3 14.8 %input_grad.1 = bf16[2048,768]{1,0:T(8,128)(2,1)} custom-call(bf16[2048,768]{1,0:T(8,128)(2,1)} %get-tuple-element.61.dq_ref.b_ref, bf16[2048,768]{1,0:T(8,128)(2,1)} %get-tuple-element.62.dk_ref.b_ref, bf16[2048,768]{1,0:T(8,128)(2,1)} %get-tuple-element.63.dv_ref.b_ref, f32[2048,768]{1,0:T(8,128)} %get-tuple-element.64.gr1_ref, ...), custom_call_target="tpu_custom_call" | custom-call | flops 7247757312 | bytes 22413312 | tf_op jit(solution)/shard_map/input_grad/pallas_call | solution.py:703
  311.0 2.8 constant_dynamic-slice_fusion.9
  317.2 1.5 fusion.1
  318.8 2.1 collective-permute-start.20
  322.5 2.2 collective-permute-start.32
  324.7 9.8 %collective-permute-done.20 = bf16[4,48,768]{2,1,0:T(8,128)(2,1)S(1)} collective-permute-done((bf16[4,48,768]{2,1,0:T(8,128)(2,1)S(1)}, bf16[4,48,768]{2,1,0:T(8,128)(2,1)S(1)}, u32[]{:S(2)}, u32[]{:S(2)}) %collective-permute-start.20) | collective-permute-done | bytes 294944 | tf_op jit(solution)/shard_map/ppermute | solution.py:831
  334.8 7.4 %collective-permute-done.26 = bf16[4,48,768]{2,1,0:T(8,128)(2,1)S(1)} collective-permute-done((bf16[4,48,768]{2,1,0:T(8,128)(2,1)S(1)}, bf16[4,48,768]{2,1,0:T(8,128)(2,1)S(1)}, u32[]{:S(2)}, u32[]{:S(2)}) %collective-permute-start.26) | collective-permute-done | bytes 294944 | tf_op jit(solution)/shard_map/ppermute | solution.py:831
  342.4 2.1 collective-permute-start.27
  344.4 3.2 collective-permute-start.28
  347.7 5.5 %collective-permute-done.23 = bf16[1,48,768]{2,1,0:T(8,128)(2,1)S(1)} collective-permute-done((bf16[1,48,768]{2,1,0:T(8,128)(2,1)S(1)}, bf16[1,48,768]{2,1,0:T(8,128)(2,1)S(1)}, u32[]{:S(2)}, u32[]{:S(2)}) %collective-permute-start.23) | collective-permute-done | bytes 73760 | tf_op jit(solution)/shard_map/ppermute | solution.py:831
  353.2 2.8 collective-permute-start.17
  356.1 1.6 collective-permute-start.24
  358.8 2.6 collective-permute-start.34
  361.4 28.0 %collective-permute-done.24 = bf16[48,768]{1,0:T(8,128)(2,1)S(1)} collective-permute-done((bf16[48,768]{1,0:T(8,128)(2,1)S(1)}, bf16[48,768]{1,0:T(8,128)(2,1)S(1)}, u32[]{:S(2)}, u32[]{:S(2)}) %collective-permute-start.24) | collective-permute-done | bytes 73760 | tf_op jit(solution)/shard_map/ppermute | solution.py:803
  389.7 1.8 collective-permute-start.30
  391.5 2.8 collective-permute-done.35
  394.3 1.8 collective-permute-start.36
  396.1 3.9 collective-permute-done.36
  402.4 1.8 collective-permute-start.37
  404.2 3.6 broadcast_select_fusion.1
  407.8 1.9 pad_maximum_fusion.1
  409.7 1.9 pad_maximum_fusion
  411.6 1.7 collective-permute-done.37
  (120 shorter events, 23.1 us)
Async XLA Ops:
  7.2 113.7 %all-gather.3.cloned.1.call-start = ((), (), s32[]{:S(2)}) async-start(), calls=%async_computation.2 | async-start | bytes 11280384 | tf_op jit(solution)/shard_map/all_gather | solution.py:900
  9.7 392.7 %reduce-scatter.2.cloned.1.call-start = ((), (), s32[]{:S(2)}) async-start(), calls=%async_computation.1 | async-start | bytes 11280384 | tf_op jit(solution)/shard_map/reduce_scatter | solution.py:961
  9.8 63.3 %copy-start.2 = (bf16[4,512,768]{2,1,0:T(8,128)(2,1)S(1)}, bf16[4,512,768]{2,1,0:T(8,128)(2,1)}, u32[]{:S(2)}) copy-start(bf16[4,512,768]{2,1,0:T(8,128)(2,1)} %param.29) | copy-start | bytes 9437188
  13.2 67.2 %collective-permute-start = (bf16[2,512,768]{2,1,0:T(8,128)(2,1)S(1)}, bf16[2,512,768]{2,1,0:T(8,128)(2,1)}, u32[]{:S(2)}, u32[]{:S(2)}) collective-permute-start(bf16[2,512,768]{2,1,0:T(8,128)(2,1)S(1)} %get-tuple-element.76), channel_id=1, source_target_pairs={{0,1},{1,0},{2,3},{3,2},{4,5},{5,4},{6,7},{7,6},{8,9},{9,8},{10,11... | collective-permute-start | bytes 4718600 | tf_op jit(solution)/shard_map/ppermute | solution.py:803
  13.7 65.2 %copy-start.6 = (s32[4,8]{1,0:T(4,128)S(1)}, s32[4,8]{1,0:T(4,128)}, u32[]{:S(2)}) copy-start(s32[4,8]{1,0:T(4,128)} %param.28) | copy-start | bytes 388
  13.7 17.7 %collective-permute-start.1 = (bf16[48,2432]{1,0:T(8,128)(2,1)S(1)}, bf16[48,2432]{1,0:T(8,128)(2,1)S(1)}, u32[]{:S(2)}, u32[]{:S(2)}) collective-permute-start(bf16[48,2432]{1,0:T(8,128)(2,1)S(1)} %copy-done.7), channel_id=1, source_target_pairs={{0,8},{2,10},{4,12},{6,14},{8,16},{10,18},{12,20},{14,22},{16,24},... | collective-permute-start | bytes 700424 | tf_op jit(solution)/shard_map/ppermute | solution.py:831
  15.2 37.0 %collective-permute-start.2 = (bf16[48,2432]{1,0:T(8,128)(2,1)S(1)}, bf16[48,2432]{1,0:T(8,128)(2,1)S(1)}, u32[]{:S(2)}, u32[]{:S(2)}) collective-permute-start(bf16[48,2432]{1,0:T(8,128)(2,1)S(1)} %copy-done.7), channel_id=1, source_target_pairs={{0,16},{2,18},{4,20},{6,22},{8,24},{10,26},{12,28},{14,30},{16,0},... | collective-permute-start | bytes 700424 | tf_op jit(solution)/shard_map/ppermute | solution.py:831
  16.3 40.2 %collective-permute-start.3 = (bf16[48,2432]{1,0:T(8,128)(2,1)S(1)}, bf16[48,2432]{1,0:T(8,128)(2,1)S(1)}, u32[]{:S(2)}, u32[]{:S(2)}) collective-permute-start(bf16[48,2432]{1,0:T(8,128)(2,1)S(1)} %copy-done.7), channel_id=1, source_target_pairs={{0,24},{2,26},{4,28},{6,30},{8,0},{10,2},{12,4},{14,6},{16,8},{18,... | collective-permute-start | bytes 700424 | tf_op jit(solution)/shard_map/ppermute | solution.py:831
  18.3 39.7 %collective-permute-start.4 = (bf16[48,2432]{1,0:T(8,128)(2,1)S(1)}, bf16[48,2432]{1,0:T(8,128)(2,1)S(1)}, u32[]{:S(2)}, u32[]{:S(2)}) collective-permute-start(bf16[48,2432]{1,0:T(8,128)(2,1)S(1)} %copy-done.7), channel_id=1, source_target_pairs={{0,4},{2,6},{4,0},{6,2},{8,12},{10,14},{12,8},{14,10},{16,20},{18,... | collective-permute-start | bytes 700424 | tf_op jit(solution)/shard_map/ppermute | solution.py:831
  31.3 43.1 %copy-start.8 = (bf16[48,2432]{1,0:T(8,128)(2,1)}, bf16[48,2432]{1,0:T(8,128)(2,1)S(1)}, u32[]{:S(2)}) copy-start(bf16[48,2432]{1,0:T(8,128)(2,1)S(1)} %collective-permute-done.1.refs_1_) | copy-start | bytes 700420
  31.3 27.2 %collective-permute-start.8 = (bf16[48,2432]{1,0:T(8,128)(2,1)S(1)}, bf16[48,2432]{1,0:T(8,128)(2,1)S(1)}, u32[]{:S(2)}, u32[]{:S(2)}) collective-permute-start(bf16[48,2432]{1,0:T(8,128)(2,1)S(1)} %copy-done.7), channel_id=1, source_target_pairs={{0,2},{2,0},{4,6},{6,4},{8,10},{10,8},{12,14},{14,12},{16,18},{18,... | collective-permute-start | bytes 700424 | tf_op jit(solution)/shard_map/ppermute | solution.py:831
  52.2 22.2 %copy-start.9 = (bf16[48,2432]{1,0:T(8,128)(2,1)}, bf16[48,2432]{1,0:T(8,128)(2,1)S(1)}, u32[]{:S(2)}) copy-start(bf16[48,2432]{1,0:T(8,128)(2,1)S(1)} %collective-permute-done.2.refs_2_) | copy-start | bytes 700420
  52.2 6.3 %collective-permute-start.5 = (bf16[48,2432]{1,0:T(8,128)(2,1)S(1)}, bf16[48,2432]{1,0:T(8,128)(2,1)}, u32[]{:S(2)}, u32[]{:S(2)}) collective-permute-start(bf16[48,2432]{1,0:T(8,128)(2,1)S(1)} %collective-permute-done.1.refs_1_), channel_id=1, source_target_pairs={{0,4},{2,6},{4,0},{6,2},{8,12},{10,14},{12,8},{14,10},{16,20},{18,... | collective-permute-start | bytes 700424 | tf_op jit(solution)/shard_map/ppermute | solution.py:831
  56.5 17.9 %copy-start.10 = (bf16[48,2432]{1,0:T(8,128)(2,1)}, bf16[48,2432]{1,0:T(8,128)(2,1)S(1)}, u32[]{:S(2)}) copy-start(bf16[48,2432]{1,0:T(8,128)(2,1)S(1)} %collective-permute-done.3.refs_3_) | copy-start | bytes 700420
  56.5 8.7 %collective-permute-start.6 = (bf16[48,2432]{1,0:T(8,128)(2,1)S(1)}, bf16[48,2432]{1,0:T(8,128)(2,1)}, u32[]{:S(2)}, u32[]{:S(2)}) collective-permute-start(bf16[48,2432]{1,0:T(8,128)(2,1)S(1)} %collective-permute-done.2.refs_2_), channel_id=1, source_target_pairs={{0,4},{2,6},{4,0},{6,2},{8,12},{10,14},{12,8},{14,10},{16,20},{18,... | collective-permute-start | bytes 700424 | tf_op jit(solution)/shard_map/ppermute | solution.py:831
  58.0 16.4 %copy-start.11 = (bf16[48,2432]{1,0:T(8,128)(2,1)}, bf16[48,2432]{1,0:T(8,128)(2,1)S(1)}, u32[]{:S(2)}) copy-start(bf16[48,2432]{1,0:T(8,128)(2,1)S(1)} %collective-permute-done.4.refs_4_) | copy-start | bytes 700420
  58.0 15.0 %collective-permute-start.7 = (bf16[48,2432]{1,0:T(8,128)(2,1)S(1)}, bf16[48,2432]{1,0:T(8,128)(2,1)}, u32[]{:S(2)}, u32[]{:S(2)}) collective-permute-start(bf16[48,2432]{1,0:T(8,128)(2,1)S(1)} %collective-permute-done.3.refs_3_), channel_id=1, source_target_pairs={{0,4},{2,6},{4,0},{6,2},{8,12},{10,14},{12,8},{14,10},{16,20},{18,... | collective-permute-start | bytes 700424 | tf_op jit(solution)/shard_map/ppermute | solution.py:831
  58.5 14.5 %copy-start.12 = (bf16[48,2432]{1,0:T(8,128)(2,1)}, bf16[48,2432]{1,0:T(8,128)(2,1)S(1)}, u32[]{:S(2)}) copy-start(bf16[48,2432]{1,0:T(8,128)(2,1)S(1)} %collective-permute-done.8.refs_8_) | copy-start | bytes 700420
  58.5 15.9 %collective-permute-start.10 = (bf16[48,2432]{1,0:T(8,128)(2,1)S(1)}, bf16[48,2432]{1,0:T(8,128)(2,1)S(1)}, u32[]{:S(2)}, u32[]{:S(2)}) collective-permute-start(bf16[48,2432]{1,0:T(8,128)(2,1)S(1)} %collective-permute-done.2.refs_2_), channel_id=1, source_target_pairs={{0,2},{2,0},{4,6},{6,4},{8,10},{10,8},{12,14},{14,12},{16,18},{18,... | collective-permute-start | bytes 700424 | tf_op jit(solution)/shard_map/ppermute | solution.py:831
  58.5 18.4 %collective-permute-start.11 = (bf16[48,2432]{1,0:T(8,128)(2,1)S(1)}, bf16[48,2432]{1,0:T(8,128)(2,1)S(1)}, u32[]{:S(2)}, u32[]{:S(2)}) collective-permute-start(bf16[48,2432]{1,0:T(8,128)(2,1)S(1)} %collective-permute-done.3.refs_3_), channel_id=1, source_target_pairs={{0,2},{2,0},{4,6},{6,4},{8,10},{10,8},{12,14},{14,12},{16,18},{18,... | collective-permute-start | bytes 700424 | tf_op jit(solution)/shard_map/ppermute | solution.py:831
  65.2 12.0 %collective-permute-start.9 = (bf16[48,2432]{1,0:T(8,128)(2,1)S(1)}, bf16[48,2432]{1,0:T(8,128)(2,1)S(1)}, u32[]{:S(2)}, u32[]{:S(2)}) collective-permute-start(bf16[48,2432]{1,0:T(8,128)(2,1)S(1)} %collective-permute-done.1.refs_1_), channel_id=1, source_target_pairs={{0,2},{2,0},{4,6},{6,4},{8,10},{10,8},{12,14},{14,12},{16,18},{18,... | collective-permute-start | bytes 700424 | tf_op jit(solution)/shard_map/ppermute | solution.py:831
  73.0 4.4 %collective-permute-start.12 = (bf16[48,2432]{1,0:T(8,128)(2,1)S(1)}, bf16[48,2432]{1,0:T(8,128)(2,1)S(1)}, u32[]{:S(2)}, u32[]{:S(2)}) collective-permute-start(bf16[48,2432]{1,0:T(8,128)(2,1)S(1)} %collective-permute-done.4.refs_4_), channel_id=1, source_target_pairs={{0,2},{2,0},{4,6},{6,4},{8,10},{10,8},{12,14},{14,12},{16,18},{18,... | collective-permute-start | bytes 700424 | tf_op jit(solution)/shard_map/ppermute | solution.py:831
  74.4 5.9 %copy-start.13 = (bf16[48,2432]{1,0:T(8,128)(2,1)}, bf16[48,2432]{1,0:T(8,128)(2,1)S(1)}, u32[]{:S(2)}) copy-start(bf16[48,2432]{1,0:T(8,128)(2,1)S(1)} %collective-permute-done.10.refs_10_) | copy-start | bytes 700420
  74.4 46.4 %collective-permute-start.16 = (bf16[2,512,768]{2,1,0:T(8,128)(2,1)S(1)}, bf16[2,512,768]{2,1,0:T(8,128)(2,1)}, u32[]{:S(2)}, u32[]{:S(2)}) collective-permute-start(bf16[2,512,768]{2,1,0:T(8,128)(2,1)S(1)} %get-tuple-element.74), channel_id=1, source_target_pairs={{0,1},{1,0},{2,3},{3,2},{4,5},{5,4},{6,7},{7,6},{8,9},{9,8},{10,11... | collective-permute-start | bytes 4718600 | tf_op jit(solution)/shard_map/ppermute | solution.py:803
  76.9 3.2 collective-permute-start.13
  77.1 3.0 collective-permute-start.14
  78.5 1.8 collective-permute-start.15
  275.4 40.9 %collective-permute-start.19 = (bf16[8,48,768]{2,1,0:T(8,128)(2,1)}, bf16[8,48,768]{2,1,0:T(8,128)(2,1)}, u32[]{:S(2)}, u32[]{:S(2)}) collective-permute-start(bf16[8,48,768]{2,1,0:T(8,128)(2,1)} %dynamic-slice_bitcast_fusion.2), channel_id=1, source_target_pairs={{0,2},{2,0},{4,6},{6,4},{8,10},{10,8},{12,14},{14,12},{16,18},{18,... | collective-permute-start | bytes 1769480 | tf_op jit(solution)/shard_map/ppermute | solution.py:831
  283.8 32.5 %collective-permute-start.25 = (bf16[8,48,768]{2,1,0:T(8,128)(2,1)}, bf16[8,48,768]{2,1,0:T(8,128)(2,1)}, u32[]{:S(2)}, u32[]{:S(2)}) collective-permute-start(bf16[8,48,768]{2,1,0:T(8,128)(2,1)} %dynamic-slice_bitcast_fusion.1), channel_id=1, source_target_pairs={{0,2},{2,0},{4,6},{6,4},{8,10},{10,8},{12,14},{14,12},{16,18},{18,... | collective-permute-start | bytes 1769480 | tf_op jit(solution)/shard_map/ppermute | solution.py:831
  296.2 24.8 %collective-permute-start.31 = (bf16[8,64,768]{2,1,0:T(8,128)(2,1)}, bf16[8,64,768]{2,1,0:T(8,128)(2,1)}, u32[]{:S(2)}, u32[]{:S(2)}) collective-permute-start(bf16[8,64,768]{2,1,0:T(8,128)(2,1)} %dynamic-slice_bitcast_fusion), channel_id=1, source_target_pairs={{0,2},{2,0},{4,6},{6,4},{8,10},{10,8},{12,14},{14,12},{16,18},{18,... | collective-permute-start | bytes 2359304 | tf_op jit(solution)/shard_map/ppermute | solution.py:831
  313.8 90.4 %collective-permute-start.18 = (bf16[2,512,768]{2,1,0:T(8,128)(2,1)}, bf16[2,512,768]{2,1,0:T(8,128)(2,1)}, u32[]{:S(2)}, u32[]{:S(2)}) collective-permute-start(bf16[2,512,768]{2,1,0:T(8,128)(2,1)} %constant_dynamic-slice_fusion.9), channel_id=1, source_target_pairs={{0,1},{1,0},{2,3},{3,2},{4,5},{5,4},{6,7},{7,6},{8,9},{9,8},{10,11... | collective-permute-start | bytes 4718600 | tf_op jit(solution)/shard_map/ppermute | solution.py:803
  318.8 15.7 %collective-permute-start.20 = (bf16[4,48,768]{2,1,0:T(8,128)(2,1)S(1)}, bf16[4,48,768]{2,1,0:T(8,128)(2,1)S(1)}, u32[]{:S(2)}, u32[]{:S(2)}) collective-permute-start(bf16[4,48,768]{2,1,0:T(8,128)(2,1)S(1)} %dynamic-slice_bitcast_fusion.5), channel_id=1, source_target_pairs={{0,4},{2,6},{4,0},{6,2},{8,12},{10,14},{12,8},{14,10},{16,20},{18,... | collective-permute-start | bytes 884744 | tf_op jit(solution)/shard_map/ppermute | solution.py:831
  321.0 21.3 %collective-permute-start.26 = (bf16[4,48,768]{2,1,0:T(8,128)(2,1)S(1)}, bf16[4,48,768]{2,1,0:T(8,128)(2,1)S(1)}, u32[]{:S(2)}, u32[]{:S(2)}) collective-permute-start(bf16[4,48,768]{2,1,0:T(8,128)(2,1)S(1)} %dynamic-slice_bitcast_fusion.4), channel_id=1, source_target_pairs={{0,4},{2,6},{4,0},{6,2},{8,12},{10,14},{12,8},{14,10},{16,20},{18,... | collective-permute-start | bytes 884744 | tf_op jit(solution)/shard_map/ppermute | solution.py:831
  322.5 35.5 %collective-permute-start.32 = (bf16[4,64,768]{2,1,0:T(8,128)(2,1)S(1)}, bf16[4,64,768]{2,1,0:T(8,128)(2,1)S(1)}, u32[]{:S(2)}, u32[]{:S(2)}) collective-permute-start(bf16[4,64,768]{2,1,0:T(8,128)(2,1)S(1)} %dynamic-slice_bitcast_fusion.3), channel_id=1, source_target_pairs={{0,4},{2,6},{4,0},{6,2},{8,12},{10,14},{12,8},{14,10},{16,20},{18,... | collective-permute-start | bytes 1179656 | tf_op jit(solution)/shard_map/ppermute | solution.py:831
  334.7 7.7 %collective-permute-start.21 = (bf16[1,48,768]{2,1,0:T(8,128)(2,1)S(1)}, bf16[1,48,768]{2,1,0:T(8,128)(2,1)S(1)}, u32[]{:S(2)}, u32[]{:S(2)}) collective-permute-start(bf16[1,48,768]{2,1,0:T(8,128)(2,1)S(1)} %get-tuple-element.83), channel_id=1, source_target_pairs={{0,8},{2,10},{4,12},{6,14},{8,16},{10,18},{12,20},{14,22},{16,24},... | collective-permute-start | bytes 221192 | tf_op jit(solution)/shard_map/ppermute | solution.py:831
  334.7 9.7 %collective-permute-start.22 = (bf16[1,48,768]{2,1,0:T(8,128)(2,1)S(1)}, bf16[1,48,768]{2,1,0:T(8,128)(2,1)S(1)}, u32[]{:S(2)}, u32[]{:S(2)}) collective-permute-start(bf16[1,48,768]{2,1,0:T(8,128)(2,1)S(1)} %get-tuple-element.85), channel_id=1, source_target_pairs={{0,16},{2,18},{4,20},{6,22},{8,24},{10,26},{12,28},{14,30},{16,0},... | collective-permute-start | bytes 221192 | tf_op jit(solution)/shard_map/ppermute | solution.py:831
  342.2 10.9 %collective-permute-start.23 = (bf16[1,48,768]{2,1,0:T(8,128)(2,1)S(1)}, bf16[1,48,768]{2,1,0:T(8,128)(2,1)S(1)}, u32[]{:S(2)}, u32[]{:S(2)}) collective-permute-start(bf16[1,48,768]{2,1,0:T(8,128)(2,1)S(1)} %get-tuple-element.84), channel_id=1, source_target_pairs={{0,24},{2,26},{4,28},{6,30},{8,0},{10,2},{12,4},{14,6},{16,8},{18,... | collective-permute-start | bytes 221192 | tf_op jit(solution)/shard_map/ppermute | solution.py:831
  342.4 10.8 %collective-permute-start.27 = (bf16[1,48,768]{2,1,0:T(8,128)(2,1)S(1)}, bf16[1,48,768]{2,1,0:T(8,128)(2,1)S(1)}, u32[]{:S(2)}, u32[]{:S(2)}) collective-permute-start(bf16[1,48,768]{2,1,0:T(8,128)(2,1)S(1)} %get-tuple-element.86), channel_id=1, source_target_pairs={{0,8},{2,10},{4,12},{6,14},{8,16},{10,18},{12,20},{14,22},{16,24},... | collective-permute-start | bytes 221192 | tf_op jit(solution)/shard_map/ppermute | solution.py:831
  344.4 11.6 %collective-permute-start.28 = (bf16[1,48,768]{2,1,0:T(8,128)(2,1)S(1)}, bf16[1,48,768]{2,1,0:T(8,128)(2,1)S(1)}, u32[]{:S(2)}, u32[]{:S(2)}) collective-permute-start(bf16[1,48,768]{2,1,0:T(8,128)(2,1)S(1)} %get-tuple-element.88), channel_id=1, source_target_pairs={{0,16},{2,18},{4,20},{6,22},{8,24},{10,26},{12,28},{14,30},{16,0},... | collective-permute-start | bytes 221192 | tf_op jit(solution)/shard_map/ppermute | solution.py:831
  353.2 4.8 %collective-permute-start.29 = (bf16[1,48,768]{2,1,0:T(8,128)(2,1)S(1)}, bf16[1,48,768]{2,1,0:T(8,128)(2,1)S(1)}, u32[]{:S(2)}, u32[]{:S(2)}) collective-permute-start(bf16[1,48,768]{2,1,0:T(8,128)(2,1)S(1)} %get-tuple-element.87), channel_id=1, source_target_pairs={{0,24},{2,26},{4,28},{6,30},{8,0},{10,2},{12,4},{14,6},{16,8},{18,... | collective-permute-start | bytes 221192 | tf_op jit(solution)/shard_map/ppermute | solution.py:831
  353.2 51.0 %collective-permute-start.17 = (bf16[2,512,768]{2,1,0:T(8,128)(2,1)}, bf16[2,512,768]{2,1,0:T(8,128)(2,1)}, u32[]{:S(2)}, u32[]{:S(2)}) collective-permute-start(bf16[2,512,768]{2,1,0:T(8,128)(2,1)} %constant_dynamic-slice_fusion.10), channel_id=1, source_target_pairs={{0,1},{1,0},{2,3},{3,2},{4,5},{5,4},{6,7},{7,6},{8,9},{9,8},{10,11... | collective-permute-start | bytes 4718600 | tf_op jit(solution)/shard_map/ppermute | solution.py:803
  356.1 33.3 %collective-permute-start.24 = (bf16[48,768]{1,0:T(8,128)(2,1)S(1)}, bf16[48,768]{1,0:T(8,128)(2,1)S(1)}, u32[]{:S(2)}, u32[]{:S(2)}) collective-permute-start(bf16[48,768]{1,0:T(8,128)(2,1)S(1)} %fusion.7), channel_id=1, source_target_pairs={{0,1},{1,0},{2,3},{3,2},{4,5},{5,4},{6,7},{7,6},{8,9},{9,8},{10,11... | collective-permute-start | bytes 221192 | tf_op jit(solution)/shard_map/ppermute | solution.py:803
  358.2 31.4 %collective-permute-start.33 = (bf16[1,64,768]{2,1,0:T(8,128)(2,1)S(1)}, bf16[1,64,768]{2,1,0:T(8,128)(2,1)S(1)}, u32[]{:S(2)}, u32[]{:S(2)}) collective-permute-start(bf16[1,64,768]{2,1,0:T(8,128)(2,1)S(1)} %get-tuple-element.80), channel_id=1, source_target_pairs={{0,8},{2,10},{4,12},{6,14},{8,16},{10,18},{12,20},{14,22},{16,24},... | collective-permute-start | bytes 294920 | tf_op jit(solution)/shard_map/ppermute | solution.py:831
  358.8 32.7 %collective-permute-start.34 = (bf16[1,64,768]{2,1,0:T(8,128)(2,1)S(1)}, bf16[1,64,768]{2,1,0:T(8,128)(2,1)S(1)}, u32[]{:S(2)}, u32[]{:S(2)}) collective-permute-start(bf16[1,64,768]{2,1,0:T(8,128)(2,1)S(1)} %get-tuple-element.82), channel_id=1, source_target_pairs={{0,16},{2,18},{4,20},{6,22},{8,24},{10,26},{12,28},{14,30},{16,0},... | collective-permute-start | bytes 294920 | tf_op jit(solution)/shard_map/ppermute | solution.py:831
  389.4 4.8 %collective-permute-start.35 = (bf16[1,64,768]{2,1,0:T(8,128)(2,1)S(1)}, bf16[1,64,768]{2,1,0:T(8,128)(2,1)S(1)}, u32[]{:S(2)}, u32[]{:S(2)}) collective-permute-start(bf16[1,64,768]{2,1,0:T(8,128)(2,1)S(1)} %get-tuple-element.81), channel_id=1, source_target_pairs={{0,24},{2,26},{4,28},{6,30},{8,0},{10,2},{12,4},{14,6},{16,8},{18,... | collective-permute-start | bytes 294920 | tf_op jit(solution)/shard_map/ppermute | solution.py:831
  389.7 6.4 %collective-permute-start.30 = (bf16[48,768]{1,0:T(8,128)(2,1)S(1)}, bf16[48,768]{1,0:T(8,128)(2,1)S(1)}, u32[]{:S(2)}, u32[]{:S(2)}) collective-permute-start(bf16[48,768]{1,0:T(8,128)(2,1)S(1)} %fusion.8), channel_id=1, source_target_pairs={{0,1},{1,0},{2,3},{3,2},{4,5},{5,4},{6,7},{7,6},{8,9},{9,8},{10,11... | collective-permute-start | bytes 221192 | tf_op jit(solution)/shard_map/ppermute | solution.py:803
  394.3 5.7 %collective-permute-start.36 = (bf16[64,768]{1,0:T(8,128)(2,1)S(1)}, bf16[64,768]{1,0:T(8,128)(2,1)S(1)}, u32[]{:S(2)}, u32[]{:S(2)}) collective-permute-start(bf16[64,768]{1,0:T(8,128)(2,1)S(1)} %fusion.6), channel_id=1, source_target_pairs={{0,1},{1,0},{2,3},{3,2},{4,5},{5,4},{6,7},{7,6},{8,9},{9,8},{10,11... | collective-permute-start | bytes 294920 | tf_op jit(solution)/shard_map/ppermute | solution.py:803
  402.4 10.9 %collective-permute-start.37 = (bf16[432,768]{1,0:T(8,128)(2,1)}, bf16[432,768]{1,0:T(8,128)(2,1)S(1)}, u32[]{:S(2)}, u32[]{:S(2)}) collective-permute-start(bf16[432,768]{1,0:T(8,128)(2,1)} %bitcast.112), channel_id=1, source_target_pairs={{0,1},{1,0},{2,3},{3,2},{4,5},{5,4},{6,7},{7,6},{8,9},{9,8},{10,11... | collective-permute-start | bytes 1990664 | tf_op jit(solution)/shard_map/ppermute | solution.py:803
  (9 other events, 22.4 us)
Sparse Core Ops, SparseCore 0:
  10.3 103.0 all-gather.2
  226.8 130.3 reduce-scatter.1

commit v3 on v2

--- a/solution.py
+++ b/solution.py
@@ -19,6 +19,9 @@
 MASKED = -1e30
 VMEM_LIMIT = 60 << 20
 BLOCK = 256
+COST = 4
+GROUP = H
+GROUP_ROWS = -(-GROUP // 8) * 8
 WINDOWS = (2, 3, 4, 5, 6)
 
 
@@ -36,6 +39,12 @@
 
 def column_sum(values):
     return jnp.sum(values, axis=0, keepdims=True)
+
+
+def cost(flops, bytes_accessed, transcendentals=0):
+    return pl.CostEstimate(
+        flops=flops // COST, bytes_accessed=bytes_accessed // COST, transcendentals=transcendentals // COST
+    )
 
 
 def shape_of(shape, dtype):
@@ -89,31 +98,32 @@
     )(w_qkv, w_in, w_ffo, w_out, *[v.reshape(1, -1) for v in small])
 
 
+def places(total, size):
+    at = lax.broadcasted_iota(jnp.int32, (1, total), 1)
+    return at % size, at // size
+
+
+def picker(place, at):
+    lane = lax.broadcasted_iota(jnp.int32, (LANES, place.shape[1]), 0)
+    return jnp.where(place == lane + at, 1.0, 0.0).astype(bf16)
+
+
 def spread_vector(block, row, size, shards):
-    total = size * shards
-    place = lax.broadcasted_iota(jnp.int32, (LANES, total), 1) % size
-    lane = lax.broadcasted_iota(jnp.int32, (LANES, total), 0)
-    found = jnp.zeros((shards, total), f32)
+    place, owner = places(size * shards, size)
+    found = jnp.zeros((shards, size * shards), f32)
     for at in range(0, size, LANES):
-        pick = jnp.where(place == lane + at, 1.0, 0.0).astype(bf16)
-        found = found + dot(block[:, row + at // LANES, :].astype(bf16), pick)
-    owner = lax.broadcasted_iota(jnp.int32, (shards, total), 0)
-    mine = lax.broadcasted_iota(jnp.int32, (shards, total), 1) // size
-    return column_sum(jnp.where(owner == mine, found, 0.0))
+        found = found + dot(block[:, row + at // LANES, :].astype(bf16), picker(place, at))
+    index = lax.broadcasted_iota(jnp.int32, found.shape, 0)
+    return column_sum(jnp.where(owner == index, found, 0.0))
 
 
 def gather_vector(vector, shards):
     total = vector.shape[1]
     size = total // shards
-    place = lax.broadcasted_iota(jnp.int32, (total, LANES), 0) % size
-    lane = lax.broadcasted_iota(jnp.int32, (total, LANES), 1)
-    owner = lax.broadcasted_iota(jnp.int32, (shards, total), 0)
-    mine = lax.broadcasted_iota(jnp.int32, (shards, total), 1) // size
-    own = jnp.where(owner == mine, vector, 0.0).astype(bf16)
-    return [
-        dot(own, jnp.where(place == lane + at, 1.0, 0.0).astype(bf16))
-        for at in range(0, size, LANES)
-    ]
+    place, owner = places(total, size)
+    index = lax.broadcasted_iota(jnp.int32, (shards, total), 0)
+    own = jnp.where(owner == index, vector, 0.0).astype(bf16)
+    return [dot_nt(own, picker(place, at)) for at in range(0, size, LANES)]
 
 
 def project_kernel(place_ref, mine_ref, other_ref, *refs, shards, pieces):
@@ -155,25 +165,29 @@
     outT_ref[...] = low.T
 
 
-def halves(block_rows, blocks):
+def halves(mine, other, block):
+    rows, half, _ = other.shape
+    blocks = half // block
+    skip = rows if mine.shape[0] > rows else 0
+
     def at(used, r, h, b):
         rest = jnp.where(h == 0, 0, blocks - 1)
         return (r * blocks + jnp.where(used, b, rest), 0)
 
     return (
-        lambda r, h, b, s: at(h == s[0], r, h, b),
+        lambda r, h, b, s: at(h == s[0], r + s[0] * skip, h, b),
         lambda r, h, b, s: at(h != s[0], r, h, b),
     )
 
 
 def project(place, mine, other, weight, inner, block):
-    rows, half, width = mine.shape
+    rows, half, width = other.shape
     block = min(block, half)
     blocks = half // block
     columns = 3 * width
     tokens = 2 * rows * half
     shards = lax.axis_size("dp")
-    mine_at, other_at = halves(block, blocks)
+    mine_at, other_at = halves(mine, other, block)
 
     def at(r, h, b, s):
         return ((r * 2 + h) * blocks + b, 0)
@@ -210,7 +224,7 @@
             shape_of((8, inner), f32),
         ],
         compiler_params=pltpu.CompilerParams(vmem_limit_bytes=VMEM_LIMIT),
-        cost_estimate=pl.CostEstimate(
+        cost_estimate=cost(
             flops=2 * tokens * width * columns,
             bytes_accessed=2 * (2 * tokens * width + 2 * width * columns + 2 * tokens * columns),
             transcendentals=0,
@@ -269,12 +283,16 @@
     return slice(PAIR * (h // 2), PAIR * (h // 2) + PAIR)
 
 
+def log_row(h):
+    return GROUP_ROWS * (h // GROUP) + h % GROUP
+
+
 def in_pair(h, rows):
     zero = jnp.zeros_like(rows)
     return jnp.concatenate([rows, zero] if h % 2 == 0 else [zero, rows], axis=0)
 
 
-def attend_kernel(bounds_ref, k_ref, qT_ref, vT_ref, out_ref, outT_ref, log_ref, bias_ref):
+def attend_kernel(bounds_ref, k_ref, qT_ref, vT_ref, outT_ref, log_ref, bias_ref):
     row = pl.program_id(0)
     row_len, width = k_ref.shape
     block = qT_ref.shape[1]
@@ -301,7 +319,8 @@
             summed = dot(values, weights)
             total = summed[HD : HD + 1]
             outT_ref[head_rows(h), :] = (summed[:HD] * (1.0 / total)).astype(bf16)
-            log_ref[h : h + 1, :] = best * EXP2_SCALE + jnp.log2(total)
+            at = log_row(h)
+            log_ref[at : at + 1, :] = best * EXP2_SCALE + jnp.log2(total)
 
         scores = [score(0), score(1)]
         held = None
@@ -318,7 +337,6 @@
         attend(heads - 1, *held[1])
 
     with_window(first, last, row_len, body)
-    out_ref[...] = outT_ref[...].T
 
 
 def attend_rows(bounds, qkv, qkvT, block):
@@ -338,19 +356,17 @@
                 pl.BlockSpec((width, row_len), lambda r, b, s: (2, r)),
             ],
             out_specs=[
-                pl.BlockSpec((block, width), lambda r, b, s: (r * blocks + b, 0)),
                 pl.BlockSpec((width, block), lambda r, b, s: (0, r * blocks + b)),
-                pl.BlockSpec((16, block), lambda r, b, s: (0, r * blocks + b)),
+                pl.BlockSpec((H // GROUP * GROUP_ROWS, block), lambda r, b, s: (0, r * blocks + b)),
             ],
             scratch_shapes=[pltpu.VMEM((max(WINDOWS) * LANES, block), f32)],
         ),
         out_shape=[
-            shape_of((tokens, width), bf16),
             shape_of((width, tokens), bf16),
-            shape_of((16, tokens), f32),
+            shape_of((H // GROUP * GROUP_ROWS, tokens), f32),
         ],
         compiler_params=pltpu.CompilerParams(vmem_limit_bytes=VMEM_LIMIT),
-        cost_estimate=pl.CostEstimate(
+        cost_estimate=cost(
             flops=16 * tokens * row_len * width // 4,
             bytes_accessed=10 * tokens * width,
             transcendentals=0,
@@ -361,14 +377,15 @@
 
 def attend_back_kernel(
     bounds_ref, k_ref, kT_ref, v_ref, q_ref, qT_ref, do_ref, doT_ref, outT_ref, log_ref,
-    dq_ref, dk_ref, dv_ref, sum_ref, bias_ref, dqT_ref, delta_ref,
+    grad_ref, sum_ref, bias_ref, dqT_ref, delta_ref,
 ):
-    row = pl.program_id(0)
-    at = pl.program_id(1)
+    row = pl.program_id(1)
+    at = pl.program_id(2)
     row_len, width = q_ref.shape
     block = k_ref.shape[0]
     heads = width // HD
     k_start = at * block
+    keys = pl.ds(pl.multiple_of(k_start, block), block)
 
     @pl.when((row == 0) & (at == 0))
     def _():
@@ -409,8 +426,11 @@
             if h % 2 == 0:
                 even[0] = (dv, dk)
             else:
-                dk_ref[:, lanes] = (jnp.where(low_half, even[0][1], dk) * SCORE_SCALE).astype(bf16)
-                dv_ref[:, lanes] = jnp.where(low_half, even[0][0], dv).astype(bf16)
+                dk = jnp.where(low_half, even[0][1], dk) * SCORE_SCALE
+                dv = jnp.where(low_half, even[0][0], dv)
+                for part, value in ((1, dk), (2, dv)):
+                    at_lanes = slice(part * width + lanes.start, part * width + lanes.stop)
+                    grad_ref[keys, at_lanes] = value.astype(bf16)
 
         made = products(0)
         held = None
@@ -425,51 +445,64 @@
         gather(heads - 1, *held)
 
     with_window(first, last, row_len, body)
-    sum_ref[1:2, :] += column_sum(dv_ref[...].astype(f32))
-
-    @pl.when(at == pl.num_programs(1) - 1)
+
+    @pl.when(at == pl.num_programs(2) - 1)
     def _():
-        dq = (dqT_ref[...] * SCORE_SCALE).astype(bf16).T
-        dq_ref[...] = dq
-        sum_ref[0:1, :] += column_sum(dq.astype(f32))
-
-
-def attend_rows_back(bounds, qkv, qkvT, do, doT, outT, log, block):
+        grad_ref[:, :width] = (dqT_ref[...] * SCORE_SCALE).astype(bf16).T
+        sum_ref[0:1, :] += column_sum(grad_ref[:, :width].astype(f32))
+        sum_ref[1:2, :] += column_sum(grad_ref[:, 2 * width :].astype(f32))
+
+
+def attend_rows_back(bounds, qkv, qkvT, do, doT, outT, log, first, count, block):
     rows = bounds.shape[0]
-    tokens, width = do.shape
+    tokens = do.shape[0]
+    width = GROUP * HD
+    groups = H // GROUP
     row_len = tokens // rows
     blocks = row_len // block
-    whole = pl.BlockSpec((row_len, width), lambda r, b, s: (r, 0))
-    wholeT = pl.BlockSpec((width, row_len), lambda r, b, s: (0, r))
-    part = pl.BlockSpec((block, width), lambda r, b, s: (r * blocks + b, 0))
+    whole = pl.BlockSpec((row_len, width), lambda g, r, b, s: (r, first + g))
+    wholeT = pl.BlockSpec((width, row_len), lambda g, r, b, s: (first + g, r))
+
+    def part(j):
+        return lambda g, r, b, s: (r * blocks + b, j * groups + first + g)
+
+    def partT(j):
+        return lambda g, r, b, s: (j * groups + first + g, r * blocks + b)
+
     return pl.pallas_call(
         attend_back_kernel,
         grid_spec=pltpu.PrefetchScalarGridSpec(
             num_scalar_prefetch=1,
-            grid=(rows, blocks),
+            grid=(count, rows, blocks),
             in_specs=[
-                pl.BlockSpec((block, width), lambda r, b, s: (r * blocks + b, 1)),
-                pl.BlockSpec((width, block), lambda r, b, s: (1, r * blocks + b)),
-                pl.BlockSpec((block, width), lambda r, b, s: (r * blocks + b, 2)),
+                pl.BlockSpec((block, width), part(1)),
+                pl.BlockSpec((width, block), partT(1)),
+                pl.BlockSpec((block, width), part(2)),
                 whole,
                 wholeT,
                 whole,
                 wholeT,
                 wholeT,
-                pl.BlockSpec((16, row_len), lambda r, b, s: (0, r)),
+                pl.BlockSpec((GROUP_ROWS, row_len), lambda g, r, b, s: (first + g, r)),
             ],
-            out_specs=[whole, part, part, pl.BlockSpec((8, width), lambda r, b, s: (0, 0))],
+            out_specs=[
+                pl.BlockSpec((row_len, 3 * width), lambda g, r, b, s: (r, g)),
+                pl.BlockSpec((8, width), lambda g, r, b, s: (0, g)),
+            ],
             scratch_shapes=[
                 pltpu.VMEM((block, max(WINDOWS) * LANES), f32),
                 pltpu.VMEM((width, row_len), f32),
-                pltpu.VMEM((16, row_len), f32),
+                pltpu.VMEM((GROUP_ROWS, row_len), f32),
             ],
         ),
-        out_shape=[shape_of((tokens, width), bf16)] * 3 + [shape_of((8, width), f32)],
+        out_shape=[
+            shape_of((tokens, 3 * width * count), bf16),
+            shape_of((8, width * count), f32),
+        ],
         compiler_params=pltpu.CompilerParams(vmem_limit_bytes=VMEM_LIMIT),
-        cost_estimate=pl.CostEstimate(
-            flops=40 * tokens * row_len * width // 4,
-            bytes_accessed=22 * tokens * width,
+        cost_estimate=cost(
+            flops=40 * tokens * row_len * width * count // 4,
+            bytes_accessed=22 * tokens * width * count,
             transcendentals=0,
         ),
         name="attend_back",
@@ -493,29 +526,36 @@
     return scale * (grad - jnp.mean(grad, axis=-1, keepdims=True) - normed * along)
 
 
+class Weights:
+    def __init__(self, width, inner, w_out=None, w_in=None, w_ffo=None):
+        self.width = width
+        self.inner = inner
+        self.refs = (w_out, w_in, w_ffo)
+
+    def out(self):
+        return self.refs[0][...].reshape(self.width, self.width)
+
+    def into(self, c):
+        ref = self.refs[1]
+        rows = ref.shape[1] * self.width // self.inner
+        return ref[:, c * rows : (c + 1) * rows, :].reshape(self.width, self.width)
+
+    def ffo(self, c):
+        ref = self.refs[2]
+        if ref.shape[0] == 1:
+            return ref[0, c * self.width : (c + 1) * self.width, :]
+        groups = ref.shape[0] * self.width // self.inner
+        return ref[c * groups : (c + 1) * groups].reshape(self.width, self.width)
+
+
 def dense_kernel(
     side_ref, attn_ref, x_ref, mine_ref, other_ref, wo_ref, wi_ref, wf_ref, vec_ref, bi_ref,
-    out_ref, act_ref, gp_ref, gs_ref, low_ref, gr1_ref, gb_ref, do_ref, doT_ref, sum_ref,
+    keep_ref, send_ref, act_ref, gp_ref, gs_ref, low_ref, gr1_ref, gb_ref, do_ref, doT_ref, sum_ref,
     sum_in_ref, slope_ref,
 ):
     width = x_ref.shape[1]
     inner = bi_ref.shape[1]
-    chunk = width
-    groups, per_group = wi_ref.shape[:2]
-    in_rows = per_group * chunk // inner
-    ffo_groups = max(1, groups * chunk // inner)
-
-    def w_out():
-        return wo_ref[...].reshape(width, width)
-
-    def w_in(c):
-        return wi_ref[:, c * in_rows : (c + 1) * in_rows, :].reshape(width, chunk)
-
-    def w_ffo(c):
-        if groups == 1:
-            return wf_ref[0, c * chunk : (c + 1) * chunk, :]
-        return wf_ref[c * ffo_groups : (c + 1) * ffo_groups].reshape(chunk, width)
-
+    weights = Weights(width, inner, wo_ref, wi_ref, wf_ref)
     bias_out, gain_a, shift_a, bias_ffo, gain_f, shift_f = [vec_ref[j : j + 1, :] for j in range(6)]
 
     @pl.when((pl.program_id(0) == 0) & (pl.program_id(1) == 0) & (pl.program_id(2) == 0))
@@ -523,35 +563,45 @@
         sum_ref[...] = jnp.zeros(sum_ref.shape, f32)
         sum_in_ref[...] = jnp.zeros(sum_in_ref.shape, f32)
 
-    branch = dot(attn_ref[...], w_out()) + bias_out
+    branch = dot_tn(attn_ref[...], weights.out()) + bias_out
     normed_a, scale_a = normalise(x_ref[...].astype(f32) + branch)
     hidden = normed_a * gain_a + shift_a
     low = hidden.astype(bf16)
     low_ref[...] = low
-    cuts = [slice(c * chunk, (c + 1) * chunk) for c in range(inner // chunk)]
+    cuts = [slice(c * width, (c + 1) * width) for c in range(inner // width)]
     last = len(cuts) - 1
 
     second = None
     held = None
-    made = dot(low, w_in(0))
+    made = dot(low, weights.into(0))
     for c, cut in enumerate(cuts):
         pre = made + bi_ref[0:1, cut]
         if c < last:
-            made = dot(low, w_in(c + 1))
+            made = dot(low, weights.into(c + 1))
         value, slope = gelu_and_slope(pre)
         value = value.astype(bf16)
         act_ref[:, cut] = value
         slope_ref[:, cut] = slope.astype(bf16)
         if held is not None:
-            term = dot(held, w_ffo(c - 1))
+            term = dot(held, weights.ffo(c - 1))
             second = term if second is None else second + term
         held = value
-    term = dot(held, w_ffo(last))
+    term = dot(held, weights.ffo(last))
     second = term if second is None else second + term
 
     normed_f, scale_f = normalise(hidden + (second + bias_ffo))
-    out_ref[...] = (normed_f * gain_f + shift_f).astype(bf16)
-    cot = jnp.where(pl.program_id(1) == side_ref[0], mine_ref[...], other_ref[...]).astype(f32)
+    out = (normed_f * gain_f + shift_f).astype(bf16)
+    own = pl.program_id(1) == side_ref[0]
+
+    @pl.when(own)
+    def _():
+        keep_ref[...] = out
+
+    @pl.when(jnp.logical_not(own))
+    def _():
+        send_ref[...] = out
+
+    cot = jnp.where(own, mine_ref[...], other_ref[...]).astype(f32)
     grad_r2 = normalise_back(cot * gain_f, normed_f, scale_f)
     grad_second = grad_r2.astype(bf16)
     gs_ref[...] = grad_second
@@ -561,18 +611,18 @@
 
     grad_hidden = grad_r2
     held = None
-    made = dot_nt(grad_second, w_ffo(0))
+    made = dot_nt(grad_second, weights.ffo(0))
     for c, cut in enumerate(cuts):
         grad_act = made
         if c < last:
-            made = dot_nt(grad_second, w_ffo(c + 1))
+            made = dot_nt(grad_second, weights.ffo(c + 1))
         grad_pre = (grad_act * slope_ref[:, cut].astype(f32)).astype(bf16)
         gp_ref[:, cut] = grad_pre
         sum_in_ref[0:1, cut] += column_sum(grad_pre.astype(f32))
         if held is not None:
-            grad_hidden = grad_hidden + dot_nt(held, w_in(c - 1))
+            grad_hidden = grad_hidden + dot_nt(held, weights.into(c - 1))
         held = grad_pre
-    grad_hidden = grad_hidden + dot_nt(held, w_in(last))
+    grad_hidden = grad_hidden + dot_nt(held, weights.into(last))
 
     grad_r1 = normalise_back(grad_hidden * gain_a, normed_a, scale_a)
     gr1_ref[...] = grad_r1
@@ -581,27 +631,28 @@
     sum_ref[3:4, :] += column_sum(grad_hidden * normed_a)
     sum_ref[4:5, :] += column_sum(grad_hidden)
     sum_ref[5:6, :] += column_sum(grad_branch.astype(f32))
-    grad_attn = dot_nt(grad_branch, w_out()).astype(bf16)
+    grad_attn = dot_nt(grad_branch, weights.out()).astype(bf16)
     do_ref[...] = grad_attn
     doT_ref[...] = grad_attn.T
 
 
+def held(shape, index):
+    return pl.BlockSpec(shape, lambda *_: index, pipeline_mode=pl.Buffered(1))
+
+
 def dense(side, attn, x, mine, other, weights, vectors, bias_in, block):
-    rows, half, width = mine.shape
+    rows, half, width = other.shape
     tokens = 2 * rows * half
     inner = bias_in.shape[1]
     block = min(block, half)
     blocks = half // block
-    mine_at, other_at = halves(block, blocks)
+    mine_at, other_at = halves(mine, other, block)
 
     def at(r, h, b, s):
         return ((r * 2 + h) * blocks + b, 0)
 
     narrow = pl.BlockSpec((block, width), at)
     wide = pl.BlockSpec((block, inner), at)
-
-    def held(shape, index):
-        return pl.BlockSpec(shape, lambda *_: index, pipeline_mode=pl.Buffered(1))
 
     return pl.pallas_call(
         dense_kernel,
@@ -609,7 +660,7 @@
             num_scalar_prefetch=1,
             grid=(rows, 2, blocks),
             in_specs=[
-                narrow,
+                pl.BlockSpec((width, block), lambda *i: (0, at(*i)[0])),
                 narrow,
                 pl.BlockSpec((block, width), mine_at),
                 pl.BlockSpec((block, width), other_at),
@@ -617,7 +668,9 @@
             + [held(shape, index) for _, shape, index in weights]
             + [held(vectors.shape, (0, 0)), held(bias_in.shape, (0, 0))],
             out_specs=[
-                narrow, wide, wide, narrow, narrow, narrow, narrow, narrow,
+                pl.BlockSpec((block, width), mine_at),
+                pl.BlockSpec((block, width), other_at),
+                wide, wide, narrow, narrow, narrow, narrow, narrow,
                 pl.BlockSpec((width, block), lambda *i: (0, at(*i)[0])),
                 pl.BlockSpec((8, width), lambda *_: (0, 0)),
                 pl.BlockSpec((8, inner), lambda *_: (0, 0)),
@@ -625,7 +678,8 @@
             scratch_shapes=[pltpu.VMEM((block, inner), bf16)],
         ),
         out_shape=[
-            shape_of((tokens, width), bf16),
+            shape_of((mine.shape[0] * half, width), bf16),
+            shape_of((rows * half, width), bf16),
             shape_of((tokens, inner), bf16),
             shape_of((tokens, inner), bf16),
             shape_of((tokens, width), bf16),
@@ -638,7 +692,7 @@
             shape_of((8, inner), f32),
         ],
         compiler_params=pltpu.CompilerParams(vmem_limit_bytes=VMEM_LIMIT),
-        cost_estimate=pl.CostEstimate(
+        cost_estimate=cost(
             flops=2 * tokens * width * (2 * width + 4 * inner),
             bytes_accessed=tokens * (22 * width + 4 * inner) + 4 * width * inner,
             transcendentals=2 * tokens * inner,
@@ -650,71 +704,173 @@
     )
 
 
-def product_kernel(a_ref, b_ref, *rest):
-    out_ref = rest[-1]
-    out_ref[...] = dot_tn(a_ref[...], b_ref[...]).astype(bf16).reshape(out_ref.shape)
-
-
-def product_into(buffer, shape, a, b, out_block, out_at, a_moves, steps):
+def product_kernel(*refs, more, split):
+    place_ref, a_ref, b_ref = refs[:3]
+    steps = pl.num_programs(0)
+
+    def write(x_ref, y_ref, times=dot_tn):
+        made = times(x_ref[...], y_ref[...]).astype(bf16)
+        if not split:
+            refs[-1][...] = made.reshape(refs[-1].shape)
+            return
+        keep_ref, send_ref, held_ref = refs[-3:]
+        held_ref[...] = made.reshape(held_ref.shape)
+        core = lax.rem(place_ref[1], 2)
+        keep_ref[...] = held_ref[:, core]
+        send_ref[...] = held_ref[:, 1 - core]
+
+    if more:
+        pl.when(pl.program_id(0) < steps - 1)(lambda: write(a_ref, b_ref))
+        pl.when(pl.program_id(0) == steps - 1)(lambda: write(*refs[3:5], dot))
+    else:
+        write(a_ref, b_ref)
+
+
+def product(place, shape, a, b, out_block, out_at, a_moves, steps, more=(), split=False):
     tokens = a.shape[0]
     a_cols = a.shape[1] // (steps if a_moves else 1)
     b_cols = b.shape[1] // (1 if a_moves else steps)
-    moving = {"index_map": lambda i: (0, i)}
-    still = {"index_map": lambda i: (0, 0), "pipeline_mode": pl.Buffered(1)}
+    moving = {"index_map": lambda i, s: (0, jnp.minimum(i, steps - 1))}
+    still = {"index_map": lambda i, s: (0, 0), "pipeline_mode": pl.Buffered(1)}
     in_specs = [
         pl.BlockSpec((tokens, a_cols), **(moving if a_moves else still)),
         pl.BlockSpec((tokens, b_cols), **(still if a_moves else moving)),
     ]
-    operands = [a, b]
-    aliases = {}
-    if buffer is not None:
-        in_specs.append(pl.BlockSpec(memory_space=pl.ANY))
-        operands.append(buffer)
-        aliases = {2: 0}
+    in_specs += [pl.BlockSpec(v.shape, **still) for v in more]
+    halved = [n // 2 if split else n for n in (shape[0], out_block[0])]
+    out_specs = pl.BlockSpec((halved[1],) + out_block[1:], lambda i, s: out_at(i))
+    out_shape = shape_of((halved[0],) + shape[1:], bf16)
     return pl.pallas_call(
-        product_kernel,
-        grid=(steps,),
-        in_specs=in_specs,
-        out_specs=pl.BlockSpec(out_block, out_at),
-        out_shape=shape_of(shape, bf16),
-        input_output_aliases=aliases,
+        functools.partial(product_kernel, more=bool(more), split=split),
+        grid_spec=pltpu.PrefetchScalarGridSpec(
+            num_scalar_prefetch=1,
+            grid=(steps + bool(more),),
+            in_specs=in_specs,
+            out_specs=[out_specs] * 2 if split else out_specs,
+            scratch_shapes=(
+                [pltpu.VMEM((out_block[0] // 2, 2) + out_block[1:], bf16)] if split else []
+            ),
+        ),
+        out_shape=[out_shape] * 2 if split else out_shape,
         compiler_params=pltpu.CompilerParams(vmem_limit_bytes=VMEM_LIMIT),
-        cost_estimate=pl.CostEstimate(
+        cost_estimate=cost(
             flops=2 * tokens * a.shape[1] * b.shape[1],
             bytes_accessed=2 * (a.size + b.size + a.shape[1] * b.shape[1]),
             transcendentals=0,
         ),
         name="product",
-    )(*operands)
-
-
-def input_grad_kernel(dq_ref, dk_ref, dv_ref, gr1_ref, w_ref, out_ref):
-    width = out_ref.shape[1]
-    total = gr1_ref[...]
-    for j, ref in enumerate((dq_ref, dk_ref, dv_ref)):
-        total = total + dot_nt(ref[...], w_ref[:, j * width : (j + 1) * width])
-    out_ref[...] = total.astype(bf16)
-
-
-def input_grad(dq, dk, dv, grad_r1, weight, block):
-    tokens, width = dq.shape
-    block = min(block, tokens)
-    part = pl.BlockSpec((block, width), lambda i: (i, 0))
+    )(place, a, b, *more)
+
+
+def input_grad_kernel(side_ref, g_ref, gr1_ref, w_ref, keep_ref, send_ref):
+    width = send_ref.shape[1]
+    total = gr1_ref[...] + dot_nt(g_ref[...], w_ref[:, : 3 * width])
+    low = total.astype(bf16)
+    own = pl.program_id(1) == side_ref[0]
+
+    @pl.when(own)
+    def _():
+        keep_ref[...] = low
+
+    @pl.when(jnp.logical_not(own))
+    def _():
+        send_ref[...] = low
+
+
+def input_grad(side, grad_qkv, grad_r1, weight, mine, other, block):
+    rows, half, width = other.shape
+    block = min(block, half)
+    blocks = half // block
+    mine_at, other_at = halves(mine, other, block)
+
+    def at(r, h, b, s):
+        return ((r * 2 + h) * blocks + b, 0)
+
+    keep, send = pl.pallas_call(
+        input_grad_kernel,
+        grid_spec=pltpu.PrefetchScalarGridSpec(
+            num_scalar_prefetch=1,
+            grid=(rows, 2, blocks),
+            in_specs=[
+                pl.BlockSpec((block, grad_qkv.shape[1]), at),
+                pl.BlockSpec((block, width), at),
+                pl.BlockSpec(weight.shape, lambda *_: (0, 0), pipeline_mode=pl.Buffered(1)),
+            ],
+            out_specs=[
+                pl.BlockSpec((block, width), mine_at),
+                pl.BlockSpec((block, width), other_at),
+            ],
+        ),
+        out_shape=[shape_of((v.shape[0] * half, width), bf16) for v in (mine, other)],
+        compiler_params=pltpu.CompilerParams(vmem_limit_bytes=VMEM_LIMIT),
+        cost_estimate=cost(
+            flops=12 * rows * half * width * width,
+            bytes_accessed=24 * rows * half * width + 6 * width * width,
+            transcendentals=0,
+        ),
+        name="input_grad",
+    )(side, grad_qkv, grad_r1, weight)
+    return keep.reshape(mine.shape), send.reshape(other.shape)
+
+
+def vector_block(sums_ref, sums_in_ref, sums_qv_ref, shards):
+    qv = jnp.concatenate([sums_qv_ref[j : j + 1, :] for j in range(2)], axis=1)
+    rows = [sums_ref[j : j + 1, :] for j in range(6)]
+    found = []
+    for v in (qv, rows[5], rows[3], rows[4], sums_in_ref[0:1, :], rows[2], rows[0], rows[1]):
+        found.extend(gather_vector(v, shards))
+    return [v.astype(bf16) for v in found]
+
+
+def last_product_kernel(place_ref, a_ref, b_ref, *refs, shards):
+    keep_ref, send_ref, held_ref = refs[-3:]
+    at = pl.program_id(0)
+    width = a_ref.shape[1]
+    shard = width // shards
+    core = lax.rem(place_ref[1], 2)
+    made = dot_tn(a_ref[...], b_ref[...]).astype(bf16)
+    held_ref[...] = made.reshape(held_ref.shape)
+    rows = pl.ds(pl.multiple_of(at * shard, 16), shard)
+    keep_ref[:, rows, :] = held_ref[:, core]
+    send_ref[:, rows, :] = held_ref[:, 1 - core]
+
+    @pl.when(at == pl.num_programs(0) - 1)
+    def _():
+        held_ref[:, :, :16, :] = jnp.zeros(held_ref[:, :, :16, :].shape, bf16)
+        for j, v in enumerate(vector_block(*refs[:3], shards)):
+            held_ref[:, :, j : j + 1, :LANES] = v.reshape(shards // 2, 2, 1, LANES)
+        end = slice(keep_ref.shape[1] - 16, keep_ref.shape[1])
+        keep_ref[:, end, :] = held_ref[:, core, :16]
+        send_ref[:, end, :] = held_ref[:, 1 - core, :16]
+
+
+def last_product(place, a, b, sums, shards):
+    tokens, width = a.shape
+    steps = b.shape[1] // width
+    shard = width // shards
+    out = (shards // 2, steps * shard + 16, width)
     return pl.pallas_call(
-        input_grad_kernel,
-        grid=(tokens // block,),
-        in_specs=[part] * 4
-        + [pl.BlockSpec(weight.shape, lambda i: (0, 0), pipeline_mode=pl.Buffered(1))],
-        out_specs=part,
-        out_shape=shape_of((tokens, width), bf16),
+        functools.partial(last_product_kernel, shards=shards),
+        grid_spec=pltpu.PrefetchScalarGridSpec(
+            num_scalar_prefetch=1,
+            grid=(steps,),
+            in_specs=[
+                pl.BlockSpec((tokens, width), lambda i, s: (0, 0), pipeline_mode=pl.Buffered(1)),
+                pl.BlockSpec((tokens, width), lambda i, s: (0, i)),
+            ]
+            + [pl.BlockSpec(v.shape, lambda i, s: (0, 0)) for v in sums],
+            out_specs=[pl.BlockSpec(out, lambda i, s: (0, 0, 0))] * 2,
+            scratch_shapes=[pltpu.VMEM((shards // 2, 2, shard, width), bf16)],
+        ),
+        out_shape=[shape_of(out, bf16)] * 2,
         compiler_params=pltpu.CompilerParams(vmem_limit_bytes=VMEM_LIMIT),
-        cost_estimate=pl.CostEstimate(
-            flops=6 * tokens * width * width,
-            bytes_accessed=12 * tokens * width + 6 * width * width,
+        cost_estimate=cost(
+            flops=2 * tokens * width * b.shape[1],
+            bytes_accessed=2 * (a.size + b.size + width * b.shape[1]),
             transcendentals=0,
         ),
-        name="input_grad",
-    )(dq, dk, dv, grad_r1, weight)
+        name="last_product",
+    )(place, a, b, *sums)
 
 
 def split_heads(values):
@@ -767,56 +923,21 @@
     dq = dq.astype(bf16).reshape(-1, width)
     dk, dv = pair[:, :width], pair[:, width:]
     sums = jnp.stack([jnp.sum(dq.astype(f32), axis=0), jnp.sum(dv.astype(f32), axis=0)])
-    return dq, dk, dv, sums
-
-
-def collect_kernel(sums_qv_ref, sums_ref, sums_in_ref, *refs):
-    out_ref = refs[-1]
-    shards = out_ref.shape[0]
-    qv = jnp.concatenate([sums_qv_ref[0:1, :], sums_qv_ref[1:2, :]], axis=1)
-    rows = [sums_ref[j : j + 1, :] for j in range(6)]
-    found = []
-    for v in (qv, rows[5], rows[3], rows[4], sums_in_ref[0:1, :], rows[2], rows[0], rows[1]):
-        found.extend(gather_vector(v, shards))
-    out_ref[...] = jnp.zeros(out_ref.shape, bf16)
-    for j, v in enumerate(found):
-        out_ref[:, j : j + 1, :LANES] = v.astype(bf16).reshape(shards, 1, LANES)
-
-
-def collect(buffer, sums_qv, sums, sums_in, shards):
-    rows = buffer.shape[1]
-    width = buffer.shape[2]
-    whole = [pl.BlockSpec(v.shape, lambda i: (0, 0)) for v in (sums_qv, sums, sums_in)]
-    return pl.pallas_call(
-        collect_kernel,
-        grid=(1,),
-        in_specs=whole + [pl.BlockSpec(memory_space=pl.ANY)],
-        out_specs=pl.BlockSpec((shards, 16, width), lambda i: (0, rows // 16 - 1, 0)),
-        out_shape=shape_of(buffer.shape, bf16),
-        input_output_aliases={3: 0},
-        compiler_params=pltpu.CompilerParams(vmem_limit_bytes=VMEM_LIMIT),
-        name="collect",
-    )(sums_qv, sums, sums_in, buffer)
+    return jnp.concatenate([dq, dk, dv], axis=1), jnp.pad(sums, ((0, 6), (0, 0)))
 
 
 def swapped(values):
     return lax.ppermute(values, "seq", [(0, 1), (1, 0)])
 
 
-def halves_of_rows(values, seq_index):
-    mine = values.shape[0] // 2
-    return (
-        lax.dynamic_slice_in_dim(values, seq_index * mine, mine, 0),
-        swapped(lax.dynamic_slice_in_dim(values, (1 - seq_index) * mine, mine, 0)),
-    )
-
-
-def rows_of_halves(values, seq_index):
-    half = values.shape[1] // 2
-    kept = lax.dynamic_slice_in_dim(values, seq_index * half, half, 1)
-    came = swapped(lax.dynamic_slice_in_dim(values, (1 - seq_index) * half, half, 1))
-    first = seq_index == 0
-    return jnp.concatenate([jnp.where(first, kept, came), jnp.where(first, came, kept)], axis=0)
+def other_half(values, seq_index):
+    rows = values.shape[0] // 2
+    return swapped(lax.dynamic_slice_in_dim(values, (1 - seq_index) * rows, rows, 0))
+
+
+def placed(values, came, seq_index, row=0):
+    at = (1 - seq_index) * (values.shape[0] // 2) + row
+    return lax.dynamic_update_slice_in_dim(values, came, at, 0)
 
 
 def coordinates(count):
@@ -831,18 +952,43 @@
     return lax.ppermute(values, axis, perm)
 
 
-def scatter_sum(values, axis):
-    index = lax.axis_index(axis)
-    rest = values
-    for size, stride in coordinates(lax.axis_size(axis)):
-        blocks = rest.reshape((-1, size) + values.shape[1:])
-        here = (index // stride) % size
-        total = lax.dynamic_index_in_dim(blocks, here, 1, False).astype(f32)
-        for step in range(1, size):
-            piece = lax.dynamic_index_in_dim(blocks, (here + step) % size, 1, False)
-            total = total + turned(piece, axis, size, stride, step).astype(f32)
-        rest = total.astype(values.dtype)
-    return rest[0]
+class StagedSum:
+    def __init__(self, keep, send, axis):
+        self.axis = axis
+        self.sizes = coordinates(lax.axis_size(axis))
+        self.index = lax.axis_index(axis)
+        self.own = keep
+        size, stride = self.sizes[0]
+        self.came = [turned(send, axis, size, stride, 1)]
+
+    def sum(self, pick):
+        total = pick(self.own).astype(f32)
+        for values in self.came:
+            total = total + pick(values).astype(f32)
+        return total.astype(bf16)
+
+    def step(self, at):
+        size, stride = self.sizes[at]
+        here = (self.index // stride) % size
+
+        def part(step):
+            def pick(values):
+                blocks = values.reshape((-1, size) + values.shape[1:])
+                return lax.dynamic_index_in_dim(blocks, (here + step) % size, 1, False)
+
+            return self.sum(pick)
+
+        came = [
+            turned(part(step), self.axis, size, stride, step) for step in range(1, size)
+        ]
+        self.own, self.came = part(0), came
+
+    def result(self):
+        return self.sum(lambda values: values[0])
+
+
+def tied(*values):
+    return lax.optimization_barrier(values)
 
 
 def gather_pieces(values, axis):
@@ -895,6 +1041,7 @@
     first, others = lower(weight_qkv, weight_in, weight_ffo, weight_out, small)
     if by_rows:
         first = gather_pieces(first, "dp")
+        backs = [back for _, back in first]
     else:
         first = [(lax.all_gather(first, "dp", axis=0, tiled=True), None)]
     others = lax.all_gather(others[None], "dp", axis=0, tiled=True)
@@ -917,92 +1064,98 @@
         mine = rows // 2
         bounds = lax.dynamic_slice_in_dim(bounds, seq_index * mine, mine, 0)
         side = jnp.stack([seq_index, lax.axis_index("dp")]).astype(jnp.int32)
-        x_halves = halves_of_rows(tokens, seq_index)
-        cot_halves = halves_of_rows(cotangent, seq_index)
+        x_other = other_half(tokens, seq_index)
+        first, x_other, held_cot = tied([w for w, _ in first], x_other, cotangent)
+        x_halves = tokens, x_other
+        first = list(zip(first, backs))
+        cot_halves = cotangent, other_half(held_cot, seq_index)
     else:
+        mine = 1
         side = jnp.zeros((2,), jnp.int32)
         x_halves = tokens.reshape(2, 1, -1, width)
         cot_halves = cotangent.reshape(2, 1, -1, width)
+    half = x_halves[1].shape[1]
 
     x, qkv, qkvT, w_qkv, vec, in_bias = project(side, *x_halves, first, inner, BLOCK)
     if by_rows:
-        attn, attnT, log = attend_rows(bounds, qkv, qkvT, BLOCK)
+        attnT, log = attend_rows(bounds, qkv, qkvT, BLOCK)
     else:
         attn, saved = attend_gathered(bounds, qkv, rows, seq_index)
-    out, act, gp, gs, low, gr1, gb, do, doT, sums, sums_in = dense(
-        side, attn, x, *cot_halves, weights, vec, in_bias, BLOCK
+        attnT = attn.T
+    out, out_other, act, gp, gs, low, gr1, gb, do, doT, sums, sums_in = dense(
+        side, attnT, x, *cot_halves, weights, vec, in_bias, BLOCK
     )
+    out = out.reshape(-1, half, width)
+    out_other = out_other.reshape(-1, half, width)
+    part = chunks * shard
     if by_rows:
-        out = rows_of_halves(out.reshape(mine, -1, width), seq_index)
-    else:
-        out = out.reshape(rows, tok_seq, width)
-
-    per_shard = (2 * chunks + 1) * shard
-    if shard % 16 == 0:
-        grads = product_into(
-            None, (shards, per_shard, width), low, gp,
-            (shards, shard, width), lambda i: (0, i, 0), False, chunks,
+        core_split = functools.partial(product, side, split=True)
+        out_other = swapped(out_other)
+        g_in = core_split(
+            (shards, part + shard, width), low, gp, (shards, shard, width), lambda i: (0, i, 0),
+            False, chunks, (attnT, gb),
         )
-        grads = product_into(
-            grads, grads.shape, act, gs,
-            (shards // chunks, chunks * shard, width), lambda i: (i, 1, 0), True, chunks,
-        )
-        grads = product_into(
-            grads, grads.shape, attn, gb,
-            (shards, shard, width), lambda i: (0, 2 * chunks, 0), False, 1,
+        *g_in, act = tied(*g_in, act)
+        in_sum = StagedSum(*g_in, "dp")
+        g_ffo = product(
+            side, (shards, part, width), act, gs, (shards // chunks, part, width),
+            lambda i: (i, 0, 0), True, chunks,
         )
     else:
+        out = jnp.concatenate([out, out_other], axis=1).reshape(rows, tok_seq, width)
+        g_ffo = dot_tn(act, gs).astype(bf16).reshape(shards, part, width)
         g_in = dot_tn(low, gp).astype(bf16).reshape(shards, shard, chunks, width)
-        g_in = g_in.transpose(0, 2, 1, 3).reshape(shards, chunks * shard, width)
-        g_ffo = dot_tn(act, gs).astype(bf16).reshape(shards, chunks * shard, width)
+        g_in = g_in.transpose(0, 2, 1, 3).reshape(shards, part, width)
         g_out = dot_tn(attn, gb).astype(bf16).reshape(shards, shard, width)
-        grads = jnp.concatenate([g_in, g_ffo, g_out], axis=1)
-    grads, do = lax.optimization_barrier((grads, do))
-    reduced = lax.psum_scatter(grads, "dp", scatter_dimension=0, tiled=True)[0]
-
+        g_in = jnp.concatenate([g_in, g_out], axis=1)
+        g_in = lax.psum_scatter(g_in, "dp", scatter_dimension=0, tiled=True)[0]
     if by_rows:
-        dq, dk, dv, sums_qv = attend_rows_back(bounds, qkv, qkvT, do, doT, attnT, log, BLOCK)
+        g_ffo, do, in_sum.came = tied(g_ffo, do, in_sum.came)
+    g_ffo = lax.psum_scatter(g_ffo, "dp", scatter_dimension=0, tiled=True)[0]
+
+    if by_rows:
+        in_sum.step(1)
+        g_x, sums_qv = attend_rows_back(bounds, qkv, qkvT, do, doT, attnT, log, 0, 1, BLOCK)
+        g_x, out_other, in_sum.came = tied(g_x, out_other, in_sum.came)
+        in_sum.step(2)
+        g_qkv = last_product(side, x, g_x, (sums, sums_in, sums_qv), shards)
+        g_qkv, gr1 = tied(g_qkv, gr1)
+        grad_x, grad_other = input_grad(side, g_x, gr1, w_qkv, *x_halves, BLOCK)
+        grad_other, g_qkv, in_sum.came = tied(grad_other, g_qkv, in_sum.came)
+        qkv_sum = StagedSum(*g_qkv, "dp")
+        qkv_sum.step(1)
+        grad_other = [swapped(grad_other[r : r + 1]) for r in range(mine)]
+        qkv_sum.came, grad_other[0] = tied(qkv_sum.came, grad_other[0])
+        qkv_sum.step(2)
+        g_in = in_sum.result()
+        both = swapped(jnp.concatenate([g_in, g_ffo], axis=0))
+        qkv_sum.came, both, grad_other = tied(qkv_sum.came, both, grad_other)
+        g_qkv = qkv_sum.result()
+        for r in range(mine):
+            grad_x = placed(grad_x, grad_other[r], seq_index, r)
+        out = placed(out, out_other, seq_index)
+        g_in = g_in.astype(f32) + both[: part + shard].astype(f32)
+        d_ffo = g_ffo.astype(f32) + both[part + shard :].astype(f32)
+        g_qkv = g_qkv.astype(f32) + swapped(g_qkv).astype(f32)
     else:
-        dq, dk, dv, sums_qv = attend_gathered_back(saved, attn, do)
-
-    if by_rows:
-        g_qkv = []
-        for g in (dq, dk, dv):
-            extra = 16 if g is dv else 0
-            g_qkv.append(
-                product_into(
-                    None, (shards, shard + extra, width), x, g,
-                    (shards, shard, width), lambda i: (0, 0, 0), False, 1,
-                )
-            )
-        g_qkv[2] = collect(g_qkv[2], sums_qv, sums, sums_in, shards)
-        g_qkv = [scatter_sum(g, "dp") for g in g_qkv]
-    else:
-        vectors = jnp.zeros((shards, 16, width), bf16)
-        vectors = collect(vectors, sums_qv, sums, sums_in, shards)
-        g_qkv = [dot_tn(x, g).astype(bf16).reshape(shards, shard, width) for g in (dq, dk, dv)]
-        g_qkv[2] = jnp.concatenate([g_qkv[2], vectors], axis=1)
-        g_qkv = [lax.psum_scatter(g, "dp", scatter_dimension=0, tiled=True)[0] for g in g_qkv]
-
-    grad_x = input_grad(dq, dk, dv, gr1, w_qkv, BLOCK)
-    if by_rows:
-        grad_x = rows_of_halves(grad_x.reshape(mine, -1, width), seq_index)
-    else:
-        grad_x = grad_x.reshape(rows, tok_seq, width)
-
-    def over_seq(values):
-        if seq_count == 2:
-            return values.astype(f32) + swapped(values).astype(f32)
-        return lax.psum(values, "seq").astype(f32)
-
-    reduced = over_seq(reduced)
-    g_qkv = [over_seq(g) for g in g_qkv]
-    vectors = g_qkv[2][shard:, :LANES]
-    d_qkv = jnp.concatenate([g[:shard] for g in g_qkv], axis=1)
-    d_in = reduced[: chunks * shard].reshape(chunks, shard, width).transpose(1, 0, 2)
-    d_in = d_in.reshape(shard, inner)
-    d_ffo = reduced[chunks * shard : 2 * chunks * shard]
-    d_out = reduced[2 * chunks * shard :]
+        g_x, sums_qv = attend_gathered_back(saved, attn, do)
+        vectors = []
+        for v in (sums_qv[:2].reshape(-1), sums[5], sums[3], sums[4], sums_in[0], sums[2], sums[0], sums[1]):
+            v = v.reshape(shards, -1)
+            vectors.append(jnp.pad(v, ((0, 0), (0, -v.shape[1] % LANES))).reshape(shards, -1, LANES))
+        vectors = jnp.concatenate(vectors, axis=1).astype(bf16)
+        vectors = jnp.pad(vectors, ((0, 0), (0, 16 - vectors.shape[1]), (0, width - LANES)))
+        g_qkv = dot_tn(x, g_x).astype(bf16).reshape(shards, shard, 3, width)
+        g_qkv = g_qkv.transpose(0, 2, 1, 3).reshape(shards, 3 * shard, width)
+        g_qkv = jnp.concatenate([g_qkv, vectors], axis=1)
+        g_qkv = lax.psum_scatter(g_qkv, "dp", scatter_dimension=0, tiled=True)[0]
+        grad_x, grad_other = input_grad(side, g_x, gr1, w_qkv, *x_halves, BLOCK)
+        grad_x = jnp.concatenate([grad_x, grad_other], axis=1).reshape(rows, tok_seq, width)
+        d_ffo, g_in, g_qkv = [lax.psum(v, "seq").astype(f32) for v in (g_ffo, g_in, g_qkv)]
+    vectors = g_qkv[3 * shard :, :LANES]
+    d_qkv = jnp.concatenate([g_qkv[j * shard : (j + 1) * shard] for j in range(3)], axis=1)
+    d_out = g_in[part:]
+    d_in = jnp.concatenate([g_in[c * shard : (c + 1) * shard] for c in range(chunks)], axis=1)
     sizes = [v.shape[0] for v in small]
     d_small = []
     for row, size in zip(vector_rows(sizes)[0], sizes):

time: 431 us -> 412 us (0.956)
  starting transfers between devices: 38.7 us -> 31 us
  other arithmetic: 12.5 us -> 18 us
  waiting for transfers between devices: 109 us -> 104 us
    ppermute x8 -> x7, waiting for transfers between devices: 33.5 us -> 23.5 us  [swapped(): return lax.ppermute(values, 'seq', [(0, 1), (1, 0)])]
    convert_element_type x5 -> x4, other arithmetic: 3.2 us -> 10.9 us  [sum(): return total.astype(bf16)]
    dynamic_update_slice x0 -> x3, local copies, waits for them, and re-layouts: none -> 6.77 us  [placed(): return lax.dynamic_update_slice_in_dim(values, came, at, 0)]
    pallas_call x8 -> x4, Pallas kernels: 73.2 us -> 66.8 us  [the longest x2 36.1 us: product(): pl.pallas_call(functools.partial(product_kernel, more=bool(more), split=s...]
    ppermute x8 -> x7, starting transfers between devices: 13.9 us -> 7.64 us  [swapped(): return lax.ppermute(values, 'seq', [(0, 1), (1, 0)])]
    squeeze x9 -> x0, local copies, waits for them, and re-layouts: 6.14 us -> none  [scatter_sum(): piece = lax.dynamic_index_in_dim(blocks, (here + step) % size, 1, False)]
    dynamic_slice x4 -> x2, local copies, waits for them, and re-layouts: 8.8 us -> 2.79 us  [other_half(): lax.dynamic_slice_in_dim(values, (1 - seq_index) * rows, rows, 0)]
    ppermute x30 -> x25, waiting for transfers between devices: 75.3 us -> 80 us  [turned(): return lax.ppermute(values, axis, perm)]
  transfers between devices with their start and end apart: 40 -> 34, of which waited for: 15 -> 19; matrix products, arithmetic and copies ran while one was open for 7% -> 7% of each run, Pallas kernels for 28% -> 31%
where the time goes in v3:
time: 412 us; the launch traced here: 406 us
  Pallas kernels  222 us (54%)
  waiting for transfers between devices  104 us (25%)
  starting transfers between devices  31 us (8%)
  other arithmetic  18 us (4%)
  local copies, waits for them, and re-layouts  17.4 us (4%)
  between operations  14.6 us (4%)
    ppermute x25, waiting for transfers between devices, turned(): return lax.ppermute(values, axis, perm)  80 us
    pallas_call x1, Pallas kernels, dense(): pl.pallas_call(dense_kernel, grid_spec=pltpu.PrefetchScalarGridSpec(num_s...  73.1 us
    pallas_call x1, Pallas kernels, attend_rows_back(): pl.pallas_call(attend_back_kernel, grid_spec=pltpu.PrefetchScalarGridSpec...  39.7 us
    pallas_call x2, Pallas kernels, product(): pl.pallas_call(functools.partial(product_kernel, more=bool(more), split=s...  36.1 us
    ppermute x7, waiting for transfers between devices, swapped(): return lax.ppermute(values, 'seq', [(0, 1), (1, 0)])  23.5 us
    ppermute x25, starting transfers between devices, turned(): return lax.ppermute(values, axis, perm)  23.3 us
    pallas_call x1, Pallas kernels, attend_rows(): pl.pallas_call(attend_kernel, grid_spec=pltpu.PrefetchScalarGridSpec(num_...  22 us
    pallas_call x1, Pallas kernels, project(): pl.pallas_call(functools.partial(project_kernel, shards=shards, pieces=[b...  17.6 us
  transfers between devices with their start and end apart: 34, of which 19 were waited for; matrix products, arithmetic and copies ran while one was open for 7% of the time, Pallas kernels for 31%

profile of v3, /device:TPU:12, one launch (start us, length us, event | category | flops | bytes accessed | tf_op | source)
XLA Modules:
  0.0 406.2 jit_solution(10988864782583259229)
XLA Ops:
  7.2 2.6 lower.1
  9.9 1.5 constant_dynamic-slice_fusion.1
  12.0 1.6 collective-permute-start
  14.6 2.0 collective-permute-start.2
  16.7 1.5 collective-permute-start.3
  18.1 12.6 %collective-permute-done.refs_1_ = bf16[48,2432]{1,0:T(8,128)(2,1)S(1)} collective-permute-done((bf16[48,2432]{1,0:T(8,128)(2,1)S(1)}, bf16[48,2432]{1,0:T(8,128)(2,1)S(1)}, u32[]{:S(2)}, u32[]{:S(2)}) %collective-permute-start) | collective-permute-done | bytes 233504 | tf_op jit(solution)/shard_map/ppermute | solution.py:952
  30.7 19.6 %collective-permute-done.1.refs_2_ = bf16[48,2432]{1,0:T(8,128)(2,1)S(1)} collective-permute-done((bf16[48,2432]{1,0:T(8,128)(2,1)S(1)}, bf16[48,2432]{1,0:T(8,128)(2,1)S(1)}, u32[]{:S(2)}, u32[]{:S(2)}) %collective-permute-start.1) | collective-permute-done | bytes 233504 | tf_op jit(solution)/shard_map/ppermute | solution.py:952
  50.3 1.5 collective-permute-start.4
  51.8 2.2 collective-permute-done.2.refs_3_
  54.0 1.5 collective-permute-start.5
  56.6 6.0 %collective-permute-done.5.refs_6_ = bf16[48,2432]{1,0:T(8,128)(2,1)S(1)} collective-permute-done((bf16[48,2432]{1,0:T(8,128)(2,1)S(1)}, bf16[48,2432]{1,0:T(8,128)(2,1)S(1)}, u32[]{:S(2)}, u32[]{:S(2)}) %collective-permute-start.5) | collective-permute-done | bytes 233504 | tf_op jit(solution)/shard_map/ppermute | solution.py:952
  62.6 6.4 %collective-permute-done.6.refs_7_ = bf16[48,2432]{1,0:T(8,128)(2,1)S(1)} collective-permute-done((bf16[48,2432]{1,0:T(8,128)(2,1)S(1)}, bf16[48,2432]{1,0:T(8,128)(2,1)S(1)}, u32[]{:S(2)}, u32[]{:S(2)}) %collective-permute-start.6) | collective-permute-done | bytes 233504 | tf_op jit(solution)/shard_map/ppermute | solution.py:952
  72.5 1.2 constant_dynamic-slice_fusion
  73.7 2.5 collective-permute-start.16
  77.6 17.6 %project.1 = (bf16[2048,768]{1,0:T(8,128)(2,1)}, bf16[2048,2304]{1,0:T(8,128)(2,1)}, bf16[2304,2048]{1,0:T(8,128)(2,1)}, bf16[768,2432]{1,0:T(8,128)(2,1)}, f32[8,768]{1,0:T(8,128)}, /*index=5*/f32[8,3072]{1,0:T(8,128)}) custom-call(s32[2]{0:T(128)} %pad_add_fusion.place_ref.side_ref.refs_0_, bf16[2048,768]{1,0:T(8,128)(2,1)} %bitcast.78, ...), custom_call_target="tpu_custom_call" | custom-call | flops 1811939328 | bytes 8060928 | tf_op jit(solution)/shard_map/project/pallas_call | solution.py:195
  95.2 22.0 %attend.1 = (bf16[768,2048]{1,0:T(8,128)(2,1)}, f32[16,2048]{1,0:T(8,128)}) custom-call(s32[2,8]{1,0:T(2,128)} %constant_dynamic-slice_fusion.2.bounds_ref, bf16[2048,2304]{1,0:T(8,128)(2,1)} %get-tuple-element.106.k_ref.v_ref.q_ref, bf16[2304,2048]{1,0:T(8,128)(2,1)} %get-tuple-element.107.qT_ref.vT_ref.kT_ref, ...), custom_call_target="tpu_custom_call" | custom-call | flops 1610612736 | bytes 3932160 | tf_op jit(solution)/shard_map/attend/pallas_call | solution.py:348
  118.3 73.1 %dense.1 = (bf16[2048,768]{1,0:T(8,128)(2,1)}, bf16[1024,768]{1,0:T(8,128)(2,1)}, bf16[2048,3072]{1,0:T(8,128)(2,1)}, bf16[2048,3072]{1,0:T(8,128)(2,1)}, bf16[2...) custom-call(s32[2]{0:T(128)} %pad_add_fusion.place_ref.side_ref.refs, ...), custom_call_target="tpu_custom_call" | custom-call | flops 10871635968 | bytes 17301504 | tf_op jit(solution)/shard_map/dense/pallas_call | solution.py:657
  191.3 20.9 %product.2 = (bf16[8,240,768]{2,1,0:T(8,128)(2,1)}, bf16[8,240,768]{2,1,0:T(8,128)(2,1)}) custom-call(s32[2]{0:T(128)} %pad_add_fusion.place_ref.side_ref.refs_0_, bf16[2048,768]{1,0:T(8,128)(2,1)} %get-tuple-element.115.refs_1_, bf16[2048,3072]{1,0:T(8,128)(2,1)} %get-tuple-element.116.refs_2_, ...), custom_call_target="tpu_custom_call" | custom-call | flops 2415919104 | bytes 5111808 | tf_op jit(solution)/shard_map/product/pallas_call | solution.py:743
  212.7 15.2 %product.3 = bf16[16,192,768]{2,1,0:T(8,128)(2,1)} custom-call(s32[2]{0:T(128)} %pad_add_fusion.place_ref.side_ref.refs_0_, bf16[2048,3072]{1,0:T(8,128)(2,1)} %get-tuple-element.121.refs_1_, bf16[2048,768]{1,0:T(8,128)(2,1)} %get-tuple-element.122.refs_2_), custom_call_target="tpu_custom_call" | custom-call | flops 2415919104 | bytes 5111808 | tf_op jit(solution)/shard_map/product/pallas_call | solution.py:743
  228.1 1.4 copy-done.1
  229.5 3.4 add_convert_fusion
  232.9 2.5 collective-permute-start.19
  235.3 39.7 %attend_back.1 = (bf16[2048,2304]{1,0:T(8,128)(2,1)}, f32[8,768]{1,0:T(8,128)}) custom-call(s32[2,8]{1,0:T(2,128)} %constant_dynamic-slice_fusion.2.bounds_ref, bf16[2048,2304]{1,0:T(8,128)(2,1)} %get-tuple-element.106.k_ref.v_ref.q_ref, bf16[2304,2048]{1,0:T(8,128)(2,1)} %get-tuple-element.107.qT_ref.vT_ref.kT_ref, ...), custom_call_target="tpu_custom_call" | custom-call | flops 4026531840 | bytes 8650752 | tf_op jit(solution)/shard_map/attend_back/pallas_call | solution.py:472
  275.0 2.1 collective-permute-done.19
  277.1 2.2 fusion.3
  279.3 2.0 collective-permute-start.22
  281.3 15.4 %last_product.1 = (bf16[8,160,768]{2,1,0:T(8,128)(2,1)}, bf16[8,160,768]{2,1,0:T(8,128)(2,1)}) custom-call(s32[2]{0:T(128)} %pad_add_fusion.place_ref.side_ref.refs_0_, bf16[2048,768]{1,0:T(8,128)(2,1)} %get-tuple-element.109.x_ref.a_ref, bf16[2048,2304]{1,0:T(8,128)(2,1)} %get-tuple-element.133.b_ref.g_ref, f32[8,768]{1,0:T(8,128)} %get-tuple-element.134.refs_0_, ...), custom_call_target="tpu_custom_call" | custom-call | flops 1811939328 | bytes 4030464 | tf_op jit(solution)/shard_map/last_product/pallas_call | solution.py:852
  296.7 15.3 %input_grad.1 = (bf16[2048,768]{1,0:T(8,128)(2,1)}, bf16[1024,768]{1,0:T(8,128)(2,1)}) custom-call(s32[2]{0:T(128)} %pad_add_fusion.place_ref.side_ref.refs_0_, bf16[2048,2304]{1,0:T(8,128)(2,1)} %get-tuple-element.133.b_ref.g_ref, f32[2048,768]{1,0:T(8,128)} %get-tuple-element.140.gr1_ref, bf16[768,2432]{1,0:T(8,128)(2,1)} %get-tuple-element.141.w_ref), custom_call_target="tpu_custom_call" | custom-call | flops 1811939328 | bytes 5603328 | tf_op jit(solution)/shard_map/input_grad/pallas_call | solution.py:789
  312.0 14.4 %collective-permute-done.21 = bf16[1,240,768]{2,1,0:T(8,128)(2,1)S(1)} collective-permute-done((bf16[1,240,768]{2,1,0:T(8,128)(2,1)S(1)}, bf16[1,240,768]{2,1,0:T(8,128)(2,1)S(1)}, u32[]{:S(2)}, u32[]{:S(2)}) %collective-permute-start.21) | collective-permute-done | bytes 368672 | tf_op jit(solution)/shard_map/ppermute | solution.py:952
  326.5 4.2 %collective-permute-done.23 = bf16[8,160,768]{2,1,0:T(8,128)(2,1)S(1)} collective-permute-done((bf16[8,160,768]{2,1,0:T(8,128)(2,1)}, bf16[8,160,768]{2,1,0:T(8,128)(2,1)S(1)}, u32[]{:S(2)}, u32[]{:S(2)}) %collective-permute-start.23) | collective-permute-done | bytes 1966112 | tf_op jit(solution)/shard_map/ppermute | solution.py:952
  330.6 3.1 add_convert_fusion.3
  333.8 1.9 collective-permute-start.24
  335.7 1.3 fusion.12
  339.0 1.5 fusion.10
  341.5 1.2 collective-permute-start.29
  342.7 15.0 %collective-permute-done.25 = bf16[1,512,768]{2,1,0:T(8,128)(2,1)} collective-permute-done((bf16[1,512,768]{2,1,0:T(8,128)(2,1)}, bf16[1,512,768]{2,1,0:T(8,128)(2,1)}, u32[]{:S(2)}, u32[]{:S(2)}) %collective-permute-start.25) | collective-permute-done | bytes 786464 | tf_op jit(solution)/shard_map/ppermute | solution.py:930
  358.0 2.1 fusion.7
  360.1 3.4 collective-permute-start.27
  363.6 2.0 collective-permute-start.28
  365.6 2.7 constant_dynamic-update-slice_fusion.2
  368.3 6.3 %collective-permute-done.30 = bf16[1,512,768]{2,1,0:T(8,128)(2,1)} collective-permute-done((bf16[1,512,768]{2,1,0:T(8,128)(2,1)}, bf16[1,512,768]{2,1,0:T(8,128)(2,1)}, u32[]{:S(2)}, u32[]{:S(2)}) %collective-permute-start.30) | collective-permute-done | bytes 786464 | tf_op jit(solution)/shard_map/ppermute | solution.py:930
  374.6 6.8 %collective-permute-done.27 = bf16[1,160,768]{2,1,0:T(8,128)(2,1)S(1)} collective-permute-done((bf16[1,160,768]{2,1,0:T(8,128)(2,1)}, bf16[1,160,768]{2,1,0:T(8,128)(2,1)S(1)}, u32[]{:S(2)}, u32[]{:S(2)}) %collective-permute-start.27) | collective-permute-done | bytes 245792 | tf_op jit(solution)/shard_map/ppermute | solution.py:952
  381.4 3.9 collective-permute-done.28
  385.3 2.2 collective-permute-done.29
  387.5 1.2 fusion.11
  388.8 1.2 collective-permute-start.31
  390.8 2.1 constant_dynamic-update-slice_fusion.1
  392.9 2.1 constant_dynamic-update-slice_fusion
  (105 shorter events, 17.8 us)
Async XLA Ops:
  7.2 65.3 %copy-start = (bf16[4,512,768]{2,1,0:T(8,128)(2,1)S(1)}, bf16[4,512,768]{2,1,0:T(8,128)(2,1)}, u32[]{:S(2)}) copy-start(bf16[4,512,768]{2,1,0:T(8,128)(2,1)} %param.29) | copy-start | bytes 9437188
  7.2 110.0 %all-gather.3.cloned.1.call-start = ((), (), s32[]{:S(2)}) async-start(), calls=%async_computation.2 | async-start | bytes 11280384 | tf_op jit(solution)/shard_map/all_gather | solution.py:1047
  9.8 330.6 %reduce-scatter.2.cloned.1.call-start = ((), (), s32[]{:S(2)}) async-start(), calls=%async_computation.1 | async-start | bytes 5013504 | tf_op jit(solution)/shard_map/reduce_scatter | solution.py:1114
  9.9 66.3 %copy-start.23 = (s32[4,8]{1,0:T(4,128)S(1)}, s32[4,8]{1,0:T(4,128)}, u32[]{:S(2)}) copy-start(s32[4,8]{1,0:T(4,128)} %param.28) | copy-start | bytes 388
  11.5 61.0 %collective-permute-start.15 = (bf16[2,512,768]{2,1,0:T(8,128)(2,1)S(1)}, bf16[2,512,768]{2,1,0:T(8,128)(2,1)}, u32[]{:S(2)}, u32[]{:S(2)}) collective-permute-start(bf16[2,512,768]{2,1,0:T(8,128)(2,1)S(1)} %constant_dynamic-slice_fusion.1), channel_id=1, source_target_pairs={{0,1},{1,0},{2,3},{3,2},{4,5},{5,4},{6,7},{7,6},{8,9},{9,8},{10,11... | collective-permute-start | bytes 4718600 | tf_op jit(solution)/shard_map/ppermute | solution.py:930
  12.0 18.7 %collective-permute-start = (bf16[48,2432]{1,0:T(8,128)(2,1)S(1)}, bf16[48,2432]{1,0:T(8,128)(2,1)S(1)}, u32[]{:S(2)}, u32[]{:S(2)}) collective-permute-start(bf16[48,2432]{1,0:T(8,128)(2,1)S(1)} %copy-done.7), channel_id=1, source_target_pairs={{0,8},{2,10},{4,12},{6,14},{8,16},{10,18},{12,20},{14,22},{16,24},... | collective-permute-start | bytes 700424 | tf_op jit(solution)/shard_map/ppermute | solution.py:952
  13.6 36.7 %collective-permute-start.1 = (bf16[48,2432]{1,0:T(8,128)(2,1)S(1)}, bf16[48,2432]{1,0:T(8,128)(2,1)S(1)}, u32[]{:S(2)}, u32[]{:S(2)}) collective-permute-start(bf16[48,2432]{1,0:T(8,128)(2,1)S(1)} %copy-done.7), channel_id=1, source_target_pairs={{0,16},{2,18},{4,20},{6,22},{8,24},{10,26},{12,28},{14,30},{16,0},... | collective-permute-start | bytes 700424 | tf_op jit(solution)/shard_map/ppermute | solution.py:952
  14.6 39.4 %collective-permute-start.2 = (bf16[48,2432]{1,0:T(8,128)(2,1)S(1)}, bf16[48,2432]{1,0:T(8,128)(2,1)S(1)}, u32[]{:S(2)}, u32[]{:S(2)}) collective-permute-start(bf16[48,2432]{1,0:T(8,128)(2,1)S(1)} %copy-done.7), channel_id=1, source_target_pairs={{0,24},{2,26},{4,28},{6,30},{8,0},{10,2},{12,4},{14,6},{16,8},{18,... | collective-permute-start | bytes 700424 | tf_op jit(solution)/shard_map/ppermute | solution.py:952
  16.7 38.8 %collective-permute-start.3 = (bf16[48,2432]{1,0:T(8,128)(2,1)S(1)}, bf16[48,2432]{1,0:T(8,128)(2,1)S(1)}, u32[]{:S(2)}, u32[]{:S(2)}) collective-permute-start(bf16[48,2432]{1,0:T(8,128)(2,1)S(1)} %copy-done.7), channel_id=1, source_target_pairs={{0,4},{2,6},{4,0},{6,2},{8,12},{10,14},{12,8},{14,10},{16,20},{18,... | collective-permute-start | bytes 700424 | tf_op jit(solution)/shard_map/ppermute | solution.py:952
  30.7 25.3 %copy-start.8 = (bf16[48,2432]{1,0:T(8,128)(2,1)}, bf16[48,2432]{1,0:T(8,128)(2,1)S(1)}, u32[]{:S(2)}) copy-start(bf16[48,2432]{1,0:T(8,128)(2,1)S(1)} %collective-permute-done.refs_1_) | copy-start | bytes 700420
  30.7 25.3 %collective-permute-start.7 = (bf16[48,2432]{1,0:T(8,128)(2,1)S(1)}, bf16[48,2432]{1,0:T(8,128)(2,1)S(1)}, u32[]{:S(2)}, u32[]{:S(2)}) collective-permute-start(bf16[48,2432]{1,0:T(8,128)(2,1)S(1)} %copy-done.7), channel_id=1, source_target_pairs={{0,2},{2,0},{4,6},{6,4},{8,10},{10,8},{12,14},{14,12},{16,18},{18,... | collective-permute-start | bytes 700424 | tf_op jit(solution)/shard_map/ppermute | solution.py:952
  50.3 18.6 %copy-start.9 = (bf16[48,2432]{1,0:T(8,128)(2,1)}, bf16[48,2432]{1,0:T(8,128)(2,1)S(1)}, u32[]{:S(2)}) copy-start(bf16[48,2432]{1,0:T(8,128)(2,1)S(1)} %collective-permute-done.1.refs_2_) | copy-start | bytes 700420
  50.3 6.1 %collective-permute-start.4 = (bf16[48,2432]{1,0:T(8,128)(2,1)S(1)}, bf16[48,2432]{1,0:T(8,128)(2,1)S(1)}, u32[]{:S(2)}, u32[]{:S(2)}) collective-permute-start(bf16[48,2432]{1,0:T(8,128)(2,1)S(1)} %collective-permute-done.refs_1_), channel_id=1, source_target_pairs={{0,4},{2,6},{4,0},{6,2},{8,12},{10,14},{12,8},{14,10},{16,20},{18,... | collective-permute-start | bytes 700424 | tf_op jit(solution)/shard_map/ppermute | solution.py:952
  54.0 15.5 %copy-start.10 = (bf16[48,2432]{1,0:T(8,128)(2,1)}, bf16[48,2432]{1,0:T(8,128)(2,1)S(1)}, u32[]{:S(2)}) copy-start(bf16[48,2432]{1,0:T(8,128)(2,1)S(1)} %collective-permute-done.2.refs_3_) | copy-start | bytes 700420
  54.0 8.6 %collective-permute-start.5 = (bf16[48,2432]{1,0:T(8,128)(2,1)S(1)}, bf16[48,2432]{1,0:T(8,128)(2,1)S(1)}, u32[]{:S(2)}, u32[]{:S(2)}) collective-permute-start(bf16[48,2432]{1,0:T(8,128)(2,1)S(1)} %collective-permute-done.1.refs_2_), channel_id=1, source_target_pairs={{0,4},{2,6},{4,0},{6,2},{8,12},{10,14},{12,8},{14,10},{16,20},{18,... | collective-permute-start | bytes 700424 | tf_op jit(solution)/shard_map/ppermute | solution.py:952
  55.5 14.1 %copy-start.11 = (bf16[48,2432]{1,0:T(8,128)(2,1)}, bf16[48,2432]{1,0:T(8,128)(2,1)S(1)}, u32[]{:S(2)}) copy-start(bf16[48,2432]{1,0:T(8,128)(2,1)S(1)} %collective-permute-done.3.refs_4_) | copy-start | bytes 700420
  55.5 13.4 %collective-permute-start.6 = (bf16[48,2432]{1,0:T(8,128)(2,1)S(1)}, bf16[48,2432]{1,0:T(8,128)(2,1)S(1)}, u32[]{:S(2)}, u32[]{:S(2)}) collective-permute-start(bf16[48,2432]{1,0:T(8,128)(2,1)S(1)} %collective-permute-done.2.refs_3_), channel_id=1, source_target_pairs={{0,4},{2,6},{4,0},{6,2},{8,12},{10,14},{12,8},{14,10},{16,20},{18,... | collective-permute-start | bytes 700424 | tf_op jit(solution)/shard_map/ppermute | solution.py:952
  56.0 14.4 %copy-start.12 = (bf16[48,2432]{1,0:T(8,128)(2,1)}, bf16[48,2432]{1,0:T(8,128)(2,1)S(1)}, u32[]{:S(2)}) copy-start(bf16[48,2432]{1,0:T(8,128)(2,1)S(1)} %collective-permute-done.7.refs_8_) | copy-start | bytes 700420
  56.0 12.9 %collective-permute-start.8 = (bf16[48,2432]{1,0:T(8,128)(2,1)S(1)}, bf16[48,2432]{1,0:T(8,128)(2,1)S(1)}, u32[]{:S(2)}, u32[]{:S(2)}) collective-permute-start(bf16[48,2432]{1,0:T(8,128)(2,1)S(1)} %collective-permute-done.refs_1_), channel_id=1, source_target_pairs={{0,2},{2,0},{4,6},{6,4},{8,10},{10,8},{12,14},{14,12},{16,18},{18,... | collective-permute-start | bytes 700424 | tf_op jit(solution)/shard_map/ppermute | solution.py:952
  56.4 14.4 %copy-start.13 = (bf16[48,2432]{1,0:T(8,128)(2,1)}, bf16[48,2432]{1,0:T(8,128)(2,1)S(1)}, u32[]{:S(2)}) copy-start(bf16[48,2432]{1,0:T(8,128)(2,1)S(1)} %collective-permute-done.4.refs_5_) | copy-start | bytes 700420
  56.4 13.1 %collective-permute-start.9 = (bf16[48,2432]{1,0:T(8,128)(2,1)S(1)}, bf16[48,2432]{1,0:T(8,128)(2,1)S(1)}, u32[]{:S(2)}, u32[]{:S(2)}) collective-permute-start(bf16[48,2432]{1,0:T(8,128)(2,1)S(1)} %collective-permute-done.1.refs_2_), channel_id=1, source_target_pairs={{0,2},{2,0},{4,6},{6,4},{8,10},{10,8},{12,14},{14,12},{16,18},{18,... | collective-permute-start | bytes 700424 | tf_op jit(solution)/shard_map/ppermute | solution.py:952
  62.6 8.5 %copy-start.14 = (bf16[48,2432]{1,0:T(8,128)(2,1)}, bf16[48,2432]{1,0:T(8,128)(2,1)S(1)}, u32[]{:S(2)}) copy-start(bf16[48,2432]{1,0:T(8,128)(2,1)S(1)} %collective-permute-done.5.refs_6_) | copy-start | bytes 700420
  62.6 7.1 %collective-permute-start.10 = (bf16[48,2432]{1,0:T(8,128)(2,1)S(1)}, bf16[48,2432]{1,0:T(8,128)(2,1)S(1)}, u32[]{:S(2)}, u32[]{:S(2)}) collective-permute-start(bf16[48,2432]{1,0:T(8,128)(2,1)S(1)} %collective-permute-done.2.refs_3_), channel_id=1, source_target_pairs={{0,2},{2,0},{4,6},{6,4},{8,10},{10,8},{12,14},{14,12},{16,18},{18,... | collective-permute-start | bytes 700424 | tf_op jit(solution)/shard_map/ppermute | solution.py:952
  68.9 1.5 collective-permute-start.11
  68.9 8.6 %copy-start.16 = (bf16[48,2432]{1,0:T(8,128)(2,1)}, bf16[48,2432]{1,0:T(8,128)(2,1)S(1)}, u32[]{:S(2)}) copy-start(bf16[48,2432]{1,0:T(8,128)(2,1)S(1)} %collective-permute-done.8.refs_9_) | copy-start | bytes 700420
  69.0 1.8 collective-permute-start.12
  69.5 1.6 collective-permute-start.13
  69.6 1.8 collective-permute-start.14
  73.7 43.4 %collective-permute-start.16 = (bf16[2,512,768]{2,1,0:T(8,128)(2,1)}, bf16[2,512,768]{2,1,0:T(8,128)(2,1)S(1)}, u32[]{:S(2)}, u32[]{:S(2)}) collective-permute-start(bf16[2,512,768]{2,1,0:T(8,128)(2,1)} %constant_dynamic-slice_fusion), channel_id=1, source_target_pairs={{0,1},{1,0},{2,3},{3,2},{4,5},{5,4},{6,7},{7,6},{8,9},{9,8},{10,11... | collective-permute-start | bytes 4718600 | tf_op jit(solution)/shard_map/ppermute | solution.py:930
  212.3 15.6 %collective-permute-start.17 = (bf16[8,240,768]{2,1,0:T(8,128)(2,1)}, bf16[8,240,768]{2,1,0:T(8,128)(2,1)S(1)}, u32[]{:S(2)}, u32[]{:S(2)}) collective-permute-start(bf16[8,240,768]{2,1,0:T(8,128)(2,1)} %get-tuple-element.124), channel_id=1, source_target_pairs={{0,2},{2,0},{4,6},{6,4},{8,10},{10,8},{12,14},{14,12},{16,18},{18,... | collective-permute-start | bytes 8847368 | tf_op jit(solution)/shard_map/ppermute | solution.py:952
  228.0 47.1 %collective-permute-start.18 = (bf16[2,512,768]{2,1,0:T(8,128)(2,1)}, bf16[2,512,768]{2,1,0:T(8,128)(2,1)}, u32[]{:S(2)}, u32[]{:S(2)}) collective-permute-start(bf16[2,512,768]{2,1,0:T(8,128)(2,1)} %bitcast.97), channel_id=1, source_target_pairs={{0,1},{1,0},{2,3},{3,2},{4,5},{5,4},{6,7},{7,6},{8,9},{9,8},{10,11... | collective-permute-start | bytes 4718600 | tf_op jit(solution)/shard_map/ppermute | solution.py:930
  232.9 44.2 %collective-permute-start.19 = (bf16[4,240,768]{2,1,0:T(8,128)(2,1)S(1)}, bf16[4,240,768]{2,1,0:T(8,128)(2,1)}, u32[]{:S(2)}, u32[]{:S(2)}) collective-permute-start(bf16[4,240,768]{2,1,0:T(8,128)(2,1)S(1)} %get-tuple-element.163), channel_id=1, source_target_pairs={{0,4},{2,6},{4,0},{6,2},{8,12},{10,14},{12,8},{14,10},{16,20},{18,... | collective-permute-start | bytes 4423688 | tf_op jit(solution)/shard_map/ppermute | solution.py:952
  279.3 32.7 %collective-permute-start.20 = (bf16[1,240,768]{2,1,0:T(8,128)(2,1)}, bf16[1,240,768]{2,1,0:T(8,128)(2,1)S(1)}, u32[]{:S(2)}, u32[]{:S(2)}) collective-permute-start(bf16[1,240,768]{2,1,0:T(8,128)(2,1)} %get-tuple-element.168), channel_id=1, source_target_pairs={{0,8},{2,10},{4,12},{6,14},{8,16},{10,18},{12,20},{14,22},{16,24},... | collective-permute-start | bytes 1105928 | tf_op jit(solution)/shard_map/ppermute | solution.py:952
  279.3 47.1 %collective-permute-start.21 = (bf16[1,240,768]{2,1,0:T(8,128)(2,1)S(1)}, bf16[1,240,768]{2,1,0:T(8,128)(2,1)S(1)}, u32[]{:S(2)}, u32[]{:S(2)}) collective-permute-start(bf16[1,240,768]{2,1,0:T(8,128)(2,1)S(1)} %get-tuple-element.167), channel_id=1, source_target_pairs={{0,16},{2,18},{4,20},{6,22},{8,24},{10,26},{12,28},{14,30},{16,0},... | collective-permute-start | bytes 1105928 | tf_op jit(solution)/shard_map/ppermute | solution.py:952
  279.3 47.1 %collective-permute-start.22 = (bf16[1,240,768]{2,1,0:T(8,128)(2,1)S(1)}, bf16[1,240,768]{2,1,0:T(8,128)(2,1)S(1)}, u32[]{:S(2)}, u32[]{:S(2)}) collective-permute-start(bf16[1,240,768]{2,1,0:T(8,128)(2,1)S(1)} %get-tuple-element.166), channel_id=1, source_target_pairs={{0,24},{2,26},{4,28},{6,30},{8,0},{10,2},{12,4},{14,6},{16,8},{18,... | collective-permute-start | bytes 1105928 | tf_op jit(solution)/shard_map/ppermute | solution.py:952
  326.4 7.3 %copy-start.5 = (bf16[1,240,768]{2,1,0:T(8,128)(2,1)}, bf16[1,240,768]{2,1,0:T(8,128)(2,1)S(1)}, u32[]{:S(2)}) copy-start(bf16[1,240,768]{2,1,0:T(8,128)(2,1)S(1)} %collective-permute-done.21) | copy-start | bytes 1105924
  326.4 4.2 %copy-start.6 = (bf16[1,240,768]{2,1,0:T(8,128)(2,1)}, bf16[1,240,768]{2,1,0:T(8,128)(2,1)S(1)}, u32[]{:S(2)}) copy-start(bf16[1,240,768]{2,1,0:T(8,128)(2,1)S(1)} %collective-permute-done.22) | copy-start | bytes 1105924
  326.4 4.2 %collective-permute-start.23 = (bf16[8,160,768]{2,1,0:T(8,128)(2,1)}, bf16[8,160,768]{2,1,0:T(8,128)(2,1)S(1)}, u32[]{:S(2)}, u32[]{:S(2)}) collective-permute-start(bf16[8,160,768]{2,1,0:T(8,128)(2,1)} %get-tuple-element.148), channel_id=1, source_target_pairs={{0,2},{2,0},{4,6},{6,4},{8,10},{10,8},{12,14},{14,12},{16,18},{18,... | collective-permute-start | bytes 5898248 | tf_op jit(solution)/shard_map/ppermute | solution.py:952
  330.6 5.0 %copy-start.3 = (bf16[1024,768]{1,0:T(8,128)(2,1)S(1)}, bf16[1024,768]{1,0:T(8,128)(2,1)}, u32[]{:S(2)}) copy-start(bf16[1024,768]{1,0:T(8,128)(2,1)} %get-tuple-element.143) | copy-start | bytes 4718596
  333.8 24.2 %collective-permute-start.24 = (bf16[4,160,768]{2,1,0:T(8,128)(2,1)}, bf16[4,160,768]{2,1,0:T(8,128)(2,1)}, u32[]{:S(2)}, u32[]{:S(2)}) collective-permute-start(bf16[4,160,768]{2,1,0:T(8,128)(2,1)} %get-tuple-element.165), channel_id=1, source_target_pairs={{0,4},{2,6},{4,0},{6,2},{8,12},{10,14},{12,8},{14,10},{16,20},{18,... | collective-permute-start | bytes 2949128 | tf_op jit(solution)/shard_map/ppermute | solution.py:952
  337.0 20.7 %collective-permute-start.25 = (bf16[1,512,768]{2,1,0:T(8,128)(2,1)}, bf16[1,512,768]{2,1,0:T(8,128)(2,1)}, u32[]{:S(2)}, u32[]{:S(2)}) collective-permute-start(bf16[1,512,768]{2,1,0:T(8,128)(2,1)} %get-tuple-element.173), channel_id=1, source_target_pairs={{0,1},{1,0},{2,3},{3,2},{4,5},{5,4},{6,7},{7,6},{8,9},{9,8},{10,11... | collective-permute-start | bytes 2359304 | tf_op jit(solution)/shard_map/ppermute | solution.py:930
  338.1 36.5 %collective-permute-start.30 = (bf16[1,512,768]{2,1,0:T(8,128)(2,1)}, bf16[1,512,768]{2,1,0:T(8,128)(2,1)}, u32[]{:S(2)}, u32[]{:S(2)}) collective-permute-start(bf16[1,512,768]{2,1,0:T(8,128)(2,1)} %get-tuple-element.172), channel_id=1, source_target_pairs={{0,1},{1,0},{2,3},{3,2},{4,5},{5,4},{6,7},{7,6},{8,9},{9,8},{10,11... | collective-permute-start | bytes 2359304 | tf_op jit(solution)/shard_map/ppermute | solution.py:930
  341.5 46.0 %collective-permute-start.29 = (bf16[432,768]{1,0:T(8,128)(2,1)S(1)}, bf16[432,768]{1,0:T(8,128)(2,1)S(1)}, u32[]{:S(2)}, u32[]{:S(2)}) collective-permute-start(bf16[432,768]{1,0:T(8,128)(2,1)S(1)} %pad_maximum_fusion), channel_id=1, source_target_pairs={{0,1},{1,0},{2,3},{3,2},{4,5},{5,4},{6,7},{7,6},{8,9},{9,8},{10,11... | collective-permute-start | bytes 1990664 | tf_op jit(solution)/shard_map/ppermute | solution.py:930
  360.1 14.4 %collective-permute-start.26 = (bf16[1,160,768]{2,1,0:T(8,128)(2,1)}, bf16[1,160,768]{2,1,0:T(8,128)(2,1)S(1)}, u32[]{:S(2)}, u32[]{:S(2)}) collective-permute-start(bf16[1,160,768]{2,1,0:T(8,128)(2,1)} %get-tuple-element.171), channel_id=1, source_target_pairs={{0,8},{2,10},{4,12},{6,14},{8,16},{10,18},{12,20},{14,22},{16,24},... | collective-permute-start | bytes 737288 | tf_op jit(solution)/shard_map/ppermute | solution.py:952
  360.1 21.2 %collective-permute-start.27 = (bf16[1,160,768]{2,1,0:T(8,128)(2,1)}, bf16[1,160,768]{2,1,0:T(8,128)(2,1)S(1)}, u32[]{:S(2)}, u32[]{:S(2)}) collective-permute-start(bf16[1,160,768]{2,1,0:T(8,128)(2,1)} %get-tuple-element.170), channel_id=1, source_target_pairs={{0,16},{2,18},{4,20},{6,22},{8,24},{10,26},{12,28},{14,30},{16,0},... | collective-permute-start | bytes 737288 | tf_op jit(solution)/shard_map/ppermute | solution.py:952
  363.6 21.7 %collective-permute-start.28 = (bf16[1,160,768]{2,1,0:T(8,128)(2,1)}, bf16[1,160,768]{2,1,0:T(8,128)(2,1)}, u32[]{:S(2)}, u32[]{:S(2)}) collective-permute-start(bf16[1,160,768]{2,1,0:T(8,128)(2,1)} %get-tuple-element.169), channel_id=1, source_target_pairs={{0,24},{2,26},{4,28},{6,30},{8,0},{10,2},{12,4},{14,6},{16,8},{18,... | collective-permute-start | bytes 737288 | tf_op jit(solution)/shard_map/ppermute | solution.py:952
  388.8 7.9 %collective-permute-start.31 = (bf16[160,768]{1,0:T(8,128)(2,1)S(1)}, bf16[160,768]{1,0:T(8,128)(2,1)S(1)}, u32[]{:S(2)}, u32[]{:S(2)}) collective-permute-start(bf16[160,768]{1,0:T(8,128)(2,1)S(1)} %fusion.11), channel_id=1, source_target_pairs={{0,1},{1,0},{2,3},{3,2},{4,5},{5,4},{6,7},{7,6},{8,9},{9,8},{10,11... | collective-permute-start | bytes 737288 | tf_op jit(solution)/shard_map/ppermute | solution.py:930
  390.1 5.7 %copy-start.4 = (bf16[1,192,768]{2,1,0:T(8,128)(2,1)S(1)}, bf16[1,192,768]{2,1,0:T(8,128)(2,1)}, u32[]{:S(2)}) copy-start(bf16[1,192,768]{2,1,0:T(8,128)(2,1)} %reduce-scatter.2.cloned.1.call-done) | copy-start | bytes 884740
  (10 other events, 14.3 us)
Sparse Core Ops, SparseCore 0:
  10.3 101.8 all-gather.2
  228.0 97.7 reduce-scatter.1

commit v4 on v3

--- a/solution.py
+++ b/solution.py
@@ -704,62 +704,91 @@
     )
 
 
-def product_kernel(*refs, more, split):
-    place_ref, a_ref, b_ref = refs[:3]
-    steps = pl.num_programs(0)
-
-    def write(x_ref, y_ref, times=dot_tn):
-        made = times(x_ref[...], y_ref[...]).astype(bf16)
-        if not split:
-            refs[-1][...] = made.reshape(refs[-1].shape)
-            return
-        keep_ref, send_ref, held_ref = refs[-3:]
-        held_ref[...] = made.reshape(held_ref.shape)
-        core = lax.rem(place_ref[1], 2)
-        keep_ref[...] = held_ref[:, core]
-        send_ref[...] = held_ref[:, 1 - core]
-
-    if more:
-        pl.when(pl.program_id(0) < steps - 1)(lambda: write(a_ref, b_ref))
-        pl.when(pl.program_id(0) == steps - 1)(lambda: write(*refs[3:5], dot))
-    else:
-        write(a_ref, b_ref)
-
-
-def product(place, shape, a, b, out_block, out_at, a_moves, steps, more=(), split=False):
-    tokens = a.shape[0]
-    a_cols = a.shape[1] // (steps if a_moves else 1)
-    b_cols = b.shape[1] // (1 if a_moves else steps)
-    moving = {"index_map": lambda i, s: (0, jnp.minimum(i, steps - 1))}
-    still = {"index_map": lambda i, s: (0, 0), "pipeline_mode": pl.Buffered(1)}
-    in_specs = [
-        pl.BlockSpec((tokens, a_cols), **(moving if a_moves else still)),
-        pl.BlockSpec((tokens, b_cols), **(still if a_moves else moving)),
-    ]
-    in_specs += [pl.BlockSpec(v.shape, **still) for v in more]
-    halved = [n // 2 if split else n for n in (shape[0], out_block[0])]
-    out_specs = pl.BlockSpec((halved[1],) + out_block[1:], lambda i, s: out_at(i))
-    out_shape = shape_of((halved[0],) + shape[1:], bf16)
+def share(place_ref, blocks, keep, send):
+    core = lax.rem(place_ref[1], 2)
+
+    @pl.when(core == 0)
+    def _():
+        keep(blocks[:, 0])
+        send(blocks[:, 1])
+
+    @pl.when(core == 1)
+    def _():
+        keep(blocks[:, 1])
+        send(blocks[:, 0])
+
+
+def store(ref, *at):
+    def body(value):
+        ref[at if at else ...] = value
+
+    return body
+
+
+def split_product_kernel(place_ref, a_ref, b_ref, keep_ref, send_ref):
+    made = dot_tn(a_ref[...], b_ref[...]).astype(bf16)
+    made = made.reshape((keep_ref.shape[0], 2) + keep_ref.shape[1:])
+    share(place_ref, made, store(keep_ref), store(send_ref))
+
+
+def split_product(place, a, b, shards):
+    tokens, width = a.shape
+    steps = b.shape[1] // width
+    shard = width // shards
+    out = pl.BlockSpec((shards // 2, shard, width), lambda i, s: (0, i, 0))
     return pl.pallas_call(
-        functools.partial(product_kernel, more=bool(more), split=split),
+        split_product_kernel,
         grid_spec=pltpu.PrefetchScalarGridSpec(
             num_scalar_prefetch=1,
-            grid=(steps + bool(more),),
-            in_specs=in_specs,
-            out_specs=[out_specs] * 2 if split else out_specs,
-            scratch_shapes=(
-                [pltpu.VMEM((out_block[0] // 2, 2) + out_block[1:], bf16)] if split else []
-            ),
-        ),
-        out_shape=[out_shape] * 2 if split else out_shape,
+            grid=(steps,),
+            in_specs=[
+                pl.BlockSpec((tokens, width), lambda i, s: (0, 0), pipeline_mode=pl.Buffered(1)),
+                pl.BlockSpec((tokens, width), lambda i, s: (0, i)),
+            ],
+            out_specs=[out] * 2,
+        ),
+        out_shape=[shape_of((shards // 2, steps * shard, width), bf16)] * 2,
         compiler_params=pltpu.CompilerParams(vmem_limit_bytes=VMEM_LIMIT),
         cost_estimate=cost(
-            flops=2 * tokens * a.shape[1] * b.shape[1],
-            bytes_accessed=2 * (a.size + b.size + a.shape[1] * b.shape[1]),
-            transcendentals=0,
-        ),
-        name="product",
-    )(place, a, b, *more)
+            flops=2 * tokens * width * b.shape[1],
+            bytes_accessed=2 * (a.size + b.size + width * b.shape[1]),
+        ),
+        name="split_product",
+    )(place, a, b)
+
+
+def pair_product_kernel(a_ref, b_ref, cT_ref, d_ref, out_ref):
+    groups, rows, width = out_ref.shape
+    first = a_ref.shape[1] // groups
+    made = dot_tn(a_ref[...], b_ref[...]).astype(bf16)
+    out_ref[:, :first, :] = made.reshape(groups, first, width)
+    made = dot(cT_ref[...], d_ref[...]).astype(bf16)
+    out_ref[:, first:, :] = made.reshape(groups, rows - first, width)
+
+
+def pair_product(a, b, cT, d, shards):
+    tokens, width = b.shape
+    steps = a.shape[1] // width
+    rows = (a.shape[1] + cT.shape[0]) // shards
+    still = {"index_map": lambda i: (0, 0), "pipeline_mode": pl.Buffered(1)}
+    return pl.pallas_call(
+        pair_product_kernel,
+        grid=(steps,),
+        in_specs=[
+            pl.BlockSpec((tokens, width), lambda i: (0, i)),
+            pl.BlockSpec((tokens, width), **still),
+            pl.BlockSpec((cT.shape[0] // steps, tokens), lambda i: (i, 0)),
+            pl.BlockSpec((tokens, width), **still),
+        ],
+        out_specs=pl.BlockSpec((shards // steps, rows, width), lambda i: (i, 0, 0)),
+        out_shape=shape_of((shards, rows, width), bf16),
+        compiler_params=pltpu.CompilerParams(vmem_limit_bytes=VMEM_LIMIT),
+        cost_estimate=cost(
+            flops=2 * tokens * width * (a.shape[1] + cT.shape[0]),
+            bytes_accessed=2 * (a.size + b.size + cT.size + d.size + shards * rows * width),
+        ),
+        name="pair_product",
+    )(a, b, cT, d)
 
 
 def input_grad_kernel(side_ref, g_ref, gr1_ref, w_ref, keep_ref, send_ref):
@@ -823,25 +852,24 @@
 
 
 def last_product_kernel(place_ref, a_ref, b_ref, *refs, shards):
-    keep_ref, send_ref, held_ref = refs[-3:]
+    keep_ref, send_ref = refs[-2:]
     at = pl.program_id(0)
     width = a_ref.shape[1]
     shard = width // shards
-    core = lax.rem(place_ref[1], 2)
     made = dot_tn(a_ref[...], b_ref[...]).astype(bf16)
-    held_ref[...] = made.reshape(held_ref.shape)
-    rows = pl.ds(pl.multiple_of(at * shard, 16), shard)
-    keep_ref[:, rows, :] = held_ref[:, core]
-    send_ref[:, rows, :] = held_ref[:, 1 - core]
+    here = (slice(None), pl.ds(pl.multiple_of(at * shard, 16), shard), slice(None))
+    made = made.reshape(shards // 2, 2, shard, width)
+    share(place_ref, made, store(keep_ref, *here), store(send_ref, *here))
 
     @pl.when(at == pl.num_programs(0) - 1)
     def _():
-        held_ref[:, :, :16, :] = jnp.zeros(held_ref[:, :, :16, :].shape, bf16)
+        end = keep_ref.shape[1] - 16
+        for ref in (keep_ref, send_ref):
+            ref[:, end:, :] = jnp.zeros((shards // 2, 16, width), bf16)
         for j, v in enumerate(vector_block(*refs[:3], shards)):
-            held_ref[:, :, j : j + 1, :LANES] = v.reshape(shards // 2, 2, 1, LANES)
-        end = slice(keep_ref.shape[1] - 16, keep_ref.shape[1])
-        keep_ref[:, end, :] = held_ref[:, core, :16]
-        send_ref[:, end, :] = held_ref[:, 1 - core, :16]
+            here = (slice(None), slice(end + j, end + j + 1), slice(0, LANES))
+            v = v.reshape(shards // 2, 2, 1, LANES)
+            share(place_ref, v, store(keep_ref, *here), store(send_ref, *here))
 
 
 def last_product(place, a, b, sums, shards):
@@ -860,7 +888,6 @@
             ]
             + [pl.BlockSpec(v.shape, lambda i, s: (0, 0)) for v in sums],
             out_specs=[pl.BlockSpec(out, lambda i, s: (0, 0, 0))] * 2,
-            scratch_shapes=[pltpu.VMEM((shards // 2, 2, shard, width), bf16)],
         ),
         out_shape=[shape_of(out, bf16)] * 2,
         compiler_params=pltpu.CompilerParams(vmem_limit_bytes=VMEM_LIMIT),
@@ -1089,25 +1116,18 @@
     out_other = out_other.reshape(-1, half, width)
     part = chunks * shard
     if by_rows:
-        core_split = functools.partial(product, side, split=True)
         out_other = swapped(out_other)
-        g_in = core_split(
-            (shards, part + shard, width), low, gp, (shards, shard, width), lambda i: (0, i, 0),
-            False, chunks, (attnT, gb),
-        )
+        g_in = split_product(side, low, gp, shards)
         *g_in, act = tied(*g_in, act)
         in_sum = StagedSum(*g_in, "dp")
-        g_ffo = product(
-            side, (shards, part, width), act, gs, (shards // chunks, part, width),
-            lambda i: (i, 0, 0), True, chunks,
-        )
+        g_ffo = pair_product(act, gs, attnT, gb, shards)
     else:
         out = jnp.concatenate([out, out_other], axis=1).reshape(rows, tok_seq, width)
         g_ffo = dot_tn(act, gs).astype(bf16).reshape(shards, part, width)
         g_in = dot_tn(low, gp).astype(bf16).reshape(shards, shard, chunks, width)
         g_in = g_in.transpose(0, 2, 1, 3).reshape(shards, part, width)
         g_out = dot_tn(attn, gb).astype(bf16).reshape(shards, shard, width)
-        g_in = jnp.concatenate([g_in, g_out], axis=1)
+        g_ffo = jnp.concatenate([g_ffo, g_out], axis=1)
         g_in = lax.psum_scatter(g_in, "dp", scatter_dimension=0, tiled=True)[0]
     if by_rows:
         g_ffo, do, in_sum.came = tied(g_ffo, do, in_sum.came)
@@ -1120,12 +1140,14 @@
         in_sum.step(2)
         g_qkv = last_product(side, x, g_x, (sums, sums_in, sums_qv), shards)
         g_qkv, gr1 = tied(g_qkv, gr1)
+        qkv_sum = StagedSum(*g_qkv, "dp")
         grad_x, grad_other = input_grad(side, g_x, gr1, w_qkv, *x_halves, BLOCK)
-        grad_other, g_qkv, in_sum.came = tied(grad_other, g_qkv, in_sum.came)
-        qkv_sum = StagedSum(*g_qkv, "dp")
+        grad_other, qkv_sum.came = tied(grad_other, qkv_sum.came)
         qkv_sum.step(1)
         grad_other = [swapped(grad_other[r : r + 1]) for r in range(mine)]
-        qkv_sum.came, grad_other[0] = tied(qkv_sum.came, grad_other[0])
+        qkv_sum.came, in_sum.came, grad_other[0] = tied(
+            qkv_sum.came, in_sum.came, grad_other[0]
+        )
         qkv_sum.step(2)
         g_in = in_sum.result()
         both = swapped(jnp.concatenate([g_in, g_ffo], axis=0))
@@ -1134,8 +1156,8 @@
         for r in range(mine):
             grad_x = placed(grad_x, grad_other[r], seq_index, r)
         out = placed(out, out_other, seq_index)
-        g_in = g_in.astype(f32) + both[: part + shard].astype(f32)
-        d_ffo = g_ffo.astype(f32) + both[part + shard :].astype(f32)
+        g_in = g_in.astype(f32) + both[:part].astype(f32)
+        g_ffo = g_ffo.astype(f32) + both[part:].astype(f32)
         g_qkv = g_qkv.astype(f32) + swapped(g_qkv).astype(f32)
     else:
         g_x, sums_qv = attend_gathered_back(saved, attn, do)
@@ -1151,10 +1173,10 @@
         g_qkv = lax.psum_scatter(g_qkv, "dp", scatter_dimension=0, tiled=True)[0]
         grad_x, grad_other = input_grad(side, g_x, gr1, w_qkv, *x_halves, BLOCK)
         grad_x = jnp.concatenate([grad_x, grad_other], axis=1).reshape(rows, tok_seq, width)
-        d_ffo, g_in, g_qkv = [lax.psum(v, "seq").astype(f32) for v in (g_ffo, g_in, g_qkv)]
+        g_ffo, g_in, g_qkv = [lax.psum(v, "seq").astype(f32) for v in (g_ffo, g_in, g_qkv)]
     vectors = g_qkv[3 * shard :, :LANES]
     d_qkv = jnp.concatenate([g_qkv[j * shard : (j + 1) * shard] for j in range(3)], axis=1)
-    d_out = g_in[part:]
+    d_ffo, d_out = g_ffo[:part], g_ffo[part:]
     d_in = jnp.concatenate([g_in[c * shard : (c + 1) * shard] for c in range(chunks)], axis=1)
     sizes = [v.shape[0] for v in small]
     d_small = []

time: 412 us -> 395 us (0.959)
  waiting for transfers between devices: 104 us -> 91.6 us
    ppermute x7, waiting for transfers between devices: 23.5 us -> 3.69 us  [swapped(): return lax.ppermute(values, 'seq', [(0, 1), (1, 0)])]
    ppermute x25, waiting for transfers between devices: 80 us -> 87.8 us  [turned(): return lax.ppermute(values, axis, perm)]
  transfers between devices with their start and end apart: 34 -> 34, of which waited for: 19 -> 16; matrix products, arithmetic and copies ran while one was open for 7% -> 6% of each run, Pallas kernels for 31% -> 33%
where the time goes in v4:
time: 395 us; the launch traced here: 390 us
  Pallas kernels  219 us (55%)
  waiting for transfers between devices  91.6 us (23%)
  starting transfers between devices  29 us (7%)
  other arithmetic  18.4 us (5%)
  local copies, waits for them, and re-layouts  17.4 us (4%)
  between operations  14.5 us (4%)
    ppermute x25, waiting for transfers between devices, turned(): return lax.ppermute(values, axis, perm)  87.8 us
    pallas_call x1, Pallas kernels, dense(): pl.pallas_call(dense_kernel, grid_spec=pltpu.PrefetchScalarGridSpec(num_s...  73.1 us
    pallas_call x1, Pallas kernels, attend_rows_back(): pl.pallas_call(attend_back_kernel, grid_spec=pltpu.PrefetchScalarGridSpec...  39.8 us
    pallas_call x1, Pallas kernels, attend_rows(): pl.pallas_call(attend_kernel, grid_spec=pltpu.PrefetchScalarGridSpec(num_...  21.9 us
    ppermute x25, starting transfers between devices, turned(): return lax.ppermute(values, axis, perm)  21 us
    pallas_call x1, Pallas kernels, pair_product(): pl.pallas_call(pair_product_kernel, grid=(steps,), in_specs=[pl.BlockSpec...  18.3 us
    pallas_call x1, Pallas kernels, project(): pl.pallas_call(functools.partial(project_kernel, shards=shards, pieces=[b...  17.6 us
    pallas_call x1, Pallas kernels, split_product(): pl.pallas_call(split_product_kernel, grid_spec=pltpu.PrefetchScalarGridSp...  15.7 us
  transfers between devices with their start and end apart: 34, of which 16 were waited for; matrix products, arithmetic and copies ran while one was open for 6% of the time, Pallas kernels for 33%

profile of v4, /device:TPU:12, one launch (start us, length us, event | category | flops | bytes accessed | tf_op | source)
XLA Modules:
  0.0 390.2 jit_solution(5129809068588794198)
XLA Ops:
  7.2 2.4 lower.1
  9.7 1.7 constant_dynamic-slice_fusion.1
  12.0 1.6 collective-permute-start
  13.6 1.0 collective-permute-start.1
  14.6 2.0 collective-permute-start.2
  16.6 1.5 collective-permute-start.3
  18.1 12.6 %collective-permute-done.refs_1_ = bf16[48,2432]{1,0:T(8,128)(2,1)S(1)} collective-permute-done((bf16[48,2432]{1,0:T(8,128)(2,1)S(1)}, bf16[48,2432]{1,0:T(8,128)(2,1)S(1)}, u32[]{:S(2)}, u32[]{:S(2)}) %collective-permute-start) | collective-permute-done | bytes 233504 | tf_op jit(solution)/shard_map/ppermute | solution.py:979
  30.7 19.6 %collective-permute-done.1.refs_2_ = bf16[48,2432]{1,0:T(8,128)(2,1)S(1)} collective-permute-done((bf16[48,2432]{1,0:T(8,128)(2,1)S(1)}, bf16[48,2432]{1,0:T(8,128)(2,1)S(1)}, u32[]{:S(2)}, u32[]{:S(2)}) %collective-permute-start.1) | collective-permute-done | bytes 233504 | tf_op jit(solution)/shard_map/ppermute | solution.py:979
  50.3 1.5 collective-permute-start.4
  51.8 2.2 collective-permute-done.2.refs_3_
  53.9 1.5 collective-permute-start.5
  56.6 6.0 %collective-permute-done.5.refs_6_ = bf16[48,2432]{1,0:T(8,128)(2,1)S(1)} collective-permute-done((bf16[48,2432]{1,0:T(8,128)(2,1)S(1)}, bf16[48,2432]{1,0:T(8,128)(2,1)S(1)}, u32[]{:S(2)}, u32[]{:S(2)}) %collective-permute-start.5) | collective-permute-done | bytes 233504 | tf_op jit(solution)/shard_map/ppermute | solution.py:979
  62.5 6.4 %collective-permute-done.6.refs_7_ = bf16[48,2432]{1,0:T(8,128)(2,1)S(1)} collective-permute-done((bf16[48,2432]{1,0:T(8,128)(2,1)S(1)}, bf16[48,2432]{1,0:T(8,128)(2,1)S(1)}, u32[]{:S(2)}, u32[]{:S(2)}) %collective-permute-start.6) | collective-permute-done | bytes 233504 | tf_op jit(solution)/shard_map/ppermute | solution.py:979
  72.5 1.2 constant_dynamic-slice_fusion
  73.7 2.5 collective-permute-start.16
  77.5 17.6 %project.1 = (bf16[2048,768]{1,0:T(8,128)(2,1)}, bf16[2048,2304]{1,0:T(8,128)(2,1)}, bf16[2304,2048]{1,0:T(8,128)(2,1)}, bf16[768,2432]{1,0:T(8,128)(2,1)}, f32[8,768]{1,0:T(8,128)}, /*index=5*/f32[8,3072]{1,0:T(8,128)}) custom-call(s32[2]{0:T(128)} %pad_add_fusion.place_ref.side_ref, bf16[2048,768]{1,0:T(8,128)(2,1)} %bitcast.78, ...), custom_call_target="tpu_custom_call" | custom-call | flops 1811939328 | bytes 8060928 | tf_op jit(solution)/shard_map/project/pallas_call | solution.py:195
  95.1 21.9 %attend.1 = (bf16[768,2048]{1,0:T(8,128)(2,1)}, f32[16,2048]{1,0:T(8,128)}) custom-call(s32[2,8]{1,0:T(2,128)} %constant_dynamic-slice_fusion.2.bounds_ref, bf16[2048,2304]{1,0:T(8,128)(2,1)} %get-tuple-element.105.k_ref.v_ref.q_ref, bf16[2304,2048]{1,0:T(8,128)(2,1)} %get-tuple-element.106.qT_ref.vT_ref.kT_ref, ...), custom_call_target="tpu_custom_call" | custom-call | flops 1610612736 | bytes 3932160 | tf_op jit(solution)/shard_map/attend/pallas_call | solution.py:348
  117.1 1.1 copy-done.2
  118.2 73.1 %dense.1 = (bf16[2048,768]{1,0:T(8,128)(2,1)}, bf16[1024,768]{1,0:T(8,128)(2,1)}, bf16[2048,3072]{1,0:T(8,128)(2,1)}, bf16[2048,3072]{1,0:T(8,128)(2,1)}, bf16[2...) custom-call(s32[2]{0:T(128)} %pad_add_fusion.place_ref.side_ref, ...), custom_call_target="tpu_custom_call" | custom-call | flops 10871635968 | bytes 17301504 | tf_op jit(solution)/shard_map/dense/pallas_call | solution.py:657
  191.3 15.7 %split_product.1 = (bf16[8,192,768]{2,1,0:T(8,128)(2,1)}, bf16[8,192,768]{2,1,0:T(8,128)(2,1)}) custom-call(s32[2]{0:T(128)} %pad_add_fusion.place_ref.side_ref, bf16[2048,768]{1,0:T(8,128)(2,1)} %get-tuple-element.114.a_ref, bf16[2048,3072]{1,0:T(8,128)(2,1)} %get-tuple-element.115.b_ref), custom_call_target="tpu_custom_call" | custom-call | flops 2415919104 | bytes 5111808 | tf_op jit(solution)/shard_map/split_product/pallas_call | solution.py:739
  207.0 18.3 %pair_product.1 = bf16[16,240,768]{2,1,0:T(8,128)(2,1)} custom-call(bf16[2048,3072]{1,0:T(8,128)(2,1)} %get-tuple-element.119.a_ref, bf16[2048,768]{1,0:T(8,128)(2,1)} %get-tuple-element.120.b_ref, bf16[768,2048]{1,0:T(8,128)(2,1)} %get-tuple-element.107.attn_ref.cT_ref.outT_ref, bf16[2048,768]{1,0:T(8,128)(2,1)} %get-tuple-element.121.d_ref), custom_call_target="tpu_custom_call" | custom-call | flops 3019898880 | bytes 6979584 | tf_op jit(solution)/shard_map/pair_product/pallas_call | solution.py:774
  227.0 3.2 add_convert_fusion
  230.2 2.5 collective-permute-start.19
  232.7 39.8 %attend_back.1 = (bf16[2048,2304]{1,0:T(8,128)(2,1)}, f32[8,768]{1,0:T(8,128)}) custom-call(s32[2,8]{1,0:T(2,128)} %constant_dynamic-slice_fusion.2.bounds_ref, bf16[2048,2304]{1,0:T(8,128)(2,1)} %get-tuple-element.105.k_ref.v_ref.q_ref, bf16[2304,2048]{1,0:T(8,128)(2,1)} %get-tuple-element.106.qT_ref.vT_ref.kT_ref, ...), custom_call_target="tpu_custom_call" | custom-call | flops 4026531840 | bytes 8650752 | tf_op jit(solution)/shard_map/attend_back/pallas_call | solution.py:472
  272.6 15.1 %last_product.1 = (bf16[8,160,768]{2,1,0:T(8,128)(2,1)}, bf16[8,160,768]{2,1,0:T(8,128)(2,1)}) custom-call(s32[2]{0:T(128)} %pad_add_fusion.place_ref.side_ref, bf16[2048,768]{1,0:T(8,128)(2,1)} %get-tuple-element.108.x_ref.a_ref, bf16[2048,2304]{1,0:T(8,128)(2,1)} %get-tuple-element.132.b_ref.g_ref, f32[8,768]{1,0:T(8,128)} %get-tuple-element.133.refs_0_, ...), custom_call_target="tpu_custom_call" | custom-call | flops 1811939328 | bytes 4030464 | tf_op jit(solution)/shard_map/last_product/pallas_call | solution.py:880
  287.6 15.4 %input_grad.1 = (bf16[2048,768]{1,0:T(8,128)(2,1)}, bf16[1024,768]{1,0:T(8,128)(2,1)}) custom-call(s32[2]{0:T(128)} %pad_add_fusion.place_ref.side_ref, bf16[2048,2304]{1,0:T(8,128)(2,1)} %get-tuple-element.132.b_ref.g_ref, f32[2048,768]{1,0:T(8,128)} %get-tuple-element.139.gr1_ref, bf16[768,2432]{1,0:T(8,128)(2,1)} %get-tuple-element.140.w_ref), custom_call_target="tpu_custom_call" | custom-call | flops 1811939328 | bytes 5603328 | tf_op jit(solution)/shard_map/input_grad/pallas_call | solution.py:818
  303.1 3.8 add_convert_fusion.3
  306.9 1.3 fusion.12
  308.7 1.0 fusion.3
  309.7 2.0 collective-permute-start.24
  311.7 8.1 %collective-permute-done.22 = bf16[1,192,768]{2,1,0:T(8,128)(2,1)S(1)} collective-permute-done((bf16[1,192,768]{2,1,0:T(8,128)(2,1)}, bf16[1,192,768]{2,1,0:T(8,128)(2,1)S(1)}, u32[]{:S(2)}, u32[]{:S(2)}) %collective-permute-start.22) | collective-permute-done | bytes 294944 | tf_op jit(solution)/shard_map/ppermute | solution.py:979
  319.8 1.4 collective-permute-start.30
  321.2 14.5 %collective-permute-done.23 = bf16[1,192,768]{2,1,0:T(8,128)(2,1)S(1)} collective-permute-done((bf16[1,192,768]{2,1,0:T(8,128)(2,1)}, bf16[1,192,768]{2,1,0:T(8,128)(2,1)S(1)}, u32[]{:S(2)}, u32[]{:S(2)}) %collective-permute-start.23) | collective-permute-done | bytes 294944 | tf_op jit(solution)/shard_map/ppermute | solution.py:979
  336.4 1.3 fusion.10
  337.7 1.0 pad_maximum_fusion
  338.8 1.8 collective-permute-start.29
  340.6 2.1 fusion.7
  342.7 3.3 collective-permute-start.27
  346.0 2.0 collective-permute-start.28
  348.0 2.7 constant_dynamic-update-slice_fusion.2
  350.7 1.1 collective-permute-done.26
  351.8 12.2 %collective-permute-done.27 = bf16[1,160,768]{2,1,0:T(8,128)(2,1)} collective-permute-done((bf16[1,160,768]{2,1,0:T(8,128)(2,1)}, bf16[1,160,768]{2,1,0:T(8,128)(2,1)}, u32[]{:S(2)}, u32[]{:S(2)}) %collective-permute-start.27) | collective-permute-done | bytes 245792 | tf_op jit(solution)/shard_map/ppermute | solution.py:979
  364.0 3.8 collective-permute-done.28
  367.8 1.0 convert_add_fusion.5
  368.8 1.1 convert_add_fusion
  371.4 1.3 fusion.11
  373.1 2.1 constant_dynamic-update-slice_fusion
  377.0 3.7 collective-permute-done.31
  (107 shorter events, 15.9 us)
Async XLA Ops:
  7.2 109.9 %all-gather.3.cloned.1.call-start = ((), (), s32[]{:S(2)}) async-start(), calls=%async_computation.2 | async-start | bytes 11280384 | tf_op jit(solution)/shard_map/all_gather | solution.py:1074
  9.7 62.8 %copy-start = (bf16[4,512,768]{2,1,0:T(8,128)(2,1)S(1)}, bf16[4,512,768]{2,1,0:T(8,128)(2,1)}, u32[]{:S(2)}) copy-start(bf16[4,512,768]{2,1,0:T(8,128)(2,1)} %param.29) | copy-start | bytes 9437188
  9.7 328.0 %reduce-scatter.2.cloned.1.call-start = ((), (), s32[]{:S(2)}) async-start(), calls=%async_computation.1 | async-start | bytes 6266880 | tf_op jit(solution)/shard_map/reduce_scatter | solution.py:1134
  11.4 64.8 %copy-start.23 = (s32[4,8]{1,0:T(4,128)S(1)}, s32[4,8]{1,0:T(4,128)}, u32[]{:S(2)}) copy-start(s32[4,8]{1,0:T(4,128)} %param.28) | copy-start | bytes 388
  11.4 61.0 %collective-permute-start.15 = (bf16[2,512,768]{2,1,0:T(8,128)(2,1)S(1)}, bf16[2,512,768]{2,1,0:T(8,128)(2,1)}, u32[]{:S(2)}, u32[]{:S(2)}) collective-permute-start(bf16[2,512,768]{2,1,0:T(8,128)(2,1)S(1)} %constant_dynamic-slice_fusion.1), channel_id=1, source_target_pairs={{0,1},{1,0},{2,3},{3,2},{4,5},{5,4},{6,7},{7,6},{8,9},{9,8},{10,11... | collective-permute-start | bytes 4718600 | tf_op jit(solution)/shard_map/ppermute | solution.py:957
  12.0 18.7 %collective-permute-start = (bf16[48,2432]{1,0:T(8,128)(2,1)S(1)}, bf16[48,2432]{1,0:T(8,128)(2,1)S(1)}, u32[]{:S(2)}, u32[]{:S(2)}) collective-permute-start(bf16[48,2432]{1,0:T(8,128)(2,1)S(1)} %copy-done.7), channel_id=1, source_target_pairs={{0,8},{2,10},{4,12},{6,14},{8,16},{10,18},{12,20},{14,22},{16,24},... | collective-permute-start | bytes 700424 | tf_op jit(solution)/shard_map/ppermute | solution.py:979
  13.6 36.7 %collective-permute-start.1 = (bf16[48,2432]{1,0:T(8,128)(2,1)S(1)}, bf16[48,2432]{1,0:T(8,128)(2,1)S(1)}, u32[]{:S(2)}, u32[]{:S(2)}) collective-permute-start(bf16[48,2432]{1,0:T(8,128)(2,1)S(1)} %copy-done.7), channel_id=1, source_target_pairs={{0,16},{2,18},{4,20},{6,22},{8,24},{10,26},{12,28},{14,30},{16,0},... | collective-permute-start | bytes 700424 | tf_op jit(solution)/shard_map/ppermute | solution.py:979
  14.6 39.4 %collective-permute-start.2 = (bf16[48,2432]{1,0:T(8,128)(2,1)S(1)}, bf16[48,2432]{1,0:T(8,128)(2,1)S(1)}, u32[]{:S(2)}, u32[]{:S(2)}) collective-permute-start(bf16[48,2432]{1,0:T(8,128)(2,1)S(1)} %copy-done.7), channel_id=1, source_target_pairs={{0,24},{2,26},{4,28},{6,30},{8,0},{10,2},{12,4},{14,6},{16,8},{18,... | collective-permute-start | bytes 700424 | tf_op jit(solution)/shard_map/ppermute | solution.py:979
  16.6 38.8 %collective-permute-start.3 = (bf16[48,2432]{1,0:T(8,128)(2,1)S(1)}, bf16[48,2432]{1,0:T(8,128)(2,1)S(1)}, u32[]{:S(2)}, u32[]{:S(2)}) collective-permute-start(bf16[48,2432]{1,0:T(8,128)(2,1)S(1)} %copy-done.7), channel_id=1, source_target_pairs={{0,4},{2,6},{4,0},{6,2},{8,12},{10,14},{12,8},{14,10},{16,20},{18,... | collective-permute-start | bytes 700424 | tf_op jit(solution)/shard_map/ppermute | solution.py:979
  30.7 25.3 %copy-start.8 = (bf16[48,2432]{1,0:T(8,128)(2,1)}, bf16[48,2432]{1,0:T(8,128)(2,1)S(1)}, u32[]{:S(2)}) copy-start(bf16[48,2432]{1,0:T(8,128)(2,1)S(1)} %collective-permute-done.refs_1_) | copy-start | bytes 700420
  30.7 25.3 %collective-permute-start.7 = (bf16[48,2432]{1,0:T(8,128)(2,1)S(1)}, bf16[48,2432]{1,0:T(8,128)(2,1)S(1)}, u32[]{:S(2)}, u32[]{:S(2)}) collective-permute-start(bf16[48,2432]{1,0:T(8,128)(2,1)S(1)} %copy-done.7), channel_id=1, source_target_pairs={{0,2},{2,0},{4,6},{6,4},{8,10},{10,8},{12,14},{14,12},{16,18},{18,... | collective-permute-start | bytes 700424 | tf_op jit(solution)/shard_map/ppermute | solution.py:979
  50.3 18.6 %copy-start.9 = (bf16[48,2432]{1,0:T(8,128)(2,1)}, bf16[48,2432]{1,0:T(8,128)(2,1)S(1)}, u32[]{:S(2)}) copy-start(bf16[48,2432]{1,0:T(8,128)(2,1)S(1)} %collective-permute-done.1.refs_2_) | copy-start | bytes 700420
  50.3 6.1 %collective-permute-start.4 = (bf16[48,2432]{1,0:T(8,128)(2,1)S(1)}, bf16[48,2432]{1,0:T(8,128)(2,1)S(1)}, u32[]{:S(2)}, u32[]{:S(2)}) collective-permute-start(bf16[48,2432]{1,0:T(8,128)(2,1)S(1)} %collective-permute-done.refs_1_), channel_id=1, source_target_pairs={{0,4},{2,6},{4,0},{6,2},{8,12},{10,14},{12,8},{14,10},{16,20},{18,... | collective-permute-start | bytes 700424 | tf_op jit(solution)/shard_map/ppermute | solution.py:979
  53.9 15.5 %copy-start.10 = (bf16[48,2432]{1,0:T(8,128)(2,1)}, bf16[48,2432]{1,0:T(8,128)(2,1)S(1)}, u32[]{:S(2)}) copy-start(bf16[48,2432]{1,0:T(8,128)(2,1)S(1)} %collective-permute-done.2.refs_3_) | copy-start | bytes 700420
  53.9 8.6 %collective-permute-start.5 = (bf16[48,2432]{1,0:T(8,128)(2,1)S(1)}, bf16[48,2432]{1,0:T(8,128)(2,1)S(1)}, u32[]{:S(2)}, u32[]{:S(2)}) collective-permute-start(bf16[48,2432]{1,0:T(8,128)(2,1)S(1)} %collective-permute-done.1.refs_2_), channel_id=1, source_target_pairs={{0,4},{2,6},{4,0},{6,2},{8,12},{10,14},{12,8},{14,10},{16,20},{18,... | collective-permute-start | bytes 700424 | tf_op jit(solution)/shard_map/ppermute | solution.py:979
  55.4 14.1 %copy-start.11 = (bf16[48,2432]{1,0:T(8,128)(2,1)}, bf16[48,2432]{1,0:T(8,128)(2,1)S(1)}, u32[]{:S(2)}) copy-start(bf16[48,2432]{1,0:T(8,128)(2,1)S(1)} %collective-permute-done.3.refs_4_) | copy-start | bytes 700420
  55.4 13.4 %collective-permute-start.6 = (bf16[48,2432]{1,0:T(8,128)(2,1)S(1)}, bf16[48,2432]{1,0:T(8,128)(2,1)S(1)}, u32[]{:S(2)}, u32[]{:S(2)}) collective-permute-start(bf16[48,2432]{1,0:T(8,128)(2,1)S(1)} %collective-permute-done.2.refs_3_), channel_id=1, source_target_pairs={{0,4},{2,6},{4,0},{6,2},{8,12},{10,14},{12,8},{14,10},{16,20},{18,... | collective-permute-start | bytes 700424 | tf_op jit(solution)/shard_map/ppermute | solution.py:979
  56.0 14.4 %copy-start.12 = (bf16[48,2432]{1,0:T(8,128)(2,1)}, bf16[48,2432]{1,0:T(8,128)(2,1)S(1)}, u32[]{:S(2)}) copy-start(bf16[48,2432]{1,0:T(8,128)(2,1)S(1)} %collective-permute-done.7.refs_8_) | copy-start | bytes 700420
  56.0 12.9 %collective-permute-start.8 = (bf16[48,2432]{1,0:T(8,128)(2,1)S(1)}, bf16[48,2432]{1,0:T(8,128)(2,1)S(1)}, u32[]{:S(2)}, u32[]{:S(2)}) collective-permute-start(bf16[48,2432]{1,0:T(8,128)(2,1)S(1)} %collective-permute-done.refs_1_), channel_id=1, source_target_pairs={{0,2},{2,0},{4,6},{6,4},{8,10},{10,8},{12,14},{14,12},{16,18},{18,... | collective-permute-start | bytes 700424 | tf_op jit(solution)/shard_map/ppermute | solution.py:979
  56.3 14.4 %copy-start.13 = (bf16[48,2432]{1,0:T(8,128)(2,1)}, bf16[48,2432]{1,0:T(8,128)(2,1)S(1)}, u32[]{:S(2)}) copy-start(bf16[48,2432]{1,0:T(8,128)(2,1)S(1)} %collective-permute-done.4.refs_5_) | copy-start | bytes 700420
  56.3 13.1 %collective-permute-start.9 = (bf16[48,2432]{1,0:T(8,128)(2,1)S(1)}, bf16[48,2432]{1,0:T(8,128)(2,1)S(1)}, u32[]{:S(2)}, u32[]{:S(2)}) collective-permute-start(bf16[48,2432]{1,0:T(8,128)(2,1)S(1)} %collective-permute-done.1.refs_2_), channel_id=1, source_target_pairs={{0,2},{2,0},{4,6},{6,4},{8,10},{10,8},{12,14},{14,12},{16,18},{18,... | collective-permute-start | bytes 700424 | tf_op jit(solution)/shard_map/ppermute | solution.py:979
  62.5 8.5 %copy-start.14 = (bf16[48,2432]{1,0:T(8,128)(2,1)}, bf16[48,2432]{1,0:T(8,128)(2,1)S(1)}, u32[]{:S(2)}) copy-start(bf16[48,2432]{1,0:T(8,128)(2,1)S(1)} %collective-permute-done.5.refs_6_) | copy-start | bytes 700420
  62.5 7.1 %collective-permute-start.10 = (bf16[48,2432]{1,0:T(8,128)(2,1)S(1)}, bf16[48,2432]{1,0:T(8,128)(2,1)S(1)}, u32[]{:S(2)}, u32[]{:S(2)}) collective-permute-start(bf16[48,2432]{1,0:T(8,128)(2,1)S(1)} %collective-permute-done.2.refs_3_), channel_id=1, source_target_pairs={{0,2},{2,0},{4,6},{6,4},{8,10},{10,8},{12,14},{14,12},{16,18},{18,... | collective-permute-start | bytes 700424 | tf_op jit(solution)/shard_map/ppermute | solution.py:979
  68.9 2.5 copy-start.15
  68.9 1.5 collective-permute-start.11
  68.9 8.6 %copy-start.16 = (bf16[48,2432]{1,0:T(8,128)(2,1)}, bf16[48,2432]{1,0:T(8,128)(2,1)S(1)}, u32[]{:S(2)}) copy-start(bf16[48,2432]{1,0:T(8,128)(2,1)S(1)} %collective-permute-done.8.refs_9_) | copy-start | bytes 700420
  68.9 1.8 collective-permute-start.12
  69.5 1.6 collective-permute-start.13
  69.6 1.8 collective-permute-start.14
  73.7 43.4 %collective-permute-start.16 = (bf16[2,512,768]{2,1,0:T(8,128)(2,1)}, bf16[2,512,768]{2,1,0:T(8,128)(2,1)S(1)}, u32[]{:S(2)}, u32[]{:S(2)}) collective-permute-start(bf16[2,512,768]{2,1,0:T(8,128)(2,1)} %constant_dynamic-slice_fusion), channel_id=1, source_target_pairs={{0,1},{1,0},{2,3},{3,2},{4,5},{5,4},{6,7},{7,6},{8,9},{9,8},{10,11... | collective-permute-start | bytes 4718600 | tf_op jit(solution)/shard_map/ppermute | solution.py:957
  207.0 18.3 %collective-permute-start.17 = (bf16[8,192,768]{2,1,0:T(8,128)(2,1)}, bf16[8,192,768]{2,1,0:T(8,128)(2,1)}, u32[]{:S(2)}, u32[]{:S(2)}) collective-permute-start(bf16[8,192,768]{2,1,0:T(8,128)(2,1)} %get-tuple-element.123), channel_id=1, source_target_pairs={{0,2},{2,0},{4,6},{6,4},{8,10},{10,8},{12,14},{14,12},{16,18},{18,... | collective-permute-start | bytes 7077896 | tf_op jit(solution)/shard_map/ppermute | solution.py:979
  225.3 47.2 %collective-permute-start.18 = (bf16[2,512,768]{2,1,0:T(8,128)(2,1)}, bf16[2,512,768]{2,1,0:T(8,128)(2,1)}, u32[]{:S(2)}, u32[]{:S(2)}) collective-permute-start(bf16[2,512,768]{2,1,0:T(8,128)(2,1)} %bitcast.95), channel_id=1, source_target_pairs={{0,1},{1,0},{2,3},{3,2},{4,5},{5,4},{6,7},{7,6},{8,9},{9,8},{10,11... | collective-permute-start | bytes 4718600 | tf_op jit(solution)/shard_map/ppermute | solution.py:957
  230.2 42.3 %collective-permute-start.19 = (bf16[4,192,768]{2,1,0:T(8,128)(2,1)}, bf16[4,192,768]{2,1,0:T(8,128)(2,1)S(1)}, u32[]{:S(2)}, u32[]{:S(2)}) collective-permute-start(bf16[4,192,768]{2,1,0:T(8,128)(2,1)} %get-tuple-element.161), channel_id=1, source_target_pairs={{0,4},{2,6},{4,0},{6,2},{8,12},{10,14},{12,8},{14,10},{16,20},{18,... | collective-permute-start | bytes 3538952 | tf_op jit(solution)/shard_map/ppermute | solution.py:979
  272.5 36.1 %copy-start.5 = (bf16[4,192,768]{2,1,0:T(8,128)(2,1)}, bf16[4,192,768]{2,1,0:T(8,128)(2,1)S(1)}, u32[]{:S(2)}) copy-start(bf16[4,192,768]{2,1,0:T(8,128)(2,1)S(1)} %collective-permute-done.19) | copy-start | bytes 3538948
  287.6 15.5 %collective-permute-start.20 = (bf16[8,160,768]{2,1,0:T(8,128)(2,1)}, bf16[8,160,768]{2,1,0:T(8,128)(2,1)}, u32[]{:S(2)}, u32[]{:S(2)}) collective-permute-start(bf16[8,160,768]{2,1,0:T(8,128)(2,1)} %get-tuple-element.144), channel_id=1, source_target_pairs={{0,2},{2,0},{4,6},{6,4},{8,10},{10,8},{12,14},{14,12},{16,18},{18,... | collective-permute-start | bytes 5898248 | tf_op jit(solution)/shard_map/ppermute | solution.py:979
  303.1 3.8 copy-start.3
  306.8 29.5 %collective-permute-start.21 = (bf16[4,160,768]{2,1,0:T(8,128)(2,1)}, bf16[4,160,768]{2,1,0:T(8,128)(2,1)}, u32[]{:S(2)}, u32[]{:S(2)}) collective-permute-start(bf16[4,160,768]{2,1,0:T(8,128)(2,1)} %get-tuple-element.163), channel_id=1, source_target_pairs={{0,4},{2,6},{4,0},{6,2},{8,12},{10,14},{12,8},{14,10},{16,20},{18,... | collective-permute-start | bytes 2949128 | tf_op jit(solution)/shard_map/ppermute | solution.py:979
  308.1 27.6 %collective-permute-start.25 = (bf16[1,512,768]{2,1,0:T(8,128)(2,1)}, bf16[1,512,768]{2,1,0:T(8,128)(2,1)}, u32[]{:S(2)}, u32[]{:S(2)}) collective-permute-start(bf16[1,512,768]{2,1,0:T(8,128)(2,1)} %get-tuple-element.171), channel_id=1, source_target_pairs={{0,1},{1,0},{2,3},{3,2},{4,5},{5,4},{6,7},{7,6},{8,9},{9,8},{10,11... | collective-permute-start | bytes 2359304 | tf_op jit(solution)/shard_map/ppermute | solution.py:957
  309.7 10.1 %collective-permute-start.22 = (bf16[1,192,768]{2,1,0:T(8,128)(2,1)}, bf16[1,192,768]{2,1,0:T(8,128)(2,1)S(1)}, u32[]{:S(2)}, u32[]{:S(2)}) collective-permute-start(bf16[1,192,768]{2,1,0:T(8,128)(2,1)} %get-tuple-element.166), channel_id=1, source_target_pairs={{0,8},{2,10},{4,12},{6,14},{8,16},{10,18},{12,20},{14,22},{16,24},... | collective-permute-start | bytes 884744 | tf_op jit(solution)/shard_map/ppermute | solution.py:979
  309.7 26.0 %collective-permute-start.23 = (bf16[1,192,768]{2,1,0:T(8,128)(2,1)}, bf16[1,192,768]{2,1,0:T(8,128)(2,1)S(1)}, u32[]{:S(2)}, u32[]{:S(2)}) collective-permute-start(bf16[1,192,768]{2,1,0:T(8,128)(2,1)} %get-tuple-element.165), channel_id=1, source_target_pairs={{0,16},{2,18},{4,20},{6,22},{8,24},{10,26},{12,28},{14,30},{16,0},... | collective-permute-start | bytes 884744 | tf_op jit(solution)/shard_map/ppermute | solution.py:979
  309.7 26.0 %collective-permute-start.24 = (bf16[1,192,768]{2,1,0:T(8,128)(2,1)}, bf16[1,192,768]{2,1,0:T(8,128)(2,1)}, u32[]{:S(2)}, u32[]{:S(2)}) collective-permute-start(bf16[1,192,768]{2,1,0:T(8,128)(2,1)} %get-tuple-element.164), channel_id=1, source_target_pairs={{0,24},{2,26},{4,28},{6,30},{8,0},{10,2},{12,4},{14,6},{16,8},{18,... | collective-permute-start | bytes 884744 | tf_op jit(solution)/shard_map/ppermute | solution.py:979
  319.8 30.9 %collective-permute-start.30 = (bf16[1,512,768]{2,1,0:T(8,128)(2,1)}, bf16[1,512,768]{2,1,0:T(8,128)(2,1)S(1)}, u32[]{:S(2)}, u32[]{:S(2)}) collective-permute-start(bf16[1,512,768]{2,1,0:T(8,128)(2,1)} %get-tuple-element.170), channel_id=1, source_target_pairs={{0,1},{1,0},{2,3},{3,2},{4,5},{5,4},{6,7},{7,6},{8,9},{9,8},{10,11... | collective-permute-start | bytes 2359304 | tf_op jit(solution)/shard_map/ppermute | solution.py:957
  338.8 29.0 %collective-permute-start.29 = (bf16[432,768]{1,0:T(8,128)(2,1)S(1)}, bf16[432,768]{1,0:T(8,128)(2,1)}, u32[]{:S(2)}, u32[]{:S(2)}) collective-permute-start(bf16[432,768]{1,0:T(8,128)(2,1)S(1)} %pad_maximum_fusion), channel_id=1, source_target_pairs={{0,1},{1,0},{2,3},{3,2},{4,5},{5,4},{6,7},{7,6},{8,9},{9,8},{10,11... | collective-permute-start | bytes 1990664 | tf_op jit(solution)/shard_map/ppermute | solution.py:957
  342.7 26.1 %copy-start.4 = (bf16[1,240,768]{2,1,0:T(8,128)(2,1)S(1)}, bf16[1,240,768]{2,1,0:T(8,128)(2,1)}, u32[]{:S(2)}) copy-start(bf16[1,240,768]{2,1,0:T(8,128)(2,1)} %reduce-scatter.2.cloned.1.call-done) | copy-start | bytes 1105924
  342.7 9.1 %collective-permute-start.26 = (bf16[1,160,768]{2,1,0:T(8,128)(2,1)}, bf16[1,160,768]{2,1,0:T(8,128)(2,1)S(1)}, u32[]{:S(2)}, u32[]{:S(2)}) collective-permute-start(bf16[1,160,768]{2,1,0:T(8,128)(2,1)} %get-tuple-element.169), channel_id=1, source_target_pairs={{0,8},{2,10},{4,12},{6,14},{8,16},{10,18},{12,20},{14,22},{16,24},... | collective-permute-start | bytes 737288 | tf_op jit(solution)/shard_map/ppermute | solution.py:979
  342.7 21.3 %collective-permute-start.27 = (bf16[1,160,768]{2,1,0:T(8,128)(2,1)}, bf16[1,160,768]{2,1,0:T(8,128)(2,1)}, u32[]{:S(2)}, u32[]{:S(2)}) collective-permute-start(bf16[1,160,768]{2,1,0:T(8,128)(2,1)} %get-tuple-element.168), channel_id=1, source_target_pairs={{0,16},{2,18},{4,20},{6,22},{8,24},{10,26},{12,28},{14,30},{16,0},... | collective-permute-start | bytes 737288 | tf_op jit(solution)/shard_map/ppermute | solution.py:979
  346.0 21.7 %collective-permute-start.28 = (bf16[1,160,768]{2,1,0:T(8,128)(2,1)}, bf16[1,160,768]{2,1,0:T(8,128)(2,1)}, u32[]{:S(2)}, u32[]{:S(2)}) collective-permute-start(bf16[1,160,768]{2,1,0:T(8,128)(2,1)} %get-tuple-element.167), channel_id=1, source_target_pairs={{0,24},{2,26},{4,28},{6,30},{8,0},{10,2},{12,4},{14,6},{16,8},{18,... | collective-permute-start | bytes 737288 | tf_op jit(solution)/shard_map/ppermute | solution.py:979
  372.7 7.9 %collective-permute-start.31 = (bf16[160,768]{1,0:T(8,128)(2,1)S(1)}, bf16[160,768]{1,0:T(8,128)(2,1)S(1)}, u32[]{:S(2)}, u32[]{:S(2)}) collective-permute-start(bf16[160,768]{1,0:T(8,128)(2,1)S(1)} %fusion.11), channel_id=1, source_target_pairs={{0,1},{1,0},{2,3},{3,2},{4,5},{5,4},{6,7},{7,6},{8,9},{9,8},{10,11... | collective-permute-start | bytes 737288 | tf_op jit(solution)/shard_map/ppermute | solution.py:957
  (10 other events, 12.7 us)
Sparse Core Ops, SparseCore 0:
  10.3 101.8 all-gather.2
  225.5 83.4 reduce-scatter.1

commit v5 on v4

--- a/solution.py
+++ b/solution.py
@@ -19,6 +19,7 @@
 MASKED = -1e30
 VMEM_LIMIT = 60 << 20
 BLOCK = 256
+TALL = 512
 COST = 4
 GROUP = H
 GROUP_ROWS = -(-GROUP // 8) * 8
@@ -160,9 +161,14 @@
 
     x = jnp.where(pl.program_id(1) == place_ref[0], mine_ref[...], other_ref[...])
     x_ref[...] = x
-    low = (dot(x, w_ref[:, :columns]) + bias_ref[0:1, :]).astype(bf16)
-    out_ref[...] = low
-    outT_ref[...] = low.T
+    cuts = [slice(at, at + width) for at in range(0, columns, width)]
+    made = dot(x, w_ref[:, cuts[0]])
+    for j, cut in enumerate(cuts):
+        low = (made + bias_ref[0:1, cut]).astype(bf16)
+        if j + 1 < len(cuts):
+            made = dot(x, w_ref[:, cuts[j + 1]])
+        out_ref[:, cut] = low
+        outT_ref[cut, :] = low.T
 
 
 def halves(mine, other, block):
@@ -1103,14 +1109,14 @@
         cot_halves = cotangent.reshape(2, 1, -1, width)
     half = x_halves[1].shape[1]
 
-    x, qkv, qkvT, w_qkv, vec, in_bias = project(side, *x_halves, first, inner, BLOCK)
+    x, qkv, qkvT, w_qkv, vec, in_bias = project(side, *x_halves, first, inner, TALL)
     if by_rows:
         attnT, log = attend_rows(bounds, qkv, qkvT, BLOCK)
     else:
         attn, saved = attend_gathered(bounds, qkv, rows, seq_index)
         attnT = attn.T
     out, out_other, act, gp, gs, low, gr1, gb, do, doT, sums, sums_in = dense(
-        side, attnT, x, *cot_halves, weights, vec, in_bias, BLOCK
+        side, attnT, x, *cot_halves, weights, vec, in_bias, TALL
     )
     out = out.reshape(-1, half, width)
     out_other = out_other.reshape(-1, half, width)
@@ -1141,7 +1147,7 @@
         g_qkv = last_product(side, x, g_x, (sums, sums_in, sums_qv), shards)
         g_qkv, gr1 = tied(g_qkv, gr1)
         qkv_sum = StagedSum(*g_qkv, "dp")
-        grad_x, grad_other = input_grad(side, g_x, gr1, w_qkv, *x_halves, BLOCK)
+        grad_x, grad_other = input_grad(side, g_x, gr1, w_qkv, *x_halves, TALL)
         grad_other, qkv_sum.came = tied(grad_other, qkv_sum.came)
         qkv_sum.step(1)
         grad_other = [swapped(grad_other[r : r + 1]) for r in range(mine)]
@@ -1151,8 +1157,7 @@
         qkv_sum.step(2)
         g_in = in_sum.result()
         both = swapped(jnp.concatenate([g_in, g_ffo], axis=0))
-        qkv_sum.came, both, grad_other = tied(qkv_sum.came, both, grad_other)
-        g_qkv = qkv_sum.result()
+        g_qkv, both, grad_other = tied(qkv_sum.result(), both, grad_other)
         for r in range(mine):
             grad_x = placed(grad_x, grad_other[r], seq_index, r)
         out = placed(out, out_other, seq_index)
@@ -1171,7 +1176,7 @@
         g_qkv = g_qkv.transpose(0, 2, 1, 3).reshape(shards, 3 * shard, width)
         g_qkv = jnp.concatenate([g_qkv, vectors], axis=1)
         g_qkv = lax.psum_scatter(g_qkv, "dp", scatter_dimension=0, tiled=True)[0]
-        grad_x, grad_other = input_grad(side, g_x, gr1, w_qkv, *x_halves, BLOCK)
+        grad_x, grad_other = input_grad(side, g_x, gr1, w_qkv, *x_halves, TALL)
         grad_x = jnp.concatenate([grad_x, grad_other], axis=1).reshape(rows, tok_seq, width)
         g_ffo, g_in, g_qkv = [lax.psum(v, "seq").astype(f32) for v in (g_ffo, g_in, g_qkv)]
     vectors = g_qkv[3 * shard :, :LANES]

time: 395 us -> 391 us (0.990)
  Pallas kernels: 219 us -> 213 us
    pallas_call x1, Pallas kernels: 73.1 us -> 68.6 us  [dense(): pl.pallas_call(dense_kernel, grid_spec=pltpu.PrefetchScalarGridSpec(num_s...]
  transfers between devices with their start and end apart: 34 -> 34, of which waited for: 16 -> 16; matrix products, arithmetic and copies ran while one was open for 6% -> 7% of each run, Pallas kernels for 33% -> 33%
where the time goes in v5:
time: 391 us; the launch traced here: 384 us
  Pallas kernels  213 us (54%)
  waiting for transfers between devices  87.8 us (22%)
  starting transfers between devices  29.6 us (8%)
  local copies, waits for them, and re-layouts  20.8 us (5%)
  other arithmetic  18.2 us (5%)
  between operations  14.6 us (4%)
    ppermute x25, waiting for transfers between devices, turned(): return lax.ppermute(values, axis, perm)  85.9 us
    pallas_call x1, Pallas kernels, dense(): pl.pallas_call(dense_kernel, grid_spec=pltpu.PrefetchScalarGridSpec(num_s...  68.6 us
    pallas_call x1, Pallas kernels, attend_rows_back(): pl.pallas_call(attend_back_kernel, grid_spec=pltpu.PrefetchScalarGridSpec...  39.8 us
    pallas_call x1, Pallas kernels, attend_rows(): pl.pallas_call(attend_kernel, grid_spec=pltpu.PrefetchScalarGridSpec(num_...  22.2 us
    ppermute x25, starting transfers between devices, turned(): return lax.ppermute(values, axis, perm)  21.9 us
    pallas_call x1, Pallas kernels, pair_product(): pl.pallas_call(pair_product_kernel, grid=(steps,), in_specs=[pl.BlockSpec...  18.2 us
    pallas_call x1, Pallas kernels, project(): pl.pallas_call(functools.partial(project_kernel, shards=shards, pieces=[b...  17 us
    pallas_call x1, Pallas kernels, split_product(): pl.pallas_call(split_product_kernel, grid_spec=pltpu.PrefetchScalarGridSp...  15.7 us
  transfers between devices with their start and end apart: 34, of which 16 were waited for; matrix products, arithmetic and copies ran while one was open for 7% of the time, Pallas kernels for 33%

profile of v5, /device:TPU:12, one launch (start us, length us, event | category | flops | bytes accessed | tf_op | source)
XLA Modules:
  0.0 384.3 jit_solution(801715210696986251)
XLA Ops:
  7.2 2.4 lower.1
  9.8 1.7 constant_dynamic-slice_fusion.1
  12.0 1.6 collective-permute-start
  14.6 2.0 collective-permute-start.2
  16.6 1.5 collective-permute-start.3
  18.1 12.6 %collective-permute-done.refs_1_ = bf16[48,2432]{1,0:T(8,128)(2,1)S(1)} collective-permute-done((bf16[48,2432]{1,0:T(8,128)(2,1)S(1)}, bf16[48,2432]{1,0:T(8,128)(2,1)S(1)}, u32[]{:S(2)}, u32[]{:S(2)}) %collective-permute-start) | collective-permute-done | bytes 233504 | tf_op jit(solution)/shard_map/ppermute | solution.py:985
  30.7 19.6 %collective-permute-done.1.refs_2_ = bf16[48,2432]{1,0:T(8,128)(2,1)S(1)} collective-permute-done((bf16[48,2432]{1,0:T(8,128)(2,1)S(1)}, bf16[48,2432]{1,0:T(8,128)(2,1)S(1)}, u32[]{:S(2)}, u32[]{:S(2)}) %collective-permute-start.1) | collective-permute-done | bytes 233504 | tf_op jit(solution)/shard_map/ppermute | solution.py:985
  50.3 1.5 collective-permute-start.4
  51.8 2.2 collective-permute-done.2.refs_3_
  54.0 1.5 collective-permute-start.5
  56.6 6.0 %collective-permute-done.5.refs_6_ = bf16[48,2432]{1,0:T(8,128)(2,1)S(1)} collective-permute-done((bf16[48,2432]{1,0:T(8,128)(2,1)S(1)}, bf16[48,2432]{1,0:T(8,128)(2,1)S(1)}, u32[]{:S(2)}, u32[]{:S(2)}) %collective-permute-start.5) | collective-permute-done | bytes 233504 | tf_op jit(solution)/shard_map/ppermute | solution.py:985
  62.5 6.4 %collective-permute-done.6.refs_7_ = bf16[48,2432]{1,0:T(8,128)(2,1)S(1)} collective-permute-done((bf16[48,2432]{1,0:T(8,128)(2,1)S(1)}, bf16[48,2432]{1,0:T(8,128)(2,1)S(1)}, u32[]{:S(2)}, u32[]{:S(2)}) %collective-permute-start.6) | collective-permute-done | bytes 233504 | tf_op jit(solution)/shard_map/ppermute | solution.py:985
  72.5 1.2 constant_dynamic-slice_fusion
  73.7 2.5 collective-permute-start.16
  77.5 17.0 %project.1 = (bf16[2048,768]{1,0:T(8,128)(2,1)}, bf16[2048,2304]{1,0:T(8,128)(2,1)}, bf16[2304,2048]{1,0:T(8,128)(2,1)}, bf16[768,2432]{1,0:T(8,128)(2,1)}, f32[8,768]{1,0:T(8,128)}, /*index=5*/f32[8,3072]{1,0:T(8,128)}) custom-call(s32[2]{0:T(128)} %pad_add_fusion.place_ref.side_ref, bf16[2048,768]{1,0:T(8,128)(2,1)} %bitcast.78, ...), custom_call_target="tpu_custom_call" | custom-call | flops 1811939328 | bytes 8060928 | tf_op jit(solution)/shard_map/project/pallas_call | solution.py:201
  94.6 22.2 %attend.1 = (bf16[768,2048]{1,0:T(8,128)(2,1)}, f32[16,2048]{1,0:T(8,128)}) custom-call(s32[2,8]{1,0:T(2,128)} %constant_dynamic-slice_fusion.2.bounds_ref, bf16[2048,2304]{1,0:T(8,128)(2,1)} %get-tuple-element.103.k_ref.v_ref.q_ref, bf16[2304,2048]{1,0:T(8,128)(2,1)} %get-tuple-element.104.qT_ref.vT_ref.kT_ref, ...), custom_call_target="tpu_custom_call" | custom-call | flops 1610612736 | bytes 3932160 | tf_op jit(solution)/shard_map/attend/pallas_call | solution.py:354
  116.8 1.1 copy-done.4
  117.9 68.6 %dense.1 = (bf16[2048,768]{1,0:T(8,128)(2,1)}, bf16[1024,768]{1,0:T(8,128)(2,1)}, bf16[2048,3072]{1,0:T(8,128)(2,1)}, bf16[2048,3072]{1,0:T(8,128)(2,1)}, bf16[2...) custom-call(s32[2]{0:T(128)} %pad_add_fusion.place_ref.side_ref, ...), custom_call_target="tpu_custom_call" | custom-call | flops 10871635968 | bytes 17301504 | tf_op jit(solution)/shard_map/dense/pallas_call | solution.py:663
  186.5 15.7 %split_product.1 = (bf16[8,192,768]{2,1,0:T(8,128)(2,1)}, bf16[8,192,768]{2,1,0:T(8,128)(2,1)}) custom-call(s32[2]{0:T(128)} %pad_add_fusion.place_ref.side_ref, bf16[2048,768]{1,0:T(8,128)(2,1)} %get-tuple-element.112.a_ref, bf16[2048,3072]{1,0:T(8,128)(2,1)} %get-tuple-element.113.b_ref), custom_call_target="tpu_custom_call" | custom-call | flops 2415919104 | bytes 5111808 | tf_op jit(solution)/shard_map/split_product/pallas_call | solution.py:745
  202.4 18.2 %pair_product.1 = bf16[16,240,768]{2,1,0:T(8,128)(2,1)} custom-call(bf16[2048,3072]{1,0:T(8,128)(2,1)} %get-tuple-element.117.a_ref, bf16[2048,768]{1,0:T(8,128)(2,1)} %get-tuple-element.118.b_ref, bf16[768,2048]{1,0:T(8,128)(2,1)} %get-tuple-element.105.attn_ref.cT_ref.outT_ref, bf16[2048,768]{1,0:T(8,128)(2,1)} %get-tuple-element.119.d_ref), custom_call_target="tpu_custom_call" | custom-call | flops 3019898880 | bytes 6979584 | tf_op jit(solution)/shard_map/pair_product/pallas_call | solution.py:780
  220.7 1.4 copy-done.2
  222.3 1.5 copy-done.1
  223.8 3.2 add_convert_fusion
  227.0 2.2 collective-permute-start.19
  229.2 39.8 %attend_back.1 = (bf16[2048,2304]{1,0:T(8,128)(2,1)}, f32[8,768]{1,0:T(8,128)}) custom-call(s32[2,8]{1,0:T(2,128)} %constant_dynamic-slice_fusion.2.bounds_ref, bf16[2048,2304]{1,0:T(8,128)(2,1)} %get-tuple-element.103.k_ref.v_ref.q_ref, bf16[2304,2048]{1,0:T(8,128)(2,1)} %get-tuple-element.104.qT_ref.vT_ref.kT_ref, ...), custom_call_target="tpu_custom_call" | custom-call | flops 4026531840 | bytes 8650752 | tf_op jit(solution)/shard_map/attend_back/pallas_call | solution.py:478
  269.1 15.0 %last_product.1 = (bf16[8,160,768]{2,1,0:T(8,128)(2,1)}, bf16[8,160,768]{2,1,0:T(8,128)(2,1)}) custom-call(s32[2]{0:T(128)} %pad_add_fusion.place_ref.side_ref, bf16[2048,768]{1,0:T(8,128)(2,1)} %get-tuple-element.106.x_ref.a_ref, bf16[2048,2304]{1,0:T(8,128)(2,1)} %get-tuple-element.130.b_ref.g_ref, f32[8,768]{1,0:T(8,128)} %get-tuple-element.131.refs_0_, ...), custom_call_target="tpu_custom_call" | custom-call | flops 1811939328 | bytes 4030464 | tf_op jit(solution)/shard_map/last_product/pallas_call | solution.py:886
  284.3 14.2 %input_grad.1 = (bf16[2048,768]{1,0:T(8,128)(2,1)}, bf16[1024,768]{1,0:T(8,128)(2,1)}) custom-call(s32[2]{0:T(128)} %pad_add_fusion.place_ref.side_ref, bf16[2048,2304]{1,0:T(8,128)(2,1)} %get-tuple-element.130.b_ref.g_ref, f32[2048,768]{1,0:T(8,128)} %get-tuple-element.137.gr1_ref, bf16[768,2432]{1,0:T(8,128)(2,1)} %get-tuple-element.138.w_ref), custom_call_target="tpu_custom_call" | custom-call | flops 1811939328 | bytes 5603328 | tf_op jit(solution)/shard_map/input_grad/pallas_call | solution.py:824
  298.5 1.3 copy-done.3
  299.7 3.7 add_convert_fusion.3
  303.4 1.3 fusion.12
  306.3 2.0 collective-permute-start.24
  308.3 8.0 %collective-permute-done.22 = bf16[1,192,768]{2,1,0:T(8,128)(2,1)S(1)} collective-permute-done((bf16[1,192,768]{2,1,0:T(8,128)(2,1)}, bf16[1,192,768]{2,1,0:T(8,128)(2,1)S(1)}, u32[]{:S(2)}, u32[]{:S(2)}) %collective-permute-start.22) | collective-permute-done | bytes 294944 | tf_op jit(solution)/shard_map/ppermute | solution.py:985
  316.3 1.5 collective-permute-start.30
  317.8 14.7 %collective-permute-done.23 = bf16[1,192,768]{2,1,0:T(8,128)(2,1)S(1)} collective-permute-done((bf16[1,192,768]{2,1,0:T(8,128)(2,1)}, bf16[1,192,768]{2,1,0:T(8,128)(2,1)S(1)}, u32[]{:S(2)}, u32[]{:S(2)}) %collective-permute-start.23) | collective-permute-done | bytes 294944 | tf_op jit(solution)/shard_map/ppermute | solution.py:985
  333.3 1.3 fusion.10
  334.6 1.0 pad_maximum_fusion
  335.7 1.2 collective-permute-start.29
  336.9 2.1 fusion.8
  339.0 3.3 collective-permute-start.27
  342.3 2.9 collective-permute-start.26
  345.2 2.7 constant_dynamic-update-slice_fusion.2
  348.9 9.9 %collective-permute-done.27 = bf16[1,160,768]{2,1,0:T(8,128)(2,1)S(1)} collective-permute-done((bf16[1,160,768]{2,1,0:T(8,128)(2,1)}, bf16[1,160,768]{2,1,0:T(8,128)(2,1)S(1)}, u32[]{:S(2)}, u32[]{:S(2)}) %collective-permute-start.27) | collective-permute-done | bytes 245792 | tf_op jit(solution)/shard_map/ppermute | solution.py:985
  358.8 4.1 %collective-permute-done.26 = bf16[1,160,768]{2,1,0:T(8,128)(2,1)} collective-permute-done((bf16[1,160,768]{2,1,0:T(8,128)(2,1)S(1)}, bf16[1,160,768]{2,1,0:T(8,128)(2,1)}, u32[]{:S(2)}, u32[]{:S(2)}) %collective-permute-start.26) | collective-permute-done | bytes 245792 | tf_op jit(solution)/shard_map/ppermute | solution.py:985
  362.9 1.2 fusion.11
  365.2 1.1 convert_add_fusion
  367.8 1.2 collective-permute-start.31
  369.0 2.1 constant_dynamic-update-slice_fusion
  372.9 1.8 collective-permute-done.31
  (113 shorter events, 18.4 us)
Async XLA Ops:
  7.2 109.6 %all-gather.3.cloned.1.call-start = ((), (), s32[]{:S(2)}) async-start(), calls=%async_computation.2 | async-start | bytes 11280384 | tf_op jit(solution)/shard_map/all_gather | solution.py:1080
  9.7 62.8 %copy-start = (bf16[4,512,768]{2,1,0:T(8,128)(2,1)S(1)}, bf16[4,512,768]{2,1,0:T(8,128)(2,1)}, u32[]{:S(2)}) copy-start(bf16[4,512,768]{2,1,0:T(8,128)(2,1)} %param.29) | copy-start | bytes 9437188
  9.7 324.9 %reduce-scatter.2.cloned.1.call-start = ((), (), s32[]{:S(2)}) async-start(), calls=%async_computation.1 | async-start | bytes 6266880 | tf_op jit(solution)/shard_map/reduce_scatter | solution.py:1140
  11.4 64.8 %copy-start.26 = (s32[4,8]{1,0:T(4,128)S(1)}, s32[4,8]{1,0:T(4,128)}, u32[]{:S(2)}) copy-start(s32[4,8]{1,0:T(4,128)} %param.28) | copy-start | bytes 388
  11.4 61.0 %collective-permute-start.15 = (bf16[2,512,768]{2,1,0:T(8,128)(2,1)S(1)}, bf16[2,512,768]{2,1,0:T(8,128)(2,1)}, u32[]{:S(2)}, u32[]{:S(2)}) collective-permute-start(bf16[2,512,768]{2,1,0:T(8,128)(2,1)S(1)} %constant_dynamic-slice_fusion.1), channel_id=1, source_target_pairs={{0,1},{1,0},{2,3},{3,2},{4,5},{5,4},{6,7},{7,6},{8,9},{9,8},{10,11... | collective-permute-start | bytes 4718600 | tf_op jit(solution)/shard_map/ppermute | solution.py:963
  12.0 18.7 %collective-permute-start = (bf16[48,2432]{1,0:T(8,128)(2,1)S(1)}, bf16[48,2432]{1,0:T(8,128)(2,1)S(1)}, u32[]{:S(2)}, u32[]{:S(2)}) collective-permute-start(bf16[48,2432]{1,0:T(8,128)(2,1)S(1)} %copy-done.10), channel_id=1, source_target_pairs={{0,8},{2,10},{4,12},{6,14},{8,16},{10,18},{12,20},{14,22},{16,24},... | collective-permute-start | bytes 700424 | tf_op jit(solution)/shard_map/ppermute | solution.py:985
  13.6 36.7 %collective-permute-start.1 = (bf16[48,2432]{1,0:T(8,128)(2,1)S(1)}, bf16[48,2432]{1,0:T(8,128)(2,1)S(1)}, u32[]{:S(2)}, u32[]{:S(2)}) collective-permute-start(bf16[48,2432]{1,0:T(8,128)(2,1)S(1)} %copy-done.10), channel_id=1, source_target_pairs={{0,16},{2,18},{4,20},{6,22},{8,24},{10,26},{12,28},{14,30},{16,0},... | collective-permute-start | bytes 700424 | tf_op jit(solution)/shard_map/ppermute | solution.py:985
  14.6 39.4 %collective-permute-start.2 = (bf16[48,2432]{1,0:T(8,128)(2,1)S(1)}, bf16[48,2432]{1,0:T(8,128)(2,1)S(1)}, u32[]{:S(2)}, u32[]{:S(2)}) collective-permute-start(bf16[48,2432]{1,0:T(8,128)(2,1)S(1)} %copy-done.10), channel_id=1, source_target_pairs={{0,24},{2,26},{4,28},{6,30},{8,0},{10,2},{12,4},{14,6},{16,8},{18,... | collective-permute-start | bytes 700424 | tf_op jit(solution)/shard_map/ppermute | solution.py:985
  16.6 38.8 %collective-permute-start.3 = (bf16[48,2432]{1,0:T(8,128)(2,1)S(1)}, bf16[48,2432]{1,0:T(8,128)(2,1)S(1)}, u32[]{:S(2)}, u32[]{:S(2)}) collective-permute-start(bf16[48,2432]{1,0:T(8,128)(2,1)S(1)} %copy-done.10), channel_id=1, source_target_pairs={{0,4},{2,6},{4,0},{6,2},{8,12},{10,14},{12,8},{14,10},{16,20},{18,... | collective-permute-start | bytes 700424 | tf_op jit(solution)/shard_map/ppermute | solution.py:985
  30.7 25.3 %copy-start.11 = (bf16[48,2432]{1,0:T(8,128)(2,1)}, bf16[48,2432]{1,0:T(8,128)(2,1)S(1)}, u32[]{:S(2)}) copy-start(bf16[48,2432]{1,0:T(8,128)(2,1)S(1)} %collective-permute-done.refs_1_) | copy-start | bytes 700420
  30.7 25.3 %collective-permute-start.7 = (bf16[48,2432]{1,0:T(8,128)(2,1)S(1)}, bf16[48,2432]{1,0:T(8,128)(2,1)S(1)}, u32[]{:S(2)}, u32[]{:S(2)}) collective-permute-start(bf16[48,2432]{1,0:T(8,128)(2,1)S(1)} %copy-done.10), channel_id=1, source_target_pairs={{0,2},{2,0},{4,6},{6,4},{8,10},{10,8},{12,14},{14,12},{16,18},{18,... | collective-permute-start | bytes 700424 | tf_op jit(solution)/shard_map/ppermute | solution.py:985
  50.3 18.6 %copy-start.12 = (bf16[48,2432]{1,0:T(8,128)(2,1)}, bf16[48,2432]{1,0:T(8,128)(2,1)S(1)}, u32[]{:S(2)}) copy-start(bf16[48,2432]{1,0:T(8,128)(2,1)S(1)} %collective-permute-done.1.refs_2_) | copy-start | bytes 700420
  50.3 6.1 %collective-permute-start.4 = (bf16[48,2432]{1,0:T(8,128)(2,1)S(1)}, bf16[48,2432]{1,0:T(8,128)(2,1)S(1)}, u32[]{:S(2)}, u32[]{:S(2)}) collective-permute-start(bf16[48,2432]{1,0:T(8,128)(2,1)S(1)} %collective-permute-done.refs_1_), channel_id=1, source_target_pairs={{0,4},{2,6},{4,0},{6,2},{8,12},{10,14},{12,8},{14,10},{16,20},{18,... | collective-permute-start | bytes 700424 | tf_op jit(solution)/shard_map/ppermute | solution.py:985
  54.0 15.5 %copy-start.13 = (bf16[48,2432]{1,0:T(8,128)(2,1)}, bf16[48,2432]{1,0:T(8,128)(2,1)S(1)}, u32[]{:S(2)}) copy-start(bf16[48,2432]{1,0:T(8,128)(2,1)S(1)} %collective-permute-done.2.refs_3_) | copy-start | bytes 700420
  54.0 8.6 %collective-permute-start.5 = (bf16[48,2432]{1,0:T(8,128)(2,1)S(1)}, bf16[48,2432]{1,0:T(8,128)(2,1)S(1)}, u32[]{:S(2)}, u32[]{:S(2)}) collective-permute-start(bf16[48,2432]{1,0:T(8,128)(2,1)S(1)} %collective-permute-done.1.refs_2_), channel_id=1, source_target_pairs={{0,4},{2,6},{4,0},{6,2},{8,12},{10,14},{12,8},{14,10},{16,20},{18,... | collective-permute-start | bytes 700424 | tf_op jit(solution)/shard_map/ppermute | solution.py:985
  55.4 14.1 %copy-start.14 = (bf16[48,2432]{1,0:T(8,128)(2,1)}, bf16[48,2432]{1,0:T(8,128)(2,1)S(1)}, u32[]{:S(2)}) copy-start(bf16[48,2432]{1,0:T(8,128)(2,1)S(1)} %collective-permute-done.3.refs_4_) | copy-start | bytes 700420
  55.5 13.4 %collective-permute-start.6 = (bf16[48,2432]{1,0:T(8,128)(2,1)S(1)}, bf16[48,2432]{1,0:T(8,128)(2,1)S(1)}, u32[]{:S(2)}, u32[]{:S(2)}) collective-permute-start(bf16[48,2432]{1,0:T(8,128)(2,1)S(1)} %collective-permute-done.2.refs_3_), channel_id=1, source_target_pairs={{0,4},{2,6},{4,0},{6,2},{8,12},{10,14},{12,8},{14,10},{16,20},{18,... | collective-permute-start | bytes 700424 | tf_op jit(solution)/shard_map/ppermute | solution.py:985
  56.0 14.4 %copy-start.15 = (bf16[48,2432]{1,0:T(8,128)(2,1)}, bf16[48,2432]{1,0:T(8,128)(2,1)S(1)}, u32[]{:S(2)}) copy-start(bf16[48,2432]{1,0:T(8,128)(2,1)S(1)} %collective-permute-done.7.refs_8_) | copy-start | bytes 700420
  56.0 12.9 %collective-permute-start.8 = (bf16[48,2432]{1,0:T(8,128)(2,1)S(1)}, bf16[48,2432]{1,0:T(8,128)(2,1)S(1)}, u32[]{:S(2)}, u32[]{:S(2)}) collective-permute-start(bf16[48,2432]{1,0:T(8,128)(2,1)S(1)} %collective-permute-done.refs_1_), channel_id=1, source_target_pairs={{0,2},{2,0},{4,6},{6,4},{8,10},{10,8},{12,14},{14,12},{16,18},{18,... | collective-permute-start | bytes 700424 | tf_op jit(solution)/shard_map/ppermute | solution.py:985
  56.3 14.4 %copy-start.16 = (bf16[48,2432]{1,0:T(8,128)(2,1)}, bf16[48,2432]{1,0:T(8,128)(2,1)S(1)}, u32[]{:S(2)}) copy-start(bf16[48,2432]{1,0:T(8,128)(2,1)S(1)} %collective-permute-done.4.refs_5_) | copy-start | bytes 700420
  56.4 13.1 %collective-permute-start.9 = (bf16[48,2432]{1,0:T(8,128)(2,1)S(1)}, bf16[48,2432]{1,0:T(8,128)(2,1)S(1)}, u32[]{:S(2)}, u32[]{:S(2)}) collective-permute-start(bf16[48,2432]{1,0:T(8,128)(2,1)S(1)} %collective-permute-done.1.refs_2_), channel_id=1, source_target_pairs={{0,2},{2,0},{4,6},{6,4},{8,10},{10,8},{12,14},{14,12},{16,18},{18,... | collective-permute-start | bytes 700424 | tf_op jit(solution)/shard_map/ppermute | solution.py:985
  62.5 8.5 %copy-start.17 = (bf16[48,2432]{1,0:T(8,128)(2,1)}, bf16[48,2432]{1,0:T(8,128)(2,1)S(1)}, u32[]{:S(2)}) copy-start(bf16[48,2432]{1,0:T(8,128)(2,1)S(1)} %collective-permute-done.5.refs_6_) | copy-start | bytes 700420
  62.5 7.1 %collective-permute-start.10 = (bf16[48,2432]{1,0:T(8,128)(2,1)S(1)}, bf16[48,2432]{1,0:T(8,128)(2,1)S(1)}, u32[]{:S(2)}, u32[]{:S(2)}) collective-permute-start(bf16[48,2432]{1,0:T(8,128)(2,1)S(1)} %collective-permute-done.2.refs_3_), channel_id=1, source_target_pairs={{0,2},{2,0},{4,6},{6,4},{8,10},{10,8},{12,14},{14,12},{16,18},{18,... | collective-permute-start | bytes 700424 | tf_op jit(solution)/shard_map/ppermute | solution.py:985
  68.9 2.5 copy-start.18
  68.9 1.5 collective-permute-start.11
  68.9 8.6 %copy-start.19 = (bf16[48,2432]{1,0:T(8,128)(2,1)}, bf16[48,2432]{1,0:T(8,128)(2,1)S(1)}, u32[]{:S(2)}) copy-start(bf16[48,2432]{1,0:T(8,128)(2,1)S(1)} %collective-permute-done.8.refs_9_) | copy-start | bytes 700420
  68.9 1.8 collective-permute-start.12
  69.5 1.6 collective-permute-start.13
  69.6 1.8 collective-permute-start.14
  73.7 43.1 %collective-permute-start.16 = (bf16[2,512,768]{2,1,0:T(8,128)(2,1)}, bf16[2,512,768]{2,1,0:T(8,128)(2,1)S(1)}, u32[]{:S(2)}, u32[]{:S(2)}) collective-permute-start(bf16[2,512,768]{2,1,0:T(8,128)(2,1)} %constant_dynamic-slice_fusion), channel_id=1, source_target_pairs={{0,1},{1,0},{2,3},{3,2},{4,5},{5,4},{6,7},{7,6},{8,9},{9,8},{10,11... | collective-permute-start | bytes 4718600 | tf_op jit(solution)/shard_map/ppermute | solution.py:963
  202.3 18.4 %collective-permute-start.17 = (bf16[8,192,768]{2,1,0:T(8,128)(2,1)}, bf16[8,192,768]{2,1,0:T(8,128)(2,1)S(1)}, u32[]{:S(2)}, u32[]{:S(2)}) collective-permute-start(bf16[8,192,768]{2,1,0:T(8,128)(2,1)} %get-tuple-element.121), channel_id=1, source_target_pairs={{0,2},{2,0},{4,6},{6,4},{8,10},{10,8},{12,14},{14,12},{16,18},{18,... | collective-permute-start | bytes 7077896 | tf_op jit(solution)/shard_map/ppermute | solution.py:985
  222.1 46.9 %collective-permute-start.18 = (bf16[2,512,768]{2,1,0:T(8,128)(2,1)}, bf16[2,512,768]{2,1,0:T(8,128)(2,1)}, u32[]{:S(2)}, u32[]{:S(2)}) collective-permute-start(bf16[2,512,768]{2,1,0:T(8,128)(2,1)} %bitcast.97), channel_id=1, source_target_pairs={{0,1},{1,0},{2,3},{3,2},{4,5},{5,4},{6,7},{7,6},{8,9},{9,8},{10,11... | collective-permute-start | bytes 4718600 | tf_op jit(solution)/shard_map/ppermute | solution.py:963
  227.0 42.0 %collective-permute-start.19 = (bf16[4,192,768]{2,1,0:T(8,128)(2,1)}, bf16[4,192,768]{2,1,0:T(8,128)(2,1)S(1)}, u32[]{:S(2)}, u32[]{:S(2)}) collective-permute-start(bf16[4,192,768]{2,1,0:T(8,128)(2,1)} %get-tuple-element.157), channel_id=1, source_target_pairs={{0,4},{2,6},{4,0},{6,2},{8,12},{10,14},{12,8},{14,10},{16,20},{18,... | collective-permute-start | bytes 3538952 | tf_op jit(solution)/shard_map/ppermute | solution.py:985
  269.0 15.0 %copy-start.7 = (bf16[4,192,768]{2,1,0:T(8,128)(2,1)}, bf16[4,192,768]{2,1,0:T(8,128)(2,1)S(1)}, u32[]{:S(2)}) copy-start(bf16[4,192,768]{2,1,0:T(8,128)(2,1)S(1)} %collective-permute-done.19) | copy-start | bytes 3538948
  284.1 14.4 %collective-permute-start.20 = (bf16[8,160,768]{2,1,0:T(8,128)(2,1)}, bf16[8,160,768]{2,1,0:T(8,128)(2,1)S(1)}, u32[]{:S(2)}, u32[]{:S(2)}) collective-permute-start(bf16[8,160,768]{2,1,0:T(8,128)(2,1)} %get-tuple-element.142), channel_id=1, source_target_pairs={{0,2},{2,0},{4,6},{6,4},{8,10},{10,8},{12,14},{14,12},{16,18},{18,... | collective-permute-start | bytes 5898248 | tf_op jit(solution)/shard_map/ppermute | solution.py:985
  299.7 3.7 copy-start.5
  303.4 29.8 %collective-permute-start.21 = (bf16[4,160,768]{2,1,0:T(8,128)(2,1)}, bf16[4,160,768]{2,1,0:T(8,128)(2,1)}, u32[]{:S(2)}, u32[]{:S(2)}) collective-permute-start(bf16[4,160,768]{2,1,0:T(8,128)(2,1)} %get-tuple-element.159), channel_id=1, source_target_pairs={{0,4},{2,6},{4,0},{6,2},{8,12},{10,14},{12,8},{14,10},{16,20},{18,... | collective-permute-start | bytes 2949128 | tf_op jit(solution)/shard_map/ppermute | solution.py:985
  304.7 27.9 %collective-permute-start.25 = (bf16[1,512,768]{2,1,0:T(8,128)(2,1)}, bf16[1,512,768]{2,1,0:T(8,128)(2,1)}, u32[]{:S(2)}, u32[]{:S(2)}) collective-permute-start(bf16[1,512,768]{2,1,0:T(8,128)(2,1)} %get-tuple-element.167), channel_id=1, source_target_pairs={{0,1},{1,0},{2,3},{3,2},{4,5},{5,4},{6,7},{7,6},{8,9},{9,8},{10,11... | collective-permute-start | bytes 2359304 | tf_op jit(solution)/shard_map/ppermute | solution.py:963
  306.3 10.0 %collective-permute-start.22 = (bf16[1,192,768]{2,1,0:T(8,128)(2,1)}, bf16[1,192,768]{2,1,0:T(8,128)(2,1)S(1)}, u32[]{:S(2)}, u32[]{:S(2)}) collective-permute-start(bf16[1,192,768]{2,1,0:T(8,128)(2,1)} %get-tuple-element.162), channel_id=1, source_target_pairs={{0,8},{2,10},{4,12},{6,14},{8,16},{10,18},{12,20},{14,22},{16,24},... | collective-permute-start | bytes 884744 | tf_op jit(solution)/shard_map/ppermute | solution.py:985
  306.3 26.2 %collective-permute-start.23 = (bf16[1,192,768]{2,1,0:T(8,128)(2,1)}, bf16[1,192,768]{2,1,0:T(8,128)(2,1)S(1)}, u32[]{:S(2)}, u32[]{:S(2)}) collective-permute-start(bf16[1,192,768]{2,1,0:T(8,128)(2,1)} %get-tuple-element.161), channel_id=1, source_target_pairs={{0,16},{2,18},{4,20},{6,22},{8,24},{10,26},{12,28},{14,30},{16,0},... | collective-permute-start | bytes 884744 | tf_op jit(solution)/shard_map/ppermute | solution.py:985
  306.3 26.3 %collective-permute-start.24 = (bf16[1,192,768]{2,1,0:T(8,128)(2,1)}, bf16[1,192,768]{2,1,0:T(8,128)(2,1)}, u32[]{:S(2)}, u32[]{:S(2)}) collective-permute-start(bf16[1,192,768]{2,1,0:T(8,128)(2,1)} %get-tuple-element.160), channel_id=1, source_target_pairs={{0,24},{2,26},{4,28},{6,30},{8,0},{10,2},{12,4},{14,6},{16,8},{18,... | collective-permute-start | bytes 884744 | tf_op jit(solution)/shard_map/ppermute | solution.py:985
  316.3 47.8 %collective-permute-start.30 = (bf16[1,512,768]{2,1,0:T(8,128)(2,1)}, bf16[1,512,768]{2,1,0:T(8,128)(2,1)S(1)}, u32[]{:S(2)}, u32[]{:S(2)}) collective-permute-start(bf16[1,512,768]{2,1,0:T(8,128)(2,1)} %get-tuple-element.166), channel_id=1, source_target_pairs={{0,1},{1,0},{2,3},{3,2},{4,5},{5,4},{6,7},{7,6},{8,9},{9,8},{10,11... | collective-permute-start | bytes 2359304 | tf_op jit(solution)/shard_map/ppermute | solution.py:963
  335.7 28.5 %collective-permute-start.29 = (bf16[432,768]{1,0:T(8,128)(2,1)S(1)}, bf16[432,768]{1,0:T(8,128)(2,1)}, u32[]{:S(2)}, u32[]{:S(2)}) collective-permute-start(bf16[432,768]{1,0:T(8,128)(2,1)S(1)} %pad_maximum_fusion), channel_id=1, source_target_pairs={{0,1},{1,0},{2,3},{3,2},{4,5},{5,4},{6,7},{7,6},{8,9},{9,8},{10,11... | collective-permute-start | bytes 1990664 | tf_op jit(solution)/shard_map/ppermute | solution.py:963
  339.0 9.9 %collective-permute-start.28 = (bf16[1,160,768]{2,1,0:T(8,128)(2,1)}, bf16[1,160,768]{2,1,0:T(8,128)(2,1)S(1)}, u32[]{:S(2)}, u32[]{:S(2)}) collective-permute-start(bf16[1,160,768]{2,1,0:T(8,128)(2,1)} %get-tuple-element.164), channel_id=1, source_target_pairs={{0,24},{2,26},{4,28},{6,30},{8,0},{10,2},{12,4},{14,6},{16,8},{18,... | collective-permute-start | bytes 737288 | tf_op jit(solution)/shard_map/ppermute | solution.py:985
  339.0 19.8 %collective-permute-start.27 = (bf16[1,160,768]{2,1,0:T(8,128)(2,1)}, bf16[1,160,768]{2,1,0:T(8,128)(2,1)S(1)}, u32[]{:S(2)}, u32[]{:S(2)}) collective-permute-start(bf16[1,160,768]{2,1,0:T(8,128)(2,1)} %get-tuple-element.165), channel_id=1, source_target_pairs={{0,16},{2,18},{4,20},{6,22},{8,24},{10,26},{12,28},{14,30},{16,0},... | collective-permute-start | bytes 737288 | tf_op jit(solution)/shard_map/ppermute | solution.py:985
  342.3 20.6 %collective-permute-start.26 = (bf16[1,160,768]{2,1,0:T(8,128)(2,1)S(1)}, bf16[1,160,768]{2,1,0:T(8,128)(2,1)}, u32[]{:S(2)}, u32[]{:S(2)}) collective-permute-start(bf16[1,160,768]{2,1,0:T(8,128)(2,1)S(1)} %get-tuple-element.163), channel_id=1, source_target_pairs={{0,8},{2,10},{4,12},{6,14},{8,16},{10,18},{12,20},{14,22},{16,24},... | collective-permute-start | bytes 737288 | tf_op jit(solution)/shard_map/ppermute | solution.py:985
  345.2 20.0 %copy-start.6 = (bf16[1,240,768]{2,1,0:T(8,128)(2,1)S(1)}, bf16[1,240,768]{2,1,0:T(8,128)(2,1)}, u32[]{:S(2)}) copy-start(bf16[1,240,768]{2,1,0:T(8,128)(2,1)} %reduce-scatter.2.cloned.1.call-done) | copy-start | bytes 1105924
  367.8 6.9 %collective-permute-start.31 = (bf16[160,768]{1,0:T(8,128)(2,1)S(1)}, bf16[160,768]{1,0:T(8,128)(2,1)S(1)}, u32[]{:S(2)}, u32[]{:S(2)}) collective-permute-start(bf16[160,768]{1,0:T(8,128)(2,1)S(1)} %fusion.11), channel_id=1, source_target_pairs={{0,1},{1,0},{2,3},{3,2},{4,5},{5,4},{6,7},{7,6},{8,9},{9,8},{10,11... | collective-permute-start | bytes 737288 | tf_op jit(solution)/shard_map/ppermute | solution.py:963
  (13 other events, 17.3 us)
Sparse Core Ops, SparseCore 0:
  10.3 101.8 all-gather.2
  222.2 83.4 reduce-scatter.1
